TPU v7x, 32 devices: a whole 2x2x4 slice. The times are simulated.
32 devices in a mesh: grp: 2 (over y), blk: 4 (over z), bulk: 4 (over x, core).
Axes of the slice: x: 2, y: 2, z: 4, core: 2. Of those that a mesh axis runs over, the one named last changes fastest.
Arguments:
- tokens: bfloat16 [80, 8192], P(('grp', 'blk'), 'bulk'), parts along dimension 0, may hold values from -6 to 6
- cotangent: bfloat16 [80, 8192], P(('grp', 'blk'), 'bulk'), parts along dimension 0, may hold values from -1.5 to 1.5
- gate_weight: bfloat16 [8192, 26624], P('bulk', 'blk'), may hold values from -0.0625 to 0.0625
- up_weight: bfloat16 [8192, 26624], P('bulk', 'blk'), may hold values from -0.0625 to 0.0625
- down_weight: bfloat16 [26624, 8192], P('blk', 'bulk'), may hold values from -0.0390625 to 0.0390625
Outputs:
- mixed: bfloat16 [80, 8192], P(('grp', 'blk'), 'bulk'), parts along dimension 0
- grad_input: bfloat16 [80, 8192], P(('grp', 'blk'), 'bulk'), parts along dimension 0
There are 2 independent parts, one for each index of `grp`. A program takes and returns all parts, laid end to end along the dimension named above; an argument that names none is the same for every part. Nothing has to cross between parts.
All inputs are finite; a program needn't handle non-finite values.
Results may differ from a plain program's by a relative error of at most 0.0049.
Values may be sent and summed in bfloat16 or wider, within the bound.
No kernel may reach another device: no remote copies, remote signals or barrier semaphores. Data moves between devices by JAX's collectives and lax.ppermute only.
A program may use at most 192 MiB of HBM per device.

v0:
```python
import jax
import jax.numpy as jnp
from jax import lax
from jax.sharding import PartitionSpec as P


def per_device(tokens, cotangent, gate_weight, up_weight, down_weight):
    token_all, cot_all = (
        lax.all_gather(tokens, "blk", axis=0, tiled=True),
        lax.all_gather(cotangent, "blk", axis=0, tiled=True),
    )
    width = gate_weight.shape[1]
    paired = jnp.concatenate([gate_weight, up_weight], axis=1)
    block = token_all
    gate_up = lax.psum_scatter(
        jnp.dot(block, paired, preferred_element_type=jnp.float32),
        "bulk",
        scatter_dimension=0,
        tiled=True,
    )
    gate = gate_up[:, :width]
    upward = gate_up[:, width:]
    sigma = jax.nn.sigmoid(gate)
    hidden = (gate * sigma * upward).astype(jnp.bfloat16)
    hidden_all = lax.all_gather(hidden, "bulk", axis=0, tiled=True)
    block = hidden_all
    mixed = lax.psum_scatter(
        jnp.dot(block, down_weight, preferred_element_type=jnp.float32),
        "blk",
        scatter_dimension=0,
        tiled=True,
    ).astype(jnp.bfloat16)
    block = cot_all
    back = lax.psum_scatter(
        lax.dot_general(
            block, down_weight, (((1,), (1,)), ((), ())), preferred_element_type=jnp.float32
        ),
        "bulk",
        scatter_dimension=0,
        tiled=True,
    )
    d_up = (back * gate * sigma).astype(jnp.bfloat16)
    d_gate = (back * upward * sigma * (1.0 + gate * (1.0 - sigma))).astype(jnp.bfloat16)
    grads_local = jnp.concatenate([d_gate, d_up], axis=1)
    grads_all = lax.all_gather(grads_local, "bulk", axis=0, tiled=True)
    block = grads_all
    grad_input = lax.psum_scatter(
        lax.dot_general(
            block, paired, (((1,), (1,)), ((), ())), preferred_element_type=jnp.float32
        ),
        "blk",
        scatter_dimension=0,
        tiled=True,
    ).astype(jnp.bfloat16)
    return (mixed, grad_input)


def solution(mesh):
    return jax.shard_map(
        per_device,
        mesh=mesh,
        in_specs=(
            P(("grp", "blk"), "bulk"),
            P(("grp", "blk"), "bulk"),
            P("bulk", "blk"),
            P("bulk", "blk"),
            P("blk", "bulk"),
        ),
        out_specs=(P(("grp", "blk"), "bulk"), P(("grp", "blk"), "bulk")),
        check_vma=False,
    )
```

profile of v0, /device:TPU:0, one launch (start us, length us, event | category | flops | bytes accessed | tf_op | source)
XLA Modules:
  0.0 268.9 jit_solution(2728264743056934311)
XLA Ops:
  7.2 0.0 all-reduce.9.cloned.1.call-start
  7.2 19.2 %constant_dynamic-update-slice_fusion.1 = bf16[2048,13312]{1,0:T(8,128)(2,1)} fusion(bf16[2048,6656]{1,0:T(8,128)(2,1)} %param.7), kind=kLoop, calls=%fused_computation.10 | loop fusion | bytes 54525952
  26.5 15.6 %all-gather = bf16[4,10,2048]{2,1,0:T(8,128)(2,1)S(1)} all-gather(bf16[1,10,2048]{2,1,0:T(8,128)(2,1)S(1)} %bitcast.18), channel_id=1, replica_groups=mesh['grp'=2,'blk'=4,'bulk'=4] {'blk'}, dimensions={0}, use_global_device_ids=true | all-gather | bytes 204800 | tf_op jit(solution)/shard_map/all_gather | solution.py:9
  42.1 0.1 reshape.5
  42.2 14.4 %all-gather.2 = bf16[4,10,2048]{2,1,0:T(8,128)(2,1)S(1)} all-gather(bf16[1,10,2048]{2,1,0:T(8,128)(2,1)S(1)} %bitcast.19), channel_id=1, replica_groups=mesh['grp'=2,'blk'=4,'bulk'=4] {'blk'}, dimensions={0}, use_global_device_ids=true | all-gather | bytes 204800 | tf_op jit(solution)/shard_map/all_gather | solution.py:10
  56.6 0.1 reshape.9
  56.7 19.4 %constant_dynamic-update-slice_fusion = bf16[2048,13312]{1,0:T(8,128)(2,1)} fusion(bf16[2048,13312]{1,0:T(8,128)(2,1)} %constant_dynamic-update-slice_fusion.1, bf16[2048,6656]{1,0:T(8,128)(2,1)} %param.8), kind=kLoop, calls=%fused_computation.9 | loop fusion | bytes 54525952 | tf_op jit(solution)/shard_map/concatenate | solution.py:13
  76.1 20.5 %convolution_bitcast_fusion = f32[40,13312]{1,0:T(8,128)} fusion(bf16[2048,13312]{1,0:T(8,128)(2,1)} %constant_dynamic-update-slice_fusion, bf16[40,2048]{1,0:T(8,128)(2,1)S(1)} %reshape.5), kind=kOutput, calls=%fused_computation | convolution fusion | flops 2181038080 | bytes 56819712 | tf_op jit(solution)/shard_map/dot_general | solution.py:16
  96.6 14.3 %fusion.2 = f32[40,6656]{1,0:T(8,128)} fusion(bf16[40,2048]{1,0:T(8,128)(2,1)S(1)} %reshape.9, bf16[6656,2048]{1,0:T(8,128)(2,1)} %param.9), kind=kOutput, calls=%fused_computation.12 | convolution fusion | flops 1090519040 | bytes 28491776 | tf_op jit(solution)/shard_map/dot_general | solution.py:35
  110.9 0.0 all-reduce.9.cloned.1.call-update
  110.9 0.0 all-gather.6.cloned.1.call-start
  111.0 0.6 dynamic-slice
  111.6 0.6 dynamic-slice.2
  113.5 68.2 %all-reduce.9.cloned.1.call-done = (f32[40,13312]{1,0:T(8,128)}, f32[40,6656]{1,0:T(8,128)}) async-done(((f32[40,13312]{1,0:T(8,128)}, f32[40,6656]{1,0:T(8,128)}), (f32[40,13312]{1,0:T(8,128)}, f32[40,6656]{1,0:T(8,128)})) %all-reduce.9.cloned.1.call-update) | async-done | bytes 3194896
  181.7 1.8 multiply_convert_fusion.1
  183.5 0.8 maximum_bitcast_fusion
  184.3 8.8 %all-gather.1 = bf16[4,10,6656]{2,1,0:T(8,128)(2,1)S(1)} all-gather(bf16[1,10,6656]{2,1,0:T(8,128)(2,1)S(1)} %get-tuple-element.8), channel_id=1, replica_groups=mesh['grp'=2,'blk'=4,'bulk'=4] {'bulk'}, dimensions={0}, use_global_device_ids=true | all-gather | bytes 665600 | tf_op jit(solution)/shard_map/all_gather | solution.py:25
  193.1 0.2 reshape.7
  193.3 11.3 %fusion.1 = f32[40,2048]{1,0:T(8,128)S(1)} fusion(bf16[40,6656]{1,0:T(8,128)(2,1)S(1)} %reshape.7, bf16[6656,2048]{1,0:T(8,128)(2,1)} %param.9), kind=kOutput, calls=%fused_computation.11 | convolution fusion | flops 1090519040 | bytes 28123136 | tf_op jit(solution)/shard_map/dot_general | solution.py:28
  204.6 0.3 all-gather.6.cloned.1.call-done
  204.8 1.9 reshape.11
  206.7 22.5 %fusion.3 = f32[40,2048]{1,0:T(8,128)S(1)} fusion(bf16[40,13312]{1,0:T(8,128)(2,1)S(1)} %reshape.11, bf16[2048,13312]{1,0:T(8,128)(2,1)} %constant_dynamic-update-slice_fusion), kind=kOutput, calls=%fused_computation.13 | convolution fusion | flops 2181038080 | bytes 55918592 | tf_op jit(solution)/shard_map/dot_general | solution.py:48
  229.2 32.1 %all-reduce.10 = (bf16[40,2048]{1,0:T(8,128)(2,1)S(1)}, bf16[40,2048]{1,0:T(8,128)(2,1)S(1)}) all-reduce(f32[40,2048]{1,0:T(8,128)S(1)} %fusion.1, f32[40,2048]{1,0:T(8,128)S(1)} %fusion.3), channel_id=3, replica_groups=mesh['grp'=2,'blk'=4,'bulk'=4] {'blk'}, use_global_device_ids=true, to_apply=%region_1.0.clone | all-reduce | flops 163840 | bytes 983040
  261.3 0.7 dynamic-slice_convert_fusion
  (9 shorter events, 0.0 us)
Async XLA Ops:
  7.2 19.3 %copy-start = (bf16[10,2048]{1,0:T(8,128)(2,1)S(1)}, bf16[10,2048]{1,0:T(8,128)(2,1)}, u32[]{:S(2)}) copy-start(bf16[10,2048]{1,0:T(8,128)(2,1)} %param.5) | copy-start | bytes 122884
  7.2 35.0 %copy-start.1 = (bf16[10,2048]{1,0:T(8,128)(2,1)S(1)}, bf16[10,2048]{1,0:T(8,128)(2,1)}, u32[]{:S(2)}) copy-start(bf16[10,2048]{1,0:T(8,128)(2,1)} %param.6) | copy-start | bytes 122884
  7.2 174.5 %all-reduce.9.cloned.1.call-start = ((), (), s32[]{:S(2)}) async-start(), calls=%async_computation.1 | async-start | bytes 6389760
  96.6 14.4 %copy-start.3 = (u32[32]{0:T(128)S(1)}, u32[32]{0:T(128)}, u32[]{:S(2)}) copy-start(u32[32]{0:T(128)} %constant.6) | copy-start | bytes 388
  96.6 15.0 %copy-start.2 = (u32[32]{0:T(128)S(1)}, u32[32]{0:T(128)}, u32[]{:S(2)}) copy-start(u32[32]{0:T(128)} %constant.10) | copy-start | bytes 388
  110.9 93.9 %all-gather.6.cloned.1.call-start = ((), (), s32[]{:S(2)}) async-start(), calls=%async_computation | async-start | bytes 2129920 | tf_op jit(solution)/shard_map/all_gather | solution.py:45
Sparse Core Ops, SparseCore 0:
  111.1 70.5 all-reduce.8
  184.4 20.3 all-gather.5
where the time goes:
time: 269 us
  blocking collectives  71 us (26%)
  matrix products  68.6 us (26%)
  waiting for transfers between devices  68.5 us (25%)
  local copies, waits for them, and re-layouts  42.7 us (16%)
  between operations  15.4 us (6%)
    unnamed x3, waiting for transfers between devices  68.3 us
    unnamed x1, blocking collectives  32.1 us
    unnamed x15, local copies, waits for them, and re-layouts  22.6 us
    dot_general x1, matrix products, per_device(): lax.dot_general(block, paired, (((1,), (1,)), ((), ())), preferred_elemen...  22.5 us
    dot_general x1, matrix products, per_device(): jnp.dot(block, paired, preferred_element_type=jnp.float32)  20.5 us
    concatenate x1, local copies, waits for them, and re-layouts, per_device(): paired = jnp.concatenate([gate_weight, up_weight], axis=1)  19.4 us
    all_gather x1, blocking collectives, per_device(): lax.all_gather(tokens, 'blk', axis=0, tiled=True)  15.6 us
    all_gather x1, blocking collectives, per_device(): lax.all_gather(cotangent, 'blk', axis=0, tiled=True)  14.4 us
  transfers between devices with their start and end apart: 2, of which 2 were waited for; matrix products, arithmetic and copies ran while one was open for 5% of the time, Pallas kernels for 0%

commit v1 on v0

v1 whole, which is shorter than its diff:
```python
import functools

import jax
import jax.numpy as jnp
from jax import lax
from jax.experimental import pallas as pl
from jax.experimental.pallas import tpu as pltpu
from jax.sharding import PartitionSpec as P

F32 = jnp.float32
BF16 = jnp.bfloat16
NT = (((1,), (1,)), ((), ()))
VMEM_LIMIT = 56 * 2**20


def swap(value, axis, size, bit):
    return lax.ppermute(value, axis, [(i, i ^ bit) for i in range(size)])


def bits(size, first=1):
    out = []
    while first < size:
        out.append(first)
        first *= 2
    return out


def tile(extent, largest):
    best = 128
    for t in range(128, largest + 1, 128):
        if extent % t == 0:
            best = t
    return best


def up_kernel(half, where, tok, cot, gate_w, up_w, down_w, keep, send, acc):
    step = pl.program_id(0)

    @pl.when(step == 0)
    def _():
        acc[...] = jnp.zeros_like(acc)

    acc[0] += jnp.dot(tok[...], gate_w[...], preferred_element_type=F32)
    acc[1] += jnp.dot(tok[...], up_w[...], preferred_element_type=F32)
    acc[2] += lax.dot_general(cot[...], down_w[...], NT, preferred_element_type=F32)

    @pl.when(step == pl.num_programs(0) - 1)
    def _():
        mine = pl.multiple_of(where[1] * half, 8)
        other = pl.multiple_of((1 - where[1]) * half, 8)
        keep[...] = acc[:, pl.ds(mine, half), :]
        send[...] = acc[:, pl.ds(other, half), :]


def up_call(where, tok, cot, gate_w, up_w, down_w, width, chunk, chunks):
    rows, feats = tok.shape
    half = rows // 2
    kt = tile(feats, 256)
    out = jax.ShapeDtypeStruct((3, half, width), F32)
    return pl.pallas_call(
        functools.partial(up_kernel, half),
        grid_spec=pltpu.PrefetchScalarGridSpec(
            num_scalar_prefetch=1,
            grid=(feats // kt,),
            in_specs=[
                pl.BlockSpec((rows, kt), lambda k, w: (0, k)),
                pl.BlockSpec((rows, kt), lambda k, w: (0, k)),
                pl.BlockSpec((kt, width), lambda k, w: (k, w[0] * chunks + chunk)),
                pl.BlockSpec((kt, width), lambda k, w: (k, w[0] * chunks + chunk)),
                pl.BlockSpec((width, kt), lambda k, w: (w[0] * chunks + chunk, k)),
            ],
            out_specs=[
                pl.BlockSpec((3, half, width), lambda k, w: (0, 0, 0)),
                pl.BlockSpec((3, half, width), lambda k, w: (0, 0, 0)),
            ],
            scratch_shapes=[pltpu.VMEM((3, rows, width), F32)],
        ),
        out_shape=[out, out],
        compiler_params=pltpu.CompilerParams(vmem_limit_bytes=VMEM_LIMIT),
        cost_estimate=pl.CostEstimate(
            flops=6 * rows * feats * width, bytes_accessed=6 * feats * width, transcendentals=0
        ),
        name="up",
    )(where, tok, cot, gate_w, up_w, down_w)


def down_kernel(half, padded, first, where, own, other, gate_w, up_w, down_w, *rest):
    if first:
        out, lhs = rest
    else:
        prev, out, lhs = rest

    @pl.when(pl.program_id(0) == 0)
    def _():
        lhs[:, :padded, :] = own[...]
        lhs[:, padded:, :] = other[...]

    mixed = jnp.dot(lhs[0], down_w[...], preferred_element_type=F32)
    grad = lax.dot_general(lhs[1], gate_w[...], NT, preferred_element_type=F32)
    grad += lax.dot_general(lhs[2], up_w[...], NT, preferred_element_type=F32)
    mine = pl.ds(pl.multiple_of(where[1] * half, 8), half)
    theirs = pl.ds(pl.multiple_of((1 - where[1]) * half, 8), half)
    for i, value in enumerate((mixed, grad)):
        a, b = value[:half], value[padded : padded + half]
        if not first:
            a, b = a + prev[i, mine, :], b + prev[i, theirs, :]
        out[i, mine, :] = a
        out[i, theirs, :] = b


def down_call(where, own, other, gate_w, up_w, down_w, prev, half, chunk, chunks):
    _, padded, width = own.shape
    feats = gate_w.shape[0]
    nt = tile(feats, 256)
    first = prev is None
    extra = [] if first else [pl.BlockSpec((2, 2 * half, nt), lambda j, w: (0, 0, j))]
    return pl.pallas_call(
        functools.partial(down_kernel, half, padded, first),
        grid_spec=pltpu.PrefetchScalarGridSpec(
            num_scalar_prefetch=1,
            grid=(feats // nt,),
            in_specs=[
                pl.BlockSpec((3, padded, width), lambda j, w: (0, 0, 0)),
                pl.BlockSpec((3, padded, width), lambda j, w: (0, 0, 0)),
                pl.BlockSpec((nt, width), lambda j, w: (j, w[0] * chunks + chunk)),
                pl.BlockSpec((nt, width), lambda j, w: (j, w[0] * chunks + chunk)),
                pl.BlockSpec((width, nt), lambda j, w: (w[0] * chunks + chunk, j)),
            ]
            + extra,
            out_specs=pl.BlockSpec((2, 2 * half, nt), lambda j, w: (0, 0, j)),
            scratch_shapes=[pltpu.VMEM((3, 2 * padded, width), BF16)],
        ),
        out_shape=jax.ShapeDtypeStruct((2, 2 * half, feats), F32),
        compiler_params=pltpu.CompilerParams(vmem_limit_bytes=VMEM_LIMIT),
        cost_estimate=pl.CostEstimate(
            flops=6 * 2 * half * feats * width, bytes_accessed=6 * feats * width, transcendentals=0
        ),
        name="down",
    )(where, own, other, gate_w, up_w, down_w, *([] if first else [prev]))


def per_device(sizes, tokens, cotangent, gate_weight, up_weight, down_weight):
    grp, blk, bulk = sizes["grp"], sizes["blk"], sizes["bulk"]
    units = gate_weight.shape[1]
    split = units % (grp * 128) == 0
    parts = grp if split else 1
    width = units // parts
    chunks = 2 if width % 256 == 0 else 1
    width //= chunks

    hops = [("blk", blk, b) for b in reversed(bits(blk))]
    if split:
        hops += [("grp", grp, b) for b in bits(grp)]
    tok, cot = tokens, cotangent
    for hop in hops:
        tok = jnp.concatenate([tok, swap(tok, *hop)], axis=0)
        cot = jnp.concatenate([cot, swap(cot, *hop)], axis=0)
    rows = tok.shape[0]
    half = rows // 2
    padded = -(-half // 16) * 16

    core = lax.axis_index("bulk") % 2
    group = lax.axis_index("grp") if split else jnp.int32(0)
    where = jnp.stack([group, core]).astype(jnp.int32)

    partial = [
        up_call(where, tok, cot, gate_weight, up_weight, down_weight, width, c, chunks)
        for c in range(chunks)
    ]
    total = None
    for c in range(chunks):
        keep, send = partial[c]
        sums = keep + swap(send, "bulk", bulk, 1)
        for b in bits(bulk, 2):
            sums = sums + swap(sums.astype(BF16), "bulk", bulk, b).astype(F32)
        gate, upward, back = sums[0], sums[1], sums[2]
        sigma = jax.nn.sigmoid(gate)
        hidden = gate * sigma * upward
        d_up = back * gate * sigma
        d_gate = back * upward * sigma * (1.0 + gate * (1.0 - sigma))
        own = jnp.stack([hidden, d_gate, d_up]).astype(BF16)
        own = jnp.pad(own, ((0, 0), (0, padded - half), (0, 0)))
        other = swap(own, "bulk", bulk, 1)
        total = down_call(
            where, own, other, gate_weight, up_weight, down_weight, total, half, c, chunks
        )

    for hop in reversed(hops):
        n = total.shape[1] // 2
        total = total[:, :n] + swap(total[:, n:].astype(BF16), *hop).astype(F32)
    total = total.astype(BF16)
    return total[0], total[1]


def solution(mesh):
    return jax.shard_map(
        functools.partial(per_device, dict(mesh.shape)),
        mesh=mesh,
        in_specs=(
            P(("grp", "blk"), "bulk"),
            P(("grp", "blk"), "bulk"),
            P("bulk", "blk"),
            P("bulk", "blk"),
            P("blk", "bulk"),
        ),
        out_specs=(P(("grp", "blk"), "bulk"), P(("grp", "blk"), "bulk")),
        check_vma=False,
    )
```

time: 269 us -> 132 us (0.49)
  blocking collectives: 71 us -> 0 us
  matrix products: 68.6 us -> 0 us
  Pallas kernels: 0 us -> 52.4 us
  local copies, waits for them, and re-layouts: 42.7 us -> 3.42 us
  waiting for transfers between devices: 68.5 us -> 42.8 us
  starting transfers between devices: 0.08 us -> 20.8 us
  between operations: 15.4 us -> 0.77 us
  other arithmetic: 2.57 us -> 10.5 us
    dot_general x4 -> x0, matrix products: 68.6 us -> none  [the longest x1 22.5 us: per_device(): lax.dot_general(block, paired, (((1,), (1,)), ((), ())), preferred_elemen...]
    unnamed x3 -> x0, waiting for transfers between devices: 68.3 us -> none
    pallas_call x0 -> x4, Pallas kernels: none -> 52.4 us  [the longest x2 26.7 us: down_call(): pl.pallas_call(functools.partial(down_kernel, half, padded, first), grid_...]
    ppermute x0 -> x15, waiting for transfers between devices: none -> 42.8 us  [swap(): return lax.ppermute(value, axis, [(i, i ^ bit) for i in range(size)])]
    all_gather x3 -> x0, blocking collectives: 38.8 us -> none  [the longest x1 15.6 us: per_device(): lax.all_gather(tokens, 'blk', axis=0, tiled=True)]
    unnamed x1 -> x0, blocking collectives: 32.1 us -> none
    unnamed x15 -> x10, local copies, waits for them, and re-layouts: 22.6 us -> 1.57 us
    ppermute x0 -> x15, starting transfers between devices: none -> 20.8 us  [swap(): return lax.ppermute(value, axis, [(i, i ^ bit) for i in range(size)])]
  transfers between devices with their start and end apart: 2 -> 15, of which waited for: 2 -> 12; matrix products, arithmetic and copies ran while one was open for 5% -> 6% of each run, Pallas kernels for 0% -> 20%
where the time goes in v1:
time: 132 us; the launch traced here: 131 us
  Pallas kernels  52.4 us (40%)
  waiting for transfers between devices  42.8 us (32%)
  starting transfers between devices  20.8 us (16%)
  other arithmetic  10.5 us (8%)
  local copies, waits for them, and re-layouts  3.42 us (3%)
    ppermute x15, waiting for transfers between devices, swap(): return lax.ppermute(value, axis, [(i, i ^ bit) for i in range(size)])  42.8 us
    pallas_call x2, Pallas kernels, down_call(): pl.pallas_call(functools.partial(down_kernel, half, padded, first), grid_...  26.7 us
    pallas_call x2, Pallas kernels, up_call(): pl.pallas_call(functools.partial(up_kernel, half), grid_spec=pltpu.Prefet...  25.7 us
    ppermute x15, starting transfers between devices, swap(): return lax.ppermute(value, axis, [(i, i ^ bit) for i in range(size)])  20.8 us
    concatenate x3, other arithmetic, per_device(): tok = jnp.concatenate([tok, swap(tok, *hop)], axis=0)  3.41 us
    concatenate x3, other arithmetic, per_device(): cot = jnp.concatenate([cot, swap(cot, *hop)], axis=0)  3.4 us
  transfers between devices with their start and end apart: 15, of which 12 were waited for; matrix products, arithmetic and copies ran while one was open for 6% of the time, Pallas kernels for 20%

profile of v1, /device:TPU:0, one launch (start us, length us, event | category | flops | bytes accessed | tf_op | source)
XLA Modules:
  0.0 130.7 jit_solution(4321966753746481036)
XLA Ops:
  0.6 4.1 %collective-permute-start = (bf16[10,2048]{1,0:T(8,128)(2,1)}, bf16[10,2048]{1,0:T(8,128)(2,1)S(1)}, u32[]{:S(2)}, u32[]{:S(2)}) collective-permute-start(bf16[10,2048]{1,0:T(8,128)(2,1)} %param.5), channel_id=1, source_target_pairs={{0,8},{4,12},{8,0},{12,4},{1,9},{5,13},{9,1},{13,5},{2,10},{6,14},... | collective-permute-start | bytes 122888 | tf_op jit(solution)/shard_map/ppermute | solution.py:17
  5.4 3.2 %collective-permute-done = bf16[10,2048]{1,0:T(8,128)(2,1)S(1)} collective-permute-done((bf16[10,2048]{1,0:T(8,128)(2,1)}, bf16[10,2048]{1,0:T(8,128)(2,1)S(1)}, u32[]{:S(2)}, u32[]{:S(2)}) %collective-permute-start) | collective-permute-done | bytes 40992 | tf_op jit(solution)/shard_map/ppermute | solution.py:17
  9.5 2.2 %collective-permute-start.1 = (bf16[20,2048]{1,0:T(8,128)(2,1)S(1)}, bf16[20,2048]{1,0:T(8,128)(2,1)S(1)}, u32[]{:S(2)}, u32[]{:S(2)}) collective-permute-start(bf16[20,2048]{1,0:T(8,128)(2,1)S(1)} %pad_maximum_fusion.4), channel_id=1, source_target_pairs={{0,4},{4,0},{8,12},{12,8},{1,5},{5,1},{9,13},{13,9},{2,6},{6,2},{1... | collective-permute-start | bytes 245768 | tf_op jit(solution)/shard_map/ppermute | solution.py:17
  13.0 1.6 %collective-permute-done.1 = bf16[20,2048]{1,0:T(8,128)(2,1)S(1)} collective-permute-done((bf16[20,2048]{1,0:T(8,128)(2,1)S(1)}, bf16[20,2048]{1,0:T(8,128)(2,1)S(1)}, u32[]{:S(2)}, u32[]{:S(2)}) %collective-permute-start.1) | collective-permute-done | bytes 81952 | tf_op jit(solution)/shard_map/ppermute | solution.py:17
  15.5 1.6 %collective-permute-start.2 = (bf16[40,2048]{1,0:T(8,128)(2,1)S(1)}, bf16[40,2048]{1,0:T(8,128)(2,1)S(1)}, u32[]{:S(2)}, u32[]{:S(2)}) collective-permute-start(bf16[40,2048]{1,0:T(8,128)(2,1)S(1)} %pad_maximum_fusion.2), channel_id=1, source_target_pairs={{0,16},{16,0},{1,17},{17,1},{2,18},{18,2},{3,19},{19,3},{4,20},{20... | collective-permute-start | bytes 491528 | tf_op jit(solution)/shard_map/ppermute | solution.py:17
  18.2 1.6 %collective-permute-start.5 = (bf16[40,2048]{1,0:T(8,128)(2,1)S(1)}, bf16[40,2048]{1,0:T(8,128)(2,1)S(1)}, u32[]{:S(2)}, u32[]{:S(2)}) collective-permute-start(bf16[40,2048]{1,0:T(8,128)(2,1)S(1)} %pad_maximum_fusion.3), channel_id=1, source_target_pairs={{0,16},{16,0},{1,17},{17,1},{2,18},{18,2},{3,19},{19,3},{4,20},{20... | collective-permute-start | bytes 491528 | tf_op jit(solution)/shard_map/ppermute | solution.py:17
  19.7 3.0 %collective-permute-done.2 = bf16[40,2048]{1,0:T(8,128)(2,1)S(1)} collective-permute-done((bf16[40,2048]{1,0:T(8,128)(2,1)S(1)}, bf16[40,2048]{1,0:T(8,128)(2,1)S(1)}, u32[]{:S(2)}, u32[]{:S(2)}) %collective-permute-start.2) | collective-permute-done | bytes 163872 | tf_op jit(solution)/shard_map/ppermute | solution.py:17
  22.7 1.6 %pad_maximum_fusion.tok = bf16[80,2048]{1,0:T(8,128)(2,1)} fusion(bf16[40,2048]{1,0:T(8,128)(2,1)S(1)} %collective-permute-done.2, bf16[20,2048]{1,0:T(8,128)(2,1)S(1)} %collective-permute-done.1, bf16[10,2048]{1,0:T(8,128)(2,1)S(1)} %collective-permute-done, bf16[10,2048]{1,0:T(8,128)(2,1)} %param.5), kind=kLoop, calls=%fused_computation.17 | loop fusion | flops 1310720 | bytes 655360 | tf_op jit(solution)/shard_map/concatenate | solution.py:156
  24.5 1.6 %pad_maximum_fusion.1.cot = bf16[80,2048]{1,0:T(8,128)(2,1)} fusion(bf16[40,2048]{1,0:T(8,128)(2,1)S(1)} %collective-permute-done.5, bf16[20,2048]{1,0:T(8,128)(2,1)S(1)} %collective-permute-done.4, bf16[10,2048]{1,0:T(8,128)(2,1)S(1)} %collective-permute-done.3, bf16[10,2048]{1,0:T(8,128)(2,1)} %param.6), kind=kLoop, calls=%fused_computation.18 | loop fusion | flops 1310720 | bytes 655360 | tf_op jit(solution)/shard_map/concatenate | solution.py:157
  26.2 12.8 %up.2 = (f32[3,40,1664]{2,1,0:T(8,128)}, f32[3,40,1664]{2,1,0:T(8,128)}) custom-call(s32[2]{0:T(128)} %pad_add_fusion.where, bf16[80,2048]{1,0:T(8,128)(2,1)} %pad_maximum_fusion.tok, bf16[80,2048]{1,0:T(8,128)(2,1)} %pad_maximum_fusion.1.cot, bf16[2048,6656]{1,0:T(8,128)(2,1)} %gate_w.7, bf16[2048,6656]{1,0:T(8,128)(2,1)} %up_w.7, bf16[6656,2048]{1,0:T(8,128)(2,1)} %down_w.7), custom_call_target="tpu_custom_call" | custom-call | flops 1635778560 | bytes 20447232 | tf_op jit(solution)/shard_map/up/pallas_call | solution.py:60
  39.0 12.9 %up.3 = (f32[3,40,1664]{2,1,0:T(8,128)}, f32[3,40,1664]{2,1,0:T(8,128)}) custom-call(s32[2]{0:T(128)} %pad_add_fusion.where, bf16[80,2048]{1,0:T(8,128)(2,1)} %pad_maximum_fusion.tok, bf16[80,2048]{1,0:T(8,128)(2,1)} %pad_maximum_fusion.1.cot, bf16[2048,6656]{1,0:T(8,128)(2,1)} %gate_w.7, bf16[2048,6656]{1,0:T(8,128)(2,1)} %up_w.7, bf16[6656,2048]{1,0:T(8,128)(2,1)} %down_w.7), custom_call_target="tpu_custom_call" | custom-call | flops 1635778560 | bytes 20447232 | tf_op jit(solution)/shard_map/up/pallas_call | solution.py:60
  52.4 1.4 %collective-permute-start.7 = (bf16[3,40,1664]{2,1,0:T(8,128)(2,1)S(1)}, bf16[3,40,1664]{2,1,0:T(8,128)(2,1)S(1)}, u32[]{:S(2)}, u32[]{:S(2)}) collective-permute-start(bf16[3,40,1664]{2,1,0:T(8,128)(2,1)S(1)} %get-tuple-element.12), channel_id=1, source_target_pairs={{0,2},{1,3},{2,0},{3,1},{4,6},{5,7},{6,4},{7,5},{8,10},{9,11},{10,... | collective-permute-start | bytes 1198088 | tf_op jit(solution)/shard_map/ppermute | solution.py:17
  54.4 1.3 fusion.11
  55.7 1.5 %collective-permute-start.10 = (bf16[3,40,1664]{2,1,0:T(8,128)(2,1)S(1)}, bf16[3,40,1664]{2,1,0:T(8,128)(2,1)S(1)}, u32[]{:S(2)}, u32[]{:S(2)}) collective-permute-start(bf16[3,40,1664]{2,1,0:T(8,128)(2,1)S(1)} %get-tuple-element.10), channel_id=1, source_target_pairs={{0,2},{1,3},{2,0},{3,1},{4,6},{5,7},{6,4},{7,5},{8,10},{9,11},{10,... | collective-permute-start | bytes 1198088 | tf_op jit(solution)/shard_map/ppermute | solution.py:17
  57.1 7.4 %collective-permute-done.7 = bf16[3,40,1664]{2,1,0:T(8,128)(2,1)S(1)} collective-permute-done((bf16[3,40,1664]{2,1,0:T(8,128)(2,1)S(1)}, bf16[3,40,1664]{2,1,0:T(8,128)(2,1)S(1)}, u32[]{:S(2)}, u32[]{:S(2)}) %collective-permute-start.7) | collective-permute-done | bytes 399392 | tf_op jit(solution)/shard_map/ppermute | solution.py:17
  64.8 7.5 %collective-permute-done.10 = bf16[3,40,1664]{2,1,0:T(8,128)(2,1)S(1)} collective-permute-done((bf16[3,40,1664]{2,1,0:T(8,128)(2,1)S(1)}, bf16[3,40,1664]{2,1,0:T(8,128)(2,1)S(1)}, u32[]{:S(2)}, u32[]{:S(2)}) %collective-permute-start.10) | collective-permute-done | bytes 399392 | tf_op jit(solution)/shard_map/ppermute | solution.py:17
  75.3 13.2 %down.2.rest_0_ = f32[2,80,2048]{2,1,0:T(8,128)} custom-call(s32[2]{0:T(128)} %pad_add_fusion.where, bf16[3,48,1664]{2,1,0:T(8,128)(2,1)} %copy-done, bf16[3,48,1664]{2,1,0:T(8,128)(2,1)} %copy-done.3, bf16[2048,6656]{1,0:T(8,128)(2,1)} %gate_w.7, bf16[2048,6656]{1,0:T(8,128)(2,1)} %up_w.7, bf16[6656,2048]{1,0:T(8,128)(2,1)} %down_w.7), custom_call_target="tpu_custom_call" | custom-call | flops 1635778560 | bytes 20447232 | tf_op jit(solution)/shard_map/down/pallas_call | solution.py:117
  89.3 13.5 %down.3 = f32[2,80,2048]{2,1,0:T(8,128)} custom-call(s32[2]{0:T(128)} %pad_add_fusion.where, bf16[3,48,1664]{2,1,0:T(8,128)(2,1)} %copy-done.1, bf16[3,48,1664]{2,1,0:T(8,128)(2,1)} %copy-done.4, bf16[2048,6656]{1,0:T(8,128)(2,1)} %gate_w.7, bf16[2048,6656]{1,0:T(8,128)(2,1)} %up_w.7, bf16[6656,2048]{1,0:T(8,128)(2,1)} %down_w.7, f32[2,80,2048]{2,1,0:T(8,128)} %down.2.rest_0_), custom_call_target="tpu_custom_call" | custom-call | flops 1635778560 | bytes 20447232 | tf_op jit(solution)/shard_map/down/pallas_call | solution.py:117
  103.9 1.4 %collective-permute-start.12 = (bf16[2,40,2048]{2,1,0:T(8,128)(2,1)S(1)}, bf16[2,40,2048]{2,1,0:T(8,128)(2,1)S(1)}, u32[]{:S(2)}, u32[]{:S(2)}) collective-permute-start(bf16[2,40,2048]{2,1,0:T(8,128)(2,1)S(1)} %slice.97), channel_id=1, source_target_pairs={{0,16},{16,0},{1,17},{17,1},{2,18},{18,2},{3,19},{19,3},{4,20},{20... | collective-permute-start | bytes 983048 | tf_op jit(solution)/shard_map/ppermute | solution.py:17
  105.4 8.4 %collective-permute-done.12 = bf16[2,40,2048]{2,1,0:T(8,128)(2,1)S(1)} collective-permute-done((bf16[2,40,2048]{2,1,0:T(8,128)(2,1)S(1)}, bf16[2,40,2048]{2,1,0:T(8,128)(2,1)S(1)}, u32[]{:S(2)}, u32[]{:S(2)}) %collective-permute-start.12) | collective-permute-done | bytes 327712 | tf_op jit(solution)/shard_map/ppermute | solution.py:17
  114.9 2.1 %collective-permute-start.13 = (bf16[2,20,2048]{2,1,0:T(8,128)(2,1)S(1)}, bf16[2,20,2048]{2,1,0:T(8,128)(2,1)S(1)}, u32[]{:S(2)}, u32[]{:S(2)}) collective-permute-start(bf16[2,20,2048]{2,1,0:T(8,128)(2,1)S(1)} %slice.98), channel_id=1, source_target_pairs={{0,4},{4,0},{8,12},{12,8},{1,5},{5,1},{9,13},{13,9},{2,6},{6,2},{1... | collective-permute-start | bytes 491528 | tf_op jit(solution)/shard_map/ppermute | solution.py:17
  117.0 4.4 %collective-permute-done.13 = bf16[2,20,2048]{2,1,0:T(8,128)(2,1)S(1)} collective-permute-done((bf16[2,20,2048]{2,1,0:T(8,128)(2,1)S(1)}, bf16[2,20,2048]{2,1,0:T(8,128)(2,1)S(1)}, u32[]{:S(2)}, u32[]{:S(2)}) %collective-permute-start.13) | collective-permute-done | bytes 163872 | tf_op jit(solution)/shard_map/ppermute | solution.py:17
  121.5 3.3 %collective-permute-start.14 = (bf16[2,10,2048]{2,1,0:T(8,128)(2,1)S(1)}, bf16[2,10,2048]{2,1,0:T(8,128)(2,1)S(1)}, u32[]{:S(2)}, u32[]{:S(2)}) collective-permute-start(bf16[2,10,2048]{2,1,0:T(8,128)(2,1)S(1)} %slice.99), channel_id=1, source_target_pairs={{0,8},{4,12},{8,0},{12,4},{1,9},{5,13},{9,1},{13,5},{2,10},{6,14},... | collective-permute-start | bytes 245768 | tf_op jit(solution)/shard_map/ppermute | solution.py:17
  124.8 5.2 %collective-permute-done.14 = bf16[2,10,2048]{2,1,0:T(8,128)(2,1)S(1)} collective-permute-done((bf16[2,10,2048]{2,1,0:T(8,128)(2,1)S(1)}, bf16[2,10,2048]{2,1,0:T(8,128)(2,1)S(1)}, u32[]{:S(2)}, u32[]{:S(2)}) %collective-permute-start.14) | collective-permute-done | bytes 81952 | tf_op jit(solution)/shard_map/ppermute | solution.py:17
  (42 shorter events, 13.0 us)
Async XLA Ops:
  0.6 8.0 %collective-permute-start = (bf16[10,2048]{1,0:T(8,128)(2,1)}, bf16[10,2048]{1,0:T(8,128)(2,1)S(1)}, u32[]{:S(2)}, u32[]{:S(2)}) collective-permute-start(bf16[10,2048]{1,0:T(8,128)(2,1)} %param.5), channel_id=1, source_target_pairs={{0,8},{4,12},{8,0},{12,4},{1,9},{5,13},{9,1},{13,5},{2,10},{6,14},... | collective-permute-start | bytes 122888 | tf_op jit(solution)/shard_map/ppermute | solution.py:17
  4.7 7.0 %collective-permute-start.3 = (bf16[10,2048]{1,0:T(8,128)(2,1)}, bf16[10,2048]{1,0:T(8,128)(2,1)S(1)}, u32[]{:S(2)}, u32[]{:S(2)}) collective-permute-start(bf16[10,2048]{1,0:T(8,128)(2,1)} %param.6), channel_id=1, source_target_pairs={{0,8},{4,12},{8,0},{12,4},{1,9},{5,13},{9,1},{13,5},{2,10},{6,14},... | collective-permute-start | bytes 122888 | tf_op jit(solution)/shard_map/ppermute | solution.py:17
  9.5 5.2 %collective-permute-start.1 = (bf16[20,2048]{1,0:T(8,128)(2,1)S(1)}, bf16[20,2048]{1,0:T(8,128)(2,1)S(1)}, u32[]{:S(2)}, u32[]{:S(2)}) collective-permute-start(bf16[20,2048]{1,0:T(8,128)(2,1)S(1)} %pad_maximum_fusion.4), channel_id=1, source_target_pairs={{0,4},{4,0},{8,12},{12,8},{1,5},{5,1},{9,13},{13,9},{2,6},{6,2},{1... | collective-permute-start | bytes 245768 | tf_op jit(solution)/shard_map/ppermute | solution.py:17
  12.6 4.7 %collective-permute-start.4 = (bf16[20,2048]{1,0:T(8,128)(2,1)S(1)}, bf16[20,2048]{1,0:T(8,128)(2,1)S(1)}, u32[]{:S(2)}, u32[]{:S(2)}) collective-permute-start(bf16[20,2048]{1,0:T(8,128)(2,1)S(1)} %pad_maximum_fusion.5), channel_id=1, source_target_pairs={{0,4},{4,0},{8,12},{12,8},{1,5},{5,1},{9,13},{13,9},{2,6},{6,2},{1... | collective-permute-start | bytes 245768 | tf_op jit(solution)/shard_map/ppermute | solution.py:17
  15.5 7.2 %collective-permute-start.2 = (bf16[40,2048]{1,0:T(8,128)(2,1)S(1)}, bf16[40,2048]{1,0:T(8,128)(2,1)S(1)}, u32[]{:S(2)}, u32[]{:S(2)}) collective-permute-start(bf16[40,2048]{1,0:T(8,128)(2,1)S(1)} %pad_maximum_fusion.2), channel_id=1, source_target_pairs={{0,16},{16,0},{1,17},{17,1},{2,18},{18,2},{3,19},{19,3},{4,20},{20... | collective-permute-start | bytes 491528 | tf_op jit(solution)/shard_map/ppermute | solution.py:17
  18.2 6.4 %collective-permute-start.5 = (bf16[40,2048]{1,0:T(8,128)(2,1)S(1)}, bf16[40,2048]{1,0:T(8,128)(2,1)S(1)}, u32[]{:S(2)}, u32[]{:S(2)}) collective-permute-start(bf16[40,2048]{1,0:T(8,128)(2,1)S(1)} %pad_maximum_fusion.3), channel_id=1, source_target_pairs={{0,16},{16,0},{1,17},{17,1},{2,18},{18,2},{3,19},{19,3},{4,20},{20... | collective-permute-start | bytes 491528 | tf_op jit(solution)/shard_map/ppermute | solution.py:17
  39.0 13.3 %copy-start.2 = (f32[3,40,1664]{2,1,0:T(8,128)S(1)}, f32[3,40,1664]{2,1,0:T(8,128)}, u32[]{:S(2)}) copy-start(f32[3,40,1664]{2,1,0:T(8,128)} %get-tuple-element.6) | copy-start | bytes 2396164
  39.0 13.3 %collective-permute-start.6 = (f32[3,40,1664]{2,1,0:T(8,128)}, f32[3,40,1664]{2,1,0:T(8,128)S(1)}, u32[]{:S(2)}, u32[]{:S(2)}) collective-permute-start(f32[3,40,1664]{2,1,0:T(8,128)} %get-tuple-element.7), channel_id=1, source_target_pairs={{0,1},{1,0},{2,3},{3,2},{4,5},{5,4},{6,7},{7,6},{8,9},{9,8},{10,11... | collective-permute-start | bytes 2396168 | tf_op jit(solution)/shard_map/ppermute | solution.py:17
  51.9 2.5 %collective-permute-start.9 = (f32[3,40,1664]{2,1,0:T(8,128)}, f32[3,40,1664]{2,1,0:T(8,128)S(1)}, u32[]{:S(2)}, u32[]{:S(2)}) collective-permute-start(f32[3,40,1664]{2,1,0:T(8,128)} %get-tuple-element.9), channel_id=1, source_target_pairs={{0,1},{1,0},{2,3},{3,2},{4,5},{5,4},{6,7},{7,6},{8,9},{9,8},{10,11... | collective-permute-start | bytes 2396168 | tf_op jit(solution)/shard_map/ppermute | solution.py:17
  52.4 12.2 %collective-permute-start.7 = (bf16[3,40,1664]{2,1,0:T(8,128)(2,1)S(1)}, bf16[3,40,1664]{2,1,0:T(8,128)(2,1)S(1)}, u32[]{:S(2)}, u32[]{:S(2)}) collective-permute-start(bf16[3,40,1664]{2,1,0:T(8,128)(2,1)S(1)} %get-tuple-element.12), channel_id=1, source_target_pairs={{0,2},{1,3},{2,0},{3,1},{4,6},{5,7},{6,4},{7,5},{8,10},{9,11},{10,... | collective-permute-start | bytes 1198088 | tf_op jit(solution)/shard_map/ppermute | solution.py:17
  55.7 16.6 %collective-permute-start.10 = (bf16[3,40,1664]{2,1,0:T(8,128)(2,1)S(1)}, bf16[3,40,1664]{2,1,0:T(8,128)(2,1)S(1)}, u32[]{:S(2)}, u32[]{:S(2)}) collective-permute-start(bf16[3,40,1664]{2,1,0:T(8,128)(2,1)S(1)} %get-tuple-element.10), channel_id=1, source_target_pairs={{0,2},{1,3},{2,0},{3,1},{4,6},{5,7},{6,4},{7,5},{8,10},{9,11},{10,... | collective-permute-start | bytes 1198088 | tf_op jit(solution)/shard_map/ppermute | solution.py:17
  72.6 1.9 %copy-start = (bf16[3,48,1664]{2,1,0:T(8,128)(2,1)}, bf16[3,48,1664]{2,1,0:T(8,128)(2,1)S(1)}, u32[]{:S(2)}) copy-start(bf16[3,48,1664]{2,1,0:T(8,128)(2,1)S(1)} %fusion.9.own) | copy-start | bytes 1437700
  72.6 1.9 %collective-permute-start.11 = (bf16[3,48,1664]{2,1,0:T(8,128)(2,1)S(1)}, bf16[3,48,1664]{2,1,0:T(8,128)(2,1)S(1)}, u32[]{:S(2)}, u32[]{:S(2)}) collective-permute-start(bf16[3,48,1664]{2,1,0:T(8,128)(2,1)S(1)} %fusion.9.own), channel_id=1, source_target_pairs={{0,1},{1,0},{2,3},{3,2},{4,5},{5,4},{6,7},{7,6},{8,9},{9,8},{10,11... | collective-permute-start | bytes 1437704 | tf_op jit(solution)/shard_map/ppermute | solution.py:17
  72.7 15.8 %copy-start.1 = (bf16[3,48,1664]{2,1,0:T(8,128)(2,1)}, bf16[3,48,1664]{2,1,0:T(8,128)(2,1)S(1)}, u32[]{:S(2)}) copy-start(bf16[3,48,1664]{2,1,0:T(8,128)(2,1)S(1)} %fusion.7.own) | copy-start | bytes 1437700
  72.7 15.8 %collective-permute-start.8 = (bf16[3,48,1664]{2,1,0:T(8,128)(2,1)S(1)}, bf16[3,48,1664]{2,1,0:T(8,128)(2,1)S(1)}, u32[]{:S(2)}, u32[]{:S(2)}) collective-permute-start(bf16[3,48,1664]{2,1,0:T(8,128)(2,1)S(1)} %fusion.7.own), channel_id=1, source_target_pairs={{0,1},{1,0},{2,3},{3,2},{4,5},{5,4},{6,7},{7,6},{8,9},{9,8},{10,11... | collective-permute-start | bytes 1437704 | tf_op jit(solution)/shard_map/ppermute | solution.py:17
  74.5 0.8 copy-start.3
  88.5 0.8 copy-start.4
  103.9 9.8 %collective-permute-start.12 = (bf16[2,40,2048]{2,1,0:T(8,128)(2,1)S(1)}, bf16[2,40,2048]{2,1,0:T(8,128)(2,1)S(1)}, u32[]{:S(2)}, u32[]{:S(2)}) collective-permute-start(bf16[2,40,2048]{2,1,0:T(8,128)(2,1)S(1)} %slice.97), channel_id=1, source_target_pairs={{0,16},{16,0},{1,17},{17,1},{2,18},{18,2},{3,19},{19,3},{4,20},{20... | collective-permute-start | bytes 983048 | tf_op jit(solution)/shard_map/ppermute | solution.py:17
  114.9 6.5 %collective-permute-start.13 = (bf16[2,20,2048]{2,1,0:T(8,128)(2,1)S(1)}, bf16[2,20,2048]{2,1,0:T(8,128)(2,1)S(1)}, u32[]{:S(2)}, u32[]{:S(2)}) collective-permute-start(bf16[2,20,2048]{2,1,0:T(8,128)(2,1)S(1)} %slice.98), channel_id=1, source_target_pairs={{0,4},{4,0},{8,12},{12,8},{1,5},{5,1},{9,13},{13,9},{2,6},{6,2},{1... | collective-permute-start | bytes 491528 | tf_op jit(solution)/shard_map/ppermute | solution.py:17
  121.5 8.5 %collective-permute-start.14 = (bf16[2,10,2048]{2,1,0:T(8,128)(2,1)S(1)}, bf16[2,10,2048]{2,1,0:T(8,128)(2,1)S(1)}, u32[]{:S(2)}, u32[]{:S(2)}) collective-permute-start(bf16[2,10,2048]{2,1,0:T(8,128)(2,1)S(1)} %slice.99), channel_id=1, source_target_pairs={{0,8},{4,12},{8,0},{12,4},{1,9},{5,13},{9,1},{13,5},{2,10},{6,14},... | collective-permute-start | bytes 245768 | tf_op jit(solution)/shard_map/ppermute | solution.py:17

commit v2 on v0

v2 whole, which is shorter than its diff:
```python
import functools

import jax
import jax.numpy as jnp
from jax import lax
from jax.experimental import pallas as pl
from jax.experimental.pallas import tpu as pltpu
from jax.sharding import PartitionSpec as P

F32 = jnp.float32
BF16 = jnp.bfloat16
NT = (((1,), (1,)), ((), ()))
MIB = 2**20
VMEM = pl.BlockSpec(memory_space=pltpu.VMEM)
SMEM = pl.BlockSpec(memory_space=pltpu.SMEM)
HBM = pl.BlockSpec(memory_space=pltpu.HBM)
ANY = pl.BlockSpec(memory_space=pl.ANY)


def swap(value, axis, size, bit):
    return lax.ppermute(value, axis, [(i, i ^ bit) for i in range(size)])


def bits(size, first=1):
    out = []
    while first < size:
        out.append(first)
        first *= 2
    return out


def resident(x):
    return pltpu.with_memory_space_constraint(x, pltpu.VMEM)


def in_hbm(x):
    return pltpu.with_memory_space_constraint(x, pltpu.HBM)


def cost(flops, nbytes):
    return pl.CostEstimate(flops=flops, bytes_accessed=nbytes, transcendentals=0)


def call(kernel, name, in_specs, out_shape, scratch=(), limit=2, estimate=None):
    many = isinstance(out_shape, (list, tuple))
    return pl.pallas_call(
        kernel,
        in_specs=in_specs,
        out_specs=[VMEM] * len(out_shape) if many else VMEM,
        out_shape=out_shape,
        scratch_shapes=list(scratch),
        compiler_params=pltpu.CompilerParams(vmem_limit_bytes=limit * MIB),
        cost_estimate=estimate,
        name=name,
    )


def fetch(where, weight, dim, whole, start, size, after=()):
    shape = list(weight.shape)
    shape[dim] = size

    def kernel(where, src, *rest):
        out, sem = rest[-2:]
        first = pl.multiple_of(where[0] * whole + start, 128)
        part = src.at[pl.ds(first, size), :] if dim == 0 else src.at[:, pl.ds(first, size)]
        copy = pltpu.make_async_copy(part, out, sem)
        copy.start()
        copy.wait()

    return call(
        kernel,
        "fetch",
        [SMEM, HBM] + [ANY] * len(after),
        pltpu.VMEM(tuple(shape), BF16),
        [pltpu.SemaphoreType.DMA],
        estimate=cost(0, 2 * shape[0] * shape[1]),
    )(where, in_hbm(weight), *after)


def pack(tok_a, tok_b, cot_a, cot_b):
    n, feats = tok_a.shape

    def kernel(ta, tb, ca, cb, out, wide):
        for i, (a, b) in enumerate(((ta, tb), (ca, cb))):
            wide[i, :n, :] = a[...].astype(F32)
            wide[i, n : 2 * n, :] = b[...].astype(F32)
            out[i] = wide[i].astype(BF16)

    return call(
        kernel,
        "pack",
        [VMEM] * 4,
        jax.ShapeDtypeStruct((2, 2 * n, feats), BF16),
        [pltpu.VMEM((2, 2 * n, feats), F32)],
    )(tok_a, tok_b, cot_a, cot_b)


def repack(a, b):
    _, n, feats = a.shape

    def kernel(a, b, out, wide):
        for i in range(2):
            wide[i, :n, :] = a[i].astype(F32)
            wide[i, n : 2 * n, :] = b[i].astype(F32)
            out[i] = wide[i].astype(BF16)

    return call(
        kernel,
        "pack",
        [VMEM] * 2,
        jax.ShapeDtypeStruct((2, 2 * n, feats), BF16),
        [pltpu.VMEM((2, 2 * n, feats), F32)],
        limit=4,
    )(a, b)


def up(where, near, far, gate_w, up_w, down_w, block, after):
    _, half, feats = near.shape
    width = gate_w.shape[1]

    def kernel(where, near, far, gate_w, up_w, down_w, *rest):
        keep, send, wide, lhs = rest[-4:]
        first = where[1] == 0
        for i in range(2):
            a, b = near[i].astype(F32), far[i].astype(F32)
            wide[:half, :] = jnp.where(first, a, b)
            wide[half:, :] = jnp.where(first, b, a)
            lhs[i] = wide[...].astype(BF16)

        @pl.loop(0, width // block)
        def _(step):
            cut = pl.ds(pl.multiple_of(step * block, block), block)
            outs = (
                jnp.dot(lhs[0], gate_w[:, cut], preferred_element_type=F32),
                jnp.dot(lhs[0], up_w[:, cut], preferred_element_type=F32),
                lax.dot_general(lhs[1], down_w[cut, :], NT, preferred_element_type=F32),
            )
            for i, value in enumerate(outs):
                keep[i, :, cut] = value[:half]
                send[i, :, cut] = value[half:]

    out = jax.ShapeDtypeStruct((3, half, width), F32)
    return call(
        kernel,
        "up",
        [SMEM] + [VMEM] * 5 + [ANY] * len(after),
        [out, out],
        [pltpu.VMEM((2 * half, feats), F32), pltpu.VMEM((2, 2 * half, feats), BF16)],
        limit=8,
        estimate=cost(6 * 256 * feats * width, 6 * feats * width),
    )(where, near, far, resident(gate_w), resident(up_w), resident(down_w), *after)


def add(a, b):
    def kernel(a, b, total, rounded):
        value = a[...] + b[...].astype(F32)
        total[...] = value
        rounded[...] = value.astype(BF16)

    return call(
        kernel,
        "add",
        [VMEM] * 2,
        [jax.ShapeDtypeStruct(a.shape, F32), jax.ShapeDtypeStruct(a.shape, BF16)],
    )(a, b)


def activate(sums, got, padded):
    _, half, width = sums.shape

    def kernel(sums, got, out):
        gate = sums[0] + got[0].astype(F32)
        upward = sums[1] + got[1].astype(F32)
        back = sums[2] + got[2].astype(F32)
        sigma = jax.nn.sigmoid(gate)
        hidden = gate * sigma * upward
        d_up = back * gate * sigma
        d_gate = back * upward * sigma * (1.0 + gate * (1.0 - sigma))
        for i, value in enumerate((hidden, d_gate, d_up)):
            if padded > half:
                empty = jnp.zeros((padded - half, width), F32)
                value = jnp.concatenate([value, empty], axis=0)
            out[i] = value.astype(BF16)

    return call(
        kernel,
        "activate",
        [VMEM] * 2,
        jax.ShapeDtypeStruct((3, padded, width), BF16),
        limit=4,
    )(sums, got)


def down(where, own, other, gate_w, up_w, down_w, prev, half, which, last, block):
    _, padded, width = own.shape
    feats = down_w.shape[1] if down_w is not None else gate_w.shape[0]
    weights = ([down_w] if 0 in which else []) + ([gate_w, up_w] if 1 in which else [])
    used = ([0] if 0 in which else []) + ([1, 2] if 1 in which else [])

    def kernel(where, own, other, *rest):
        refs = list(rest)
        mixed_w = refs.pop(0) if 0 in which else None
        grad_w = (refs.pop(0), refs.pop(0)) if 1 in which else None
        before = [refs.pop(0) for _ in which] if prev else None
        lhs = refs.pop()
        first = where[1] == 0
        for i in used:
            lhs[i, :padded, :] = own[i]
            lhs[i, padded:, :] = other[i]

        @pl.loop(0, feats // block)
        def _(step):
            cut = pl.ds(pl.multiple_of(step * block, block), block)
            for n, i in enumerate(which):
                if i == 0:
                    value = jnp.dot(lhs[0], mixed_w[:, cut], preferred_element_type=F32)
                else:
                    value = lax.dot_general(
                        lhs[1], grad_w[0][cut, :], NT, preferred_element_type=F32
                    ) + lax.dot_general(lhs[2], grad_w[1][cut, :], NT, preferred_element_type=F32)
                if prev:
                    value += before[n][:, cut]
                if last:
                    a, b = value[:half], value[padded : padded + half]
                    refs[2 * n][:, cut] = jnp.where(first, a, b)
                    refs[2 * n + 1][:, cut] = jnp.where(first, b, a).astype(BF16)
                else:
                    refs[n][:, cut] = value

    if last:
        shapes = [
            jax.ShapeDtypeStruct((half, feats), F32),
            jax.ShapeDtypeStruct((half, feats), BF16),
        ] * len(which)
    else:
        shapes = [jax.ShapeDtypeStruct((2 * padded, feats), F32)] * len(which)
    return call(
        kernel,
        "down",
        [SMEM] + [VMEM] * (2 + len(weights) + len(which if prev else ())),
        shapes,
        [pltpu.VMEM((3, 2 * padded, width), BF16)],
        limit=8,
        estimate=cost(2 * len(used) * 256 * feats * width, 2 * len(used) * feats * width),
    )(where, own, other, *[resident(w) for w in weights], *(prev or ()))


def fold(keep, got):
    n, feats = keep.shape
    half = n // 2

    def kernel(keep, got, stay, send):
        value = keep[...] + got[...].astype(F32)
        stay[...] = value[:half]
        send[...] = value[half:].astype(BF16)

    return call(
        kernel,
        "fold",
        [VMEM] * 2,
        [jax.ShapeDtypeStruct((half, feats), F32), jax.ShapeDtypeStruct((half, feats), BF16)],
    )(keep, got)


def finish(keep, got):
    def kernel(keep, got, out):
        out[...] = (keep[...] + got[...].astype(F32)).astype(BF16)

    return call(kernel, "finish", [VMEM] * 2, jax.ShapeDtypeStruct(keep.shape, BF16))(keep, got)


def per_device(sizes, tokens, cotangent, gate_weight, up_weight, down_weight):
    grp, blk, bulk = sizes["grp"], sizes["blk"], sizes["bulk"]
    units, feats = gate_weight.shape[1], gate_weight.shape[0]
    split = units % (grp * 128) == 0
    whole = units // grp if split else units
    block = 256 if whole % 256 == 0 else 128
    blocks = whole // block
    cuts = [0, blocks // 2, blocks] if blocks > 1 else [0, blocks]
    chunks = [(a * block, (b - a) * block) for a, b in zip(cuts, cuts[1:])]
    down_block = 256 if feats % 256 == 0 else 128

    core = lax.axis_index("bulk") % 2
    group = lax.axis_index("grp") if split else jnp.int32(0)
    where = jnp.stack([group, core]).astype(jnp.int32)

    hops = [("blk", blk, b) for b in reversed(bits(blk))]
    if split:
        hops += [("grp", grp, b) for b in bits(grp)]
    near = pack(
        tokens, swap(tokens, *hops[0]), cotangent, swap(cotangent, *hops[0])
    )
    for hop in hops[1:-1]:
        near = repack(near, swap(near, *hop))
    far = swap(near, *hops[-1])
    half = near.shape[1]
    padded = -(-half // 16) * 16

    weights = [
        (
            fetch(where, gate_weight, 1, whole, start, size),
            fetch(where, up_weight, 1, whole, start, size),
            fetch(where, down_weight, 0, whole, start, size),
        )
        for start, size in chunks
    ]

    summed = []
    after = ()
    for w in weights:
        keep, send = up(where, near, far, *w, block, after)
        sums, rounded = add(keep, swap(send, "bulk", bulk, 1))
        after = (rounded,)
        summed.append((sums, rounded))

    prev = ()
    for c, (w, (sums, rounded)) in enumerate(zip(weights, summed)):
        for b in bits(bulk, 2)[:-1]:
            sums, rounded = add(sums, swap(rounded, "bulk", bulk, b))
        got = swap(rounded, "bulk", bulk, bits(bulk, 2)[-1])
        own = activate(sums, got, padded)
        other = swap(own, "bulk", bulk, 1)
        if c < len(chunks) - 1:
            prev = down(where, own, other, *w, prev, half, (0, 1), False, down_block)
    first = down(
        where, own, other, None, None, w[2], prev[:1], half, (0,), True, down_block
    )
    second = down(
        where, own, other, w[0], w[1], None, prev[1:], half, (1,), True, down_block
    )
    outs = []
    for stay, send in (first, second):
        for hop in reversed(hops[1:]):
            stay, send = fold(stay, swap(send, *hop))
        outs.append(finish(stay, swap(send, *hops[0])))
    return tuple(outs)


def solution(mesh):
    return jax.shard_map(
        functools.partial(per_device, dict(mesh.shape)),
        mesh=mesh,
        in_specs=(
            P(("grp", "blk"), "bulk"),
            P(("grp", "blk"), "bulk"),
            P("bulk", "blk"),
            P("bulk", "blk"),
            P("blk", "bulk"),
        ),
        out_specs=(P(("grp", "blk"), "bulk"), P(("grp", "blk"), "bulk")),
        check_vma=False,
    )
```

time: 269 us -> 111 us (0.41)
  blocking collectives: 71 us -> 0 us
  matrix products: 68.6 us -> 0 us
  Pallas kernels: 0 us -> 51 us
  local copies, waits for them, and re-layouts: 42.7 us -> 1.68 us
  waiting for transfers between devices: 68.5 us -> 37.9 us
  starting transfers between devices: 0.08 us -> 19.2 us
  between operations: 15.4 us -> 0.8 us
    dot_general x4 -> x0, matrix products: 68.6 us -> none  [the longest x1 22.5 us: per_device(): lax.dot_general(block, paired, (((1,), (1,)), ((), ())), preferred_elemen...]
    unnamed x3 -> x0, waiting for transfers between devices: 68.3 us -> none
    pallas_call x0 -> x23, Pallas kernels: none -> 51 us  [the longest x6 20.9 us: fetch(): call(kernel, 'fetch', [SMEM, HBM] + [ANY] * len(after), pltpu.VMEM(tuple(...]
    all_gather x3 -> x0, blocking collectives: 38.8 us -> none  [the longest x1 15.6 us: per_device(): lax.all_gather(tokens, 'blk', axis=0, tiled=True)]
    ppermute x0 -> x16, waiting for transfers between devices: none -> 37.9 us  [swap(): return lax.ppermute(value, axis, [(i, i ^ bit) for i in range(size)])]
    unnamed x1 -> x0, blocking collectives: 32.1 us -> none
    unnamed x15 -> x4, local copies, waits for them, and re-layouts: 22.6 us -> 1.68 us
    concatenate x1 -> x0, local copies, waits for them, and re-layouts: 19.4 us -> none  [per_device(): paired = jnp.concatenate([gate_weight, up_weight], axis=1)]
  transfers between devices with their start and end apart: 2 -> 16, of which waited for: 2 -> 12; matrix products, arithmetic and copies ran while one was open for 5% -> 0% of each run, Pallas kernels for 0% -> 29%
where the time goes in v2:
time: 111 us
  Pallas kernels  51 us (46%)
  waiting for transfers between devices  37.9 us (34%)
  starting transfers between devices  19.2 us (17%)
  local copies, waits for them, and re-layouts  1.68 us (2%)
    ppermute x16, waiting for transfers between devices, swap(): return lax.ppermute(value, axis, [(i, i ^ bit) for i in range(size)])  37.9 us
    pallas_call x6, Pallas kernels, fetch(): call(kernel, 'fetch', [SMEM, HBM] + [ANY] * len(after), pltpu.VMEM(tuple(...  20.9 us
    ppermute x16, starting transfers between devices, swap(): return lax.ppermute(value, axis, [(i, i ^ bit) for i in range(size)])  19.2 us
    pallas_call x3, Pallas kernels, down(): call(kernel, 'down', [SMEM] + [VMEM] * (2 + len(weights) + len(which if p...  15.8 us
    pallas_call x2, Pallas kernels, up(): call(kernel, 'up', [SMEM] + [VMEM] * 5 + [ANY] * len(after), [out, out],...  12 us
  transfers between devices with their start and end apart: 16, of which 12 were waited for; matrix products, arithmetic and copies ran while one was open for 0% of the time, Pallas kernels for 29%

profile of v2, /device:TPU:0, one launch (start us, length us, event | category | flops | bytes accessed | tf_op | source)
XLA Modules:
  0.0 110.7 jit_solution(2375887142869515412)
XLA Ops:
  0.6 4.1 %collective-permute-start = (bf16[10,2048]{1,0:T(8,128)(2,1)}, bf16[10,2048]{1,0:T(8,128)(2,1)S(1)}, u32[]{:S(2)}, u32[]{:S(2)}) collective-permute-start(bf16[10,2048]{1,0:T(8,128)(2,1)} %ta.1), channel_id=1, source_target_pairs={{0,8},{4,12},{8,0},{12,4},{1,9},{5,13},{9,1},{13,5},{2,10},{6,14},... | collective-permute-start | bytes 122888 | tf_op jit(solution)/shard_map/ppermute | solution.py:21
  4.8 3.8 %collective-permute-done.tb = bf16[10,2048]{1,0:T(8,128)(2,1)S(1)} collective-permute-done((bf16[10,2048]{1,0:T(8,128)(2,1)}, bf16[10,2048]{1,0:T(8,128)(2,1)S(1)}, u32[]{:S(2)}, u32[]{:S(2)}) %collective-permute-start) | collective-permute-done | bytes 40992 | tf_op jit(solution)/shard_map/ppermute | solution.py:21
  8.6 2.8 %collective-permute-done.1.cb = bf16[10,2048]{1,0:T(8,128)(2,1)S(1)} collective-permute-done((bf16[10,2048]{1,0:T(8,128)(2,1)}, bf16[10,2048]{1,0:T(8,128)(2,1)S(1)}, u32[]{:S(2)}, u32[]{:S(2)}) %collective-permute-start.1) | collective-permute-done | bytes 40992 | tf_op jit(solution)/shard_map/ppermute | solution.py:21
  13.9 5.1 %collective-permute-done.2.b = bf16[2,20,2048]{2,1,0:T(8,128)(2,1)S(1)} collective-permute-done((bf16[2,20,2048]{2,1,0:T(8,128)(2,1)S(1)}, bf16[2,20,2048]{2,1,0:T(8,128)(2,1)S(1)}, u32[]{:S(2)}, u32[]{:S(2)}) %collective-permute-start.2) | collective-permute-done | bytes 163872 | tf_op jit(solution)/shard_map/ppermute | solution.py:21
  19.0 2.7 %collective-permute-start.3 = (bf16[2,40,2048]{2,1,0:T(8,128)(2,1)S(1)}, bf16[2,40,2048]{2,1,0:T(8,128)(2,1)S(1)}, u32[]{:S(2)}, u32[]{:S(2)}) collective-permute-start(bf16[2,40,2048]{2,1,0:T(8,128)(2,1)S(1)} %pack.3.near), channel_id=1, source_target_pairs={{0,16},{16,0},{1,17},{17,1},{2,18},{18,2},{3,19},{19,3},{4,20},{20... | collective-permute-start | bytes 983048 | tf_op jit(solution)/shard_map/ppermute | solution.py:21
  21.8 3.3 %fetch.9.gate_w.rest_1_ = bf16[2048,1536]{1,0:T(8,128)(2,1)S(1)} custom-call(s32[2]{0:T(128)S(1)} %pad_add_fusion.where, bf16[2048,6656]{1,0:T(8,128)(2,1)} %src.9), custom_call_target="tpu_custom_call" | custom-call | bytes 6291456 | tf_op jit(solution)/shard_map/fetch/pallas_call | solution.py:70
  25.1 3.3 %fetch.10.up_w.rest_2_ = bf16[2048,1536]{1,0:T(8,128)(2,1)S(1)} custom-call(s32[2]{0:T(128)S(1)} %pad_add_fusion.where, bf16[2048,6656]{1,0:T(8,128)(2,1)} %src.10), custom_call_target="tpu_custom_call" | custom-call | bytes 6291456 | tf_op jit(solution)/shard_map/fetch/pallas_call | solution.py:70
  28.5 3.3 %fetch.11.down_w.rest_0_ = bf16[1536,2048]{1,0:T(8,128)(2,1)S(1)} custom-call(s32[2]{0:T(128)S(1)} %pad_add_fusion.where, bf16[6656,2048]{1,0:T(8,128)(2,1)} %src.11), custom_call_target="tpu_custom_call" | custom-call | bytes 6291456 | tf_op jit(solution)/shard_map/fetch/pallas_call | solution.py:70
  31.8 5.6 %up.2 = (f32[3,40,1536]{2,1,0:T(8,128)S(1)}, f32[3,40,1536]{2,1,0:T(8,128)S(1)}) custom-call(s32[2]{0:T(128)S(1)} %pad_add_fusion.where, bf16[2,40,2048]{2,1,0:T(8,128)(2,1)S(1)} %pack.3.near, bf16[2,40,2048]{2,1,0:T(8,128)(2,1)S(1)} %collective-permute-done.3.far, bf16[2048,1536]{1,0:T(8,128)(2,1)S(1)} %fetch.9.gate_w.rest_1_, ...), custom_call_target="tpu_custom_call" | custom-call | flops 4831838208 | bytes 18874368 | tf_op jit(solution)/shard_map/up/pallas_call | solution.py:143
  37.5 3.6 %fetch.6.gate_w.rest_0_ = bf16[2048,1792]{1,0:T(8,128)(2,1)S(1)} custom-call(s32[2]{0:T(128)S(1)} %pad_add_fusion.where, bf16[2048,6656]{1,0:T(8,128)(2,1)} %src.9), custom_call_target="tpu_custom_call" | custom-call | bytes 7340032 | tf_op jit(solution)/shard_map/fetch/pallas_call | solution.py:70
  41.1 3.6 %fetch.7.up_w.rest_1_ = bf16[2048,1792]{1,0:T(8,128)(2,1)S(1)} custom-call(s32[2]{0:T(128)S(1)} %pad_add_fusion.where, bf16[2048,6656]{1,0:T(8,128)(2,1)} %src.10), custom_call_target="tpu_custom_call" | custom-call | bytes 7340032 | tf_op jit(solution)/shard_map/fetch/pallas_call | solution.py:70
  44.8 3.6 %fetch.8.down_w.rest_0_ = bf16[1792,2048]{1,0:T(8,128)(2,1)S(1)} custom-call(s32[2]{0:T(128)S(1)} %pad_add_fusion.where, bf16[6656,2048]{1,0:T(8,128)(2,1)} %src.11), custom_call_target="tpu_custom_call" | custom-call | bytes 7340032 | tf_op jit(solution)/shard_map/fetch/pallas_call | solution.py:70
  48.6 6.4 %up.3 = (f32[3,40,1792]{2,1,0:T(8,128)S(1)}, f32[3,40,1792]{2,1,0:T(8,128)S(1)}) custom-call(s32[2]{0:T(128)S(1)} %pad_add_fusion.where, bf16[2,40,2048]{2,1,0:T(8,128)(2,1)S(1)} %pack.3.near, bf16[2,40,2048]{2,1,0:T(8,128)(2,1)S(1)} %collective-permute-done.3.far, bf16[2048,1792]{1,0:T(8,128)(2,1)S(1)} %fetch.6.gate_w.rest_0_, ...), custom_call_target="tpu_custom_call" | custom-call | flops 5637144576 | bytes 22020096 | tf_op jit(solution)/shard_map/up/pallas_call | solution.py:143
  59.3 7.7 %collective-permute-done.8.got = bf16[3,40,1536]{2,1,0:T(8,128)(2,1)S(1)} collective-permute-done((bf16[3,40,1536]{2,1,0:T(8,128)(2,1)S(1)}, bf16[3,40,1536]{2,1,0:T(8,128)(2,1)S(1)}, u32[]{:S(2)}, u32[]{:S(2)}) %collective-permute-start.8) | collective-permute-done | bytes 368672 | tf_op jit(solution)/shard_map/ppermute | solution.py:21
  67.3 8.1 %collective-permute-done.6.got = bf16[3,40,1792]{2,1,0:T(8,128)(2,1)S(1)} collective-permute-done((bf16[3,40,1792]{2,1,0:T(8,128)(2,1)S(1)}, bf16[3,40,1792]{2,1,0:T(8,128)(2,1)S(1)}, u32[]{:S(2)}, u32[]{:S(2)}) %collective-permute-start.6) | collective-permute-done | bytes 430112 | tf_op jit(solution)/shard_map/ppermute | solution.py:21
  75.7 6.6 %down.3 = (f32[96,2048]{1,0:T(8,128)S(1)}, f32[96,2048]{1,0:T(8,128)S(1)}) custom-call(s32[2]{0:T(128)S(1)} %pad_add_fusion.where, bf16[3,48,1536]{2,1,0:T(8,128)(2,1)S(1)} %activate.3.own, bf16[3,48,1536]{2,1,0:T(8,128)(2,1)S(1)} %collective-permute-done.9.other, bf16[1536,2048]{1,0:T(8,128)(2,1)S(1)} %fetch.11.down_w.rest_0_, ...), custom_call_target="tpu_custom_call" | custom-call | flops 4831838208 | bytes 18874368 | tf_op jit(solution)/shard_map/down/pallas_call | solution.py:237
  82.3 6.2 %down.5 = (f32[40,2048]{1,0:T(8,128)S(1)}, bf16[40,2048]{1,0:T(8,128)(2,1)S(1)}) custom-call(s32[2]{0:T(128)S(1)} %pad_add_fusion.where, bf16[3,48,1792]{2,1,0:T(8,128)(2,1)S(1)} %activate.2.own, bf16[3,48,1792]{2,1,0:T(8,128)(2,1)S(1)} %collective-permute-done.7.other, bf16[2048,1792]{1,0:T(8,128)(2,1)S(1)} %fetch.6.gate_w.rest_0_, ...), custom_call_target="tpu_custom_call" | custom-call | flops 3758096384 | bytes 14680064 | tf_op jit(solution)/shard_map/down/pallas_call | solution.py:237
  88.9 3.0 %down.4 = (f32[40,2048]{1,0:T(8,128)S(1)}, bf16[40,2048]{1,0:T(8,128)(2,1)S(1)}) custom-call(s32[2]{0:T(128)S(1)} %pad_add_fusion.where, bf16[3,48,1792]{2,1,0:T(8,128)(2,1)S(1)} %activate.2.own, bf16[3,48,1792]{2,1,0:T(8,128)(2,1)S(1)} %collective-permute-done.7.other, bf16[1792,2048]{1,0:T(8,128)(2,1)S(1)} %fetch.8.down_w.rest_0_, ...), custom_call_target="tpu_custom_call" | custom-call | flops 1879048192 | bytes 7340032 | tf_op jit(solution)/shard_map/down/pallas_call | solution.py:237
  91.9 1.8 %collective-permute-start.10 = (bf16[40,2048]{1,0:T(8,128)(2,1)S(1)}, bf16[40,2048]{1,0:T(8,128)(2,1)S(1)}, u32[]{:S(2)}, u32[]{:S(2)}) collective-permute-start(bf16[40,2048]{1,0:T(8,128)(2,1)S(1)} %get-tuple-element.34), channel_id=1, source_target_pairs={{0,16},{16,0},{1,17},{17,1},{2,18},{18,2},{3,19},{19,3},{4,20},{20... | collective-permute-start | bytes 491528 | tf_op jit(solution)/shard_map/ppermute | solution.py:21
  93.7 1.8 %collective-permute-done.13.got = bf16[40,2048]{1,0:T(8,128)(2,1)S(1)} collective-permute-done((bf16[40,2048]{1,0:T(8,128)(2,1)S(1)}, bf16[40,2048]{1,0:T(8,128)(2,1)S(1)}, u32[]{:S(2)}, u32[]{:S(2)}) %collective-permute-start.13) | collective-permute-done | bytes 163872 | tf_op jit(solution)/shard_map/ppermute | solution.py:21
  96.0 2.7 %collective-permute-done.10.got = bf16[40,2048]{1,0:T(8,128)(2,1)S(1)} collective-permute-done((bf16[40,2048]{1,0:T(8,128)(2,1)S(1)}, bf16[40,2048]{1,0:T(8,128)(2,1)S(1)}, u32[]{:S(2)}, u32[]{:S(2)}) %collective-permute-start.10) | collective-permute-done | bytes 163872 | tf_op jit(solution)/shard_map/ppermute | solution.py:21
  100.2 2.6 %collective-permute-start.15 = (bf16[10,2048]{1,0:T(8,128)(2,1)S(1)}, bf16[10,2048]{1,0:T(8,128)(2,1)S(1)}, u32[]{:S(2)}, u32[]{:S(2)}) collective-permute-start(bf16[10,2048]{1,0:T(8,128)(2,1)S(1)} %get-tuple-element.45), channel_id=1, source_target_pairs={{0,8},{4,12},{8,0},{12,4},{1,9},{5,13},{9,1},{13,5},{2,10},{6,14},... | collective-permute-start | bytes 122888 | tf_op jit(solution)/shard_map/ppermute | solution.py:21
  104.1 1.9 %collective-permute-start.12 = (bf16[10,2048]{1,0:T(8,128)(2,1)S(1)}, bf16[10,2048]{1,0:T(8,128)(2,1)S(1)}, u32[]{:S(2)}, u32[]{:S(2)}) collective-permute-start(bf16[10,2048]{1,0:T(8,128)(2,1)S(1)} %get-tuple-element.38), channel_id=1, source_target_pairs={{0,8},{4,12},{8,0},{12,4},{1,9},{5,13},{9,1},{13,5},{2,10},{6,14},... | collective-permute-start | bytes 122888 | tf_op jit(solution)/shard_map/ppermute | solution.py:21
  107.5 2.5 %collective-permute-done.12.got = bf16[10,2048]{1,0:T(8,128)(2,1)S(1)} collective-permute-done((bf16[10,2048]{1,0:T(8,128)(2,1)S(1)}, bf16[10,2048]{1,0:T(8,128)(2,1)S(1)}, u32[]{:S(2)}, u32[]{:S(2)}) %collective-permute-start.12) | collective-permute-done | bytes 40992 | tf_op jit(solution)/shard_map/ppermute | solution.py:21
  (36 shorter events, 13.7 us)
Async XLA Ops:
  0.6 8.0 %collective-permute-start = (bf16[10,2048]{1,0:T(8,128)(2,1)}, bf16[10,2048]{1,0:T(8,128)(2,1)S(1)}, u32[]{:S(2)}, u32[]{:S(2)}) collective-permute-start(bf16[10,2048]{1,0:T(8,128)(2,1)} %ta.1), channel_id=1, source_target_pairs={{0,8},{4,12},{8,0},{12,4},{1,9},{5,13},{9,1},{13,5},{2,10},{6,14},... | collective-permute-start | bytes 122888 | tf_op jit(solution)/shard_map/ppermute | solution.py:21
  4.7 6.7 %collective-permute-start.1 = (bf16[10,2048]{1,0:T(8,128)(2,1)}, bf16[10,2048]{1,0:T(8,128)(2,1)S(1)}, u32[]{:S(2)}, u32[]{:S(2)}) collective-permute-start(bf16[10,2048]{1,0:T(8,128)(2,1)} %ca.1), channel_id=1, source_target_pairs={{0,8},{4,12},{8,0},{12,4},{1,9},{5,13},{9,1},{13,5},{2,10},{6,14},... | collective-permute-start | bytes 122888 | tf_op jit(solution)/shard_map/ppermute | solution.py:21
  11.4 0.8 copy-start
  12.2 0.8 copy-start.1
  13.1 5.8 %collective-permute-start.2 = (bf16[2,20,2048]{2,1,0:T(8,128)(2,1)S(1)}, bf16[2,20,2048]{2,1,0:T(8,128)(2,1)S(1)}, u32[]{:S(2)}, u32[]{:S(2)}) collective-permute-start(bf16[2,20,2048]{2,1,0:T(8,128)(2,1)S(1)} %pack.2.a), channel_id=1, source_target_pairs={{0,4},{4,0},{8,12},{12,8},{1,5},{5,1},{9,13},{13,9},{2,6},{6,2},{1... | collective-permute-start | bytes 491528 | tf_op jit(solution)/shard_map/ppermute | solution.py:21
  19.0 12.8 %collective-permute-start.3 = (bf16[2,40,2048]{2,1,0:T(8,128)(2,1)S(1)}, bf16[2,40,2048]{2,1,0:T(8,128)(2,1)S(1)}, u32[]{:S(2)}, u32[]{:S(2)}) collective-permute-start(bf16[2,40,2048]{2,1,0:T(8,128)(2,1)S(1)} %pack.3.near), channel_id=1, source_target_pairs={{0,16},{16,0},{1,17},{17,1},{2,18},{18,2},{3,19},{19,3},{4,20},{20... | collective-permute-start | bytes 983048 | tf_op jit(solution)/shard_map/ppermute | solution.py:21
  37.4 11.0 %collective-permute-start.4 = (f32[3,40,1536]{2,1,0:T(8,128)S(1)}, f32[3,40,1536]{2,1,0:T(8,128)S(1)}, u32[]{:S(2)}, u32[]{:S(2)}) collective-permute-start(f32[3,40,1536]{2,1,0:T(8,128)S(1)} %get-tuple-element.25), channel_id=1, source_target_pairs={{0,1},{1,0},{2,3},{3,2},{4,5},{5,4},{6,7},{7,6},{8,9},{9,8},{10,11... | collective-permute-start | bytes 2211848 | tf_op jit(solution)/shard_map/ppermute | solution.py:21
  55.0 2.6 %collective-permute-start.5 = (f32[3,40,1792]{2,1,0:T(8,128)S(1)}, f32[3,40,1792]{2,1,0:T(8,128)S(1)}, u32[]{:S(2)}, u32[]{:S(2)}) collective-permute-start(f32[3,40,1792]{2,1,0:T(8,128)S(1)} %get-tuple-element.28), channel_id=1, source_target_pairs={{0,1},{1,0},{2,3},{3,2},{4,5},{5,4},{6,7},{7,6},{8,9},{9,8},{10,11... | collective-permute-start | bytes 2580488 | tf_op jit(solution)/shard_map/ppermute | solution.py:21
  55.6 11.4 %collective-permute-start.8 = (bf16[3,40,1536]{2,1,0:T(8,128)(2,1)S(1)}, bf16[3,40,1536]{2,1,0:T(8,128)(2,1)S(1)}, u32[]{:S(2)}, u32[]{:S(2)}) collective-permute-start(bf16[3,40,1536]{2,1,0:T(8,128)(2,1)S(1)} %get-tuple-element.26.rest_0_), channel_id=1, source_target_pairs={{0,2},{1,3},{2,0},{3,1},{4,6},{5,7},{6,4},{7,5},{8,10},{9,11},{10,... | collective-permute-start | bytes 1105928 | tf_op jit(solution)/shard_map/ppermute | solution.py:21
  57.7 17.6 %collective-permute-start.6 = (bf16[3,40,1792]{2,1,0:T(8,128)(2,1)S(1)}, bf16[3,40,1792]{2,1,0:T(8,128)(2,1)S(1)}, u32[]{:S(2)}, u32[]{:S(2)}) collective-permute-start(bf16[3,40,1792]{2,1,0:T(8,128)(2,1)S(1)} %get-tuple-element.30), channel_id=1, source_target_pairs={{0,2},{1,3},{2,0},{3,1},{4,6},{5,7},{6,4},{7,5},{8,10},{9,11},{10,... | collective-permute-start | bytes 1290248 | tf_op jit(solution)/shard_map/ppermute | solution.py:21
  67.2 8.5 %collective-permute-start.9 = (bf16[3,48,1536]{2,1,0:T(8,128)(2,1)S(1)}, bf16[3,48,1536]{2,1,0:T(8,128)(2,1)S(1)}, u32[]{:S(2)}, u32[]{:S(2)}) collective-permute-start(bf16[3,48,1536]{2,1,0:T(8,128)(2,1)S(1)} %activate.3.own), channel_id=1, source_target_pairs={{0,1},{1,0},{2,3},{3,2},{4,5},{5,4},{6,7},{7,6},{8,9},{9,8},{10,11... | collective-permute-start | bytes 1327112 | tf_op jit(solution)/shard_map/ppermute | solution.py:21
  75.6 6.7 %collective-permute-start.7 = (bf16[3,48,1792]{2,1,0:T(8,128)(2,1)S(1)}, bf16[3,48,1792]{2,1,0:T(8,128)(2,1)S(1)}, u32[]{:S(2)}, u32[]{:S(2)}) collective-permute-start(bf16[3,48,1792]{2,1,0:T(8,128)(2,1)S(1)} %activate.2.own), channel_id=1, source_target_pairs={{0,1},{1,0},{2,3},{3,2},{4,5},{5,4},{6,7},{7,6},{8,9},{9,8},{10,11... | collective-permute-start | bytes 1548296 | tf_op jit(solution)/shard_map/ppermute | solution.py:21
  88.5 7.0 %collective-permute-start.13 = (bf16[40,2048]{1,0:T(8,128)(2,1)S(1)}, bf16[40,2048]{1,0:T(8,128)(2,1)S(1)}, u32[]{:S(2)}, u32[]{:S(2)}) collective-permute-start(bf16[40,2048]{1,0:T(8,128)(2,1)S(1)} %get-tuple-element.41), channel_id=1, source_target_pairs={{0,16},{16,0},{1,17},{17,1},{2,18},{18,2},{3,19},{19,3},{4,20},{20... | collective-permute-start | bytes 491528 | tf_op jit(solution)/shard_map/ppermute | solution.py:21
  91.9 6.8 %collective-permute-start.10 = (bf16[40,2048]{1,0:T(8,128)(2,1)S(1)}, bf16[40,2048]{1,0:T(8,128)(2,1)S(1)}, u32[]{:S(2)}, u32[]{:S(2)}) collective-permute-start(bf16[40,2048]{1,0:T(8,128)(2,1)S(1)} %get-tuple-element.34), channel_id=1, source_target_pairs={{0,16},{16,0},{1,17},{17,1},{2,18},{18,2},{3,19},{19,3},{4,20},{20... | collective-permute-start | bytes 491528 | tf_op jit(solution)/shard_map/ppermute | solution.py:21
  95.5 4.7 %collective-permute-start.14 = (bf16[20,2048]{1,0:T(8,128)(2,1)S(1)}, bf16[20,2048]{1,0:T(8,128)(2,1)S(1)}, u32[]{:S(2)}, u32[]{:S(2)}) collective-permute-start(bf16[20,2048]{1,0:T(8,128)(2,1)S(1)} %get-tuple-element.43), channel_id=1, source_target_pairs={{0,4},{4,0},{8,12},{12,8},{1,5},{5,1},{9,13},{13,9},{2,6},{6,2},{1... | collective-permute-start | bytes 245768 | tf_op jit(solution)/shard_map/ppermute | solution.py:21
  98.7 5.4 %collective-permute-start.11 = (bf16[20,2048]{1,0:T(8,128)(2,1)S(1)}, bf16[20,2048]{1,0:T(8,128)(2,1)S(1)}, u32[]{:S(2)}, u32[]{:S(2)}) collective-permute-start(bf16[20,2048]{1,0:T(8,128)(2,1)S(1)} %get-tuple-element.36), channel_id=1, source_target_pairs={{0,4},{4,0},{8,12},{12,8},{1,5},{5,1},{9,13},{13,9},{2,6},{6,2},{1... | collective-permute-start | bytes 245768 | tf_op jit(solution)/shard_map/ppermute | solution.py:21
  100.2 6.7 %collective-permute-start.15 = (bf16[10,2048]{1,0:T(8,128)(2,1)S(1)}, bf16[10,2048]{1,0:T(8,128)(2,1)S(1)}, u32[]{:S(2)}, u32[]{:S(2)}) collective-permute-start(bf16[10,2048]{1,0:T(8,128)(2,1)S(1)} %get-tuple-element.45), channel_id=1, source_target_pairs={{0,8},{4,12},{8,0},{12,4},{1,9},{5,13},{9,1},{13,5},{2,10},{6,14},... | collective-permute-start | bytes 122888 | tf_op jit(solution)/shard_map/ppermute | solution.py:21
  104.1 5.9 %collective-permute-start.12 = (bf16[10,2048]{1,0:T(8,128)(2,1)S(1)}, bf16[10,2048]{1,0:T(8,128)(2,1)S(1)}, u32[]{:S(2)}, u32[]{:S(2)}) collective-permute-start(bf16[10,2048]{1,0:T(8,128)(2,1)S(1)} %get-tuple-element.38), channel_id=1, source_target_pairs={{0,8},{4,12},{8,0},{12,4},{1,9},{5,13},{9,1},{13,5},{2,10},{6,14},... | collective-permute-start | bytes 122888 | tf_op jit(solution)/shard_map/ppermute | solution.py:21

commit v3 on v2

v3 whole, which is shorter than its diff:
```python
import functools

import jax
import jax.numpy as jnp
from jax import lax
from jax.experimental import pallas as pl
from jax.experimental.pallas import tpu as pltpu
from jax.sharding import PartitionSpec as P

F32 = jnp.float32
BF16 = jnp.bfloat16
NT = (((1,), (1,)), ((), ()))
MIB = 2**20
VMEM = pl.BlockSpec(memory_space=pltpu.VMEM)
SMEM = pl.BlockSpec(memory_space=pltpu.SMEM)
HBM = pl.BlockSpec(memory_space=pltpu.HBM)
ANY = pl.BlockSpec(memory_space=pl.ANY)


def swap(value, axis, size, bit):
    return lax.ppermute(value, axis, [(i, i ^ bit) for i in range(size)])


def bits(size, first=1):
    out = []
    while first < size:
        out.append(first)
        first *= 2
    return out


def resident(x):
    return pltpu.with_memory_space_constraint(x, pltpu.VMEM)


def in_hbm(x):
    return pltpu.with_memory_space_constraint(x, pltpu.HBM)


def cost(flops, nbytes):
    return pl.CostEstimate(flops=flops, bytes_accessed=nbytes, transcendentals=0)


def call(kernel, name, in_specs, out_shape, scratch=(), limit=2, estimate=None):
    many = isinstance(out_shape, (list, tuple))
    return pl.pallas_call(
        kernel,
        in_specs=in_specs,
        out_specs=[VMEM] * len(out_shape) if many else VMEM,
        out_shape=out_shape,
        scratch_shapes=list(scratch),
        compiler_params=pltpu.CompilerParams(vmem_limit_bytes=limit * MIB),
        cost_estimate=estimate,
        name=name,
    )


def copies(where, specs, srcs, outs, sems):
    made = []
    for i, ((dim, whole, start, size), src, out) in enumerate(zip(specs, srcs, outs)):
        first = pl.multiple_of(where[0] * whole + start, 128)
        part = src.at[pl.ds(first, size), :] if dim == 0 else src.at[:, pl.ds(first, size)]
        made.append(pltpu.make_async_copy(part, out, sems.at[i]))
    return made


def fetched(weight, spec):
    shape = list(weight.shape)
    shape[spec[0]] = spec[3]
    return pltpu.VMEM(tuple(shape), BF16)


def fetch(where, wanted, after=()):
    weights, specs = zip(*wanted)
    n = len(wanted)

    def kernel(where, *refs):
        made = copies(where, specs, refs[:n], refs[n + len(after) : -1], refs[-1])
        for copy in made:
            copy.start()
        for copy in made:
            copy.wait()

    outs = [fetched(w, s) for w, s in wanted]
    return call(
        kernel,
        "fetch",
        [SMEM] + [HBM] * n + [ANY] * len(after),
        outs,
        [pltpu.SemaphoreType.DMA((n,))],
        estimate=cost(0, sum(2 * o.shape[0] * o.shape[1] for o in outs)),
    )(where, *[in_hbm(w) for w in weights], *after)


def pack(near, far, after):
    n, feats = near[0].shape[-2:]

    def kernel(*refs):
        out, wide = refs[-2:]
        for i in range(2):
            a, b = (refs[i], refs[2 + i]) if len(near) == 2 else (refs[0].at[i], refs[1].at[i])
            wide[i, :n, :] = a[...].astype(F32)
            wide[i, n : 2 * n, :] = b[...].astype(F32)
            out[i] = wide[i].astype(BF16)

    return call(
        kernel,
        "pack",
        [VMEM] * (len(near) + len(far)) + [ANY] * len(after),
        jax.ShapeDtypeStruct((2, 2 * n, feats), BF16),
        [pltpu.VMEM((2, 2 * n, feats), F32)],
        limit=4,
    )(*near, *far, *after)


def up(where, near, far, which, weights, transposed, block, wanted=(), after=()):
    _, half, feats = near.shape
    width = weights[0].shape[0 if transposed else 1]
    n, m = len(weights), len(wanted)
    specs = [s for _, s in wanted]

    def kernel(where, near, far, *refs):
        refs = list(refs)
        ws = [refs.pop(0) for _ in range(n)]
        srcs = [refs.pop(0) for _ in range(m)]
        del refs[: len(after)]
        outs = [refs.pop(0) for _ in range(2 * n)]
        dsts = [refs.pop(0) for _ in range(m)]
        wide, lhs = refs[:2]
        made = copies(where, specs, srcs, dsts, refs[2]) if m else []
        for copy in made:
            copy.start()
        first = where[1] == 0
        a, b = near[which].astype(F32), far[which].astype(F32)
        wide[:half, :] = jnp.where(first, a, b)
        wide[half:, :] = jnp.where(first, b, a)
        lhs[...] = wide[...].astype(BF16)

        @pl.loop(0, width // block)
        def _(step):
            cut = pl.ds(pl.multiple_of(step * block, block), block)
            for i, w in enumerate(ws):
                if transposed:
                    value = lax.dot_general(lhs[...], w[cut, :], NT, preferred_element_type=F32)
                else:
                    value = jnp.dot(lhs[...], w[:, cut], preferred_element_type=F32)
                outs[2 * i][:, cut] = value[:half]
                outs[2 * i + 1][:, cut] = value[half:]

        for copy in made:
            copy.wait()

    out = jax.ShapeDtypeStruct((half, width), F32)
    got = call(
        kernel,
        "up",
        [SMEM] + [VMEM] * (2 + n) + [HBM] * m + [ANY] * len(after),
        [out] * (2 * n) + [fetched(w, s) for w, s in wanted],
        [pltpu.VMEM((2 * half, feats), F32), pltpu.VMEM((2 * half, feats), BF16)]
        + ([pltpu.SemaphoreType.DMA((m,))] if m else []),
        limit=6,
        estimate=cost(2 * n * 256 * feats * width, 2 * n * feats * width),
    )(where, near, far, *[resident(w) for w in weights], *[in_hbm(w) for w, _ in wanted], *after)
    return got[: 2 * n : 2], got[1 : 2 * n : 2], got[2 * n :]


def gather(keeps, gots):
    n = len(keeps)
    shape = (n,) + keeps[0].shape

    def kernel(*refs):
        total, rounded = refs[-2:]
        for i in range(n):
            value = refs[i][...] + refs[n + i][...]
            total[i] = value
            rounded[i] = value.astype(BF16)

    return call(
        kernel,
        "gather",
        [VMEM] * (2 * n),
        [jax.ShapeDtypeStruct(shape, F32), jax.ShapeDtypeStruct(shape, BF16)],
    )(*keeps, *gots)


def add(a, b):
    def kernel(a, b, total, rounded):
        value = a[...] + b[...].astype(F32)
        total[...] = value
        rounded[...] = value.astype(BF16)

    return call(
        kernel,
        "add",
        [VMEM] * 2,
        [jax.ShapeDtypeStruct(a.shape, F32), jax.ShapeDtypeStruct(a.shape, BF16)],
    )(a, b)


def activate(sums, got, padded, after):
    _, half, width = sums.shape

    def kernel(sums, got, *rest):
        out = rest[-1]
        gate = sums[0] + got[0].astype(F32)
        upward = sums[1] + got[1].astype(F32)
        back = sums[2] + got[2].astype(F32)
        sigma = jax.nn.sigmoid(gate)
        hidden = gate * sigma * upward
        d_up = back * gate * sigma
        d_gate = back * upward * sigma * (1.0 + gate * (1.0 - sigma))
        for i, value in enumerate((hidden, d_gate, d_up)):
            if padded > half:
                empty = jnp.zeros((padded - half, width), F32)
                value = jnp.concatenate([value, empty], axis=0)
            out[i] = value.astype(BF16)

    return call(
        kernel,
        "activate",
        [VMEM] * 2 + [ANY] * len(after),
        jax.ShapeDtypeStruct((3, padded, width), BF16),
        limit=4,
    )(sums, got, *after)


def down(where, own, other, weights, prev, half, part, last, block):
    _, padded, width = own.shape
    start, feats = part

    def kernel(where, own, other, gate_w, up_w, down_w, *rest):
        lhs = rest[-1]
        outs = rest[len(prev) : -1]
        first = where[1] == 0
        lhs[:, :padded, :] = own[...]
        lhs[:, padded:, :] = other[...]

        @pl.loop(0, feats // block)
        def _(step):
            cut = pl.ds(pl.multiple_of(step * block, block), block)
            full = pl.ds(pl.multiple_of(start + step * block, block), block)
            mixed = jnp.dot(lhs[0], down_w[:, full], preferred_element_type=F32)
            grad = lax.dot_general(lhs[1], gate_w[full, :], NT, preferred_element_type=F32)
            grad += lax.dot_general(lhs[2], up_w[full, :], NT, preferred_element_type=F32)
            for i, value in enumerate((mixed, grad)):
                if prev:
                    value += prev_ref(rest)[i, :, full]
                if last:
                    a, b = value[:half], value[padded : padded + half]
                    outs[0][i, :, cut] = jnp.where(first, a, b)
                    outs[1][i, :, cut] = jnp.where(first, b, a).astype(BF16)
                else:
                    outs[0][i, :, cut] = value

    def prev_ref(rest):
        return rest[0]

    if last:
        shapes = [
            jax.ShapeDtypeStruct((2, half, feats), F32),
            jax.ShapeDtypeStruct((2, half, feats), BF16),
        ]
    else:
        shapes = [jax.ShapeDtypeStruct((2, 2 * padded, feats), F32)]
    return call(
        kernel,
        "down",
        [SMEM] + [VMEM] * (5 + len(prev)),
        shapes,
        [pltpu.VMEM((3, 2 * padded, width), BF16)],
        limit=6,
        estimate=cost(6 * 256 * feats * width, 6 * feats * width),
    )(where, own, other, *[resident(w) for w in weights], *prev)


def fold(keep, got):
    _, n, feats = keep.shape
    half = n // 2

    def kernel(keep, got, stay, send):
        for i in range(2):
            value = keep[i] + got[i].astype(F32)
            stay[i] = value[:half]
            send[i] = value[half:].astype(BF16)

    return call(
        kernel,
        "fold",
        [VMEM] * 2,
        [jax.ShapeDtypeStruct((2, half, feats), F32), jax.ShapeDtypeStruct((2, half, feats), BF16)],
    )(keep, got)


def finish(keeps, gots):
    n = len(keeps)
    _, rows, feats = keeps[0].shape

    def kernel(*refs):
        outs = refs[2 * n :]
        for j in range(n):
            for i in range(2):
                value = refs[j][i] + refs[n + j][i].astype(F32)
                outs[i][:, j * feats : (j + 1) * feats] = value.astype(BF16)

    return call(
        kernel,
        "finish",
        [VMEM] * (2 * n),
        [jax.ShapeDtypeStruct((rows, n * feats), BF16)] * 2,
    )(*keeps, *gots)


def per_device(sizes, tokens, cotangent, gate_weight, up_weight, down_weight):
    grp, blk, bulk = sizes["grp"], sizes["blk"], sizes["bulk"]
    units, feats = gate_weight.shape[1], gate_weight.shape[0]
    split = units % (grp * 128) == 0
    whole = units // grp if split else units
    block = 256 if whole % 256 == 0 else 128
    blocks = whole // block
    cuts = [0, blocks - blocks // 2, blocks] if blocks > 1 else [0, blocks]
    chunks = [(a * block, (b - a) * block) for a, b in zip(cuts, cuts[1:])]
    down_block = 256 if feats % 256 == 0 else 128

    core = lax.axis_index("bulk") % 2
    group = lax.axis_index("grp") if split else jnp.int32(0)
    where = jnp.stack([group, core]).astype(jnp.int32)

    hops = [("blk", blk, b) for b in reversed(bits(blk))]
    if split:
        hops += [("grp", grp, b) for b in bits(grp)]

    gates, ups, downs = (
        [(w, (dim, whole, start, size)) for start, size in chunks]
        for w, dim in ((gate_weight, 1), (up_weight, 1), (down_weight, 0))
    )
    (gate0,) = fetch(where, [gates[0]])
    near = (tokens, cotangent)
    far = tuple(swap(v, *hops[0]) for v in near)
    near = pack(near, far, (gate0,))
    (up0,) = fetch(where, [ups[0]], (near,))
    for hop in hops[1:-1]:
        near = pack((near,), (swap(near, *hop),), (up0,))
    far = swap(near, *hops[-1])
    down0, *more = fetch(where, [downs[0]] + gates[1:], (near,))
    half = near.shape[1]
    padded = -(-half // 16) * 16

    weights = [[gate0, up0, down0]] + [[g, None, None] for g in more]
    summed = []
    after = ()
    for c, w in enumerate(weights):
        later = ups[1:] if c == 0 else downs[c : c + 1]
        keep, send, got = up(where, near, far, 0, w[:2], False, block, later, after)
        if c == 0:
            for v, value in zip(weights[1:], got):
                v[1] = value
        else:
            w[2] = got[0]
        keep_b, send_b, _ = up(where, near, far, 1, w[2:], True, block, (), after)
        keep, send = [*keep, *keep_b], [*send, *send_b]
        sums, rounded = gather(keep, [swap(v, "bulk", bulk, 1) for v in send])
        after = (rounded,)
        summed.append((sums, rounded))

    prev = ()
    for c, (w, (sums, rounded)) in enumerate(zip(weights, summed)):
        for b in bits(bulk, 2)[:-1]:
            sums, rounded = add(sums, swap(rounded, "bulk", bulk, b))
        got = swap(rounded, "bulk", bulk, bits(bulk, 2)[-1])
        own = activate(sums, got, padded, (*prev, *[r for _, r in summed[c + 1 :]]))
        other = swap(own, "bulk", bulk, 1)
        if c < len(chunks) - 1:
            prev = down(where, own, other, w, prev, half, (0, feats), False, down_block)
    pieces = 2 if feats % (2 * down_block) == 0 else 1
    stays, gots = [], []
    for p in range(pieces):
        part = (p * feats // pieces, feats // pieces)
        stay, send = down(where, own, other, w, prev, half, part, True, down_block)
        for hop in reversed(hops[1:]):
            stay, send = fold(stay, swap(send, *hop))
        stays.append(stay)
        gots.append(swap(send, *hops[0]))
    return tuple(finish(stays, gots))


def solution(mesh):
    return jax.shard_map(
        functools.partial(per_device, dict(mesh.shape)),
        mesh=mesh,
        in_specs=(
            P(("grp", "blk"), "bulk"),
            P(("grp", "blk"), "bulk"),
            P("bulk", "blk"),
            P("bulk", "blk"),
            P("blk", "bulk"),
        ),
        out_specs=(P(("grp", "blk"), "bulk"), P(("grp", "blk"), "bulk")),
        check_vma=False,
    )
```

time: 111 us -> 89.9 us (0.81)
  waiting for transfers between devices: 37.9 us -> 23 us
  Pallas kernels: 51 us -> 43.4 us
  starting transfers between devices: 19.2 us -> 22.5 us
  local copies, waits for them, and re-layouts: 1.68 us -> 0.02 us
    ppermute x16 -> x20, waiting for transfers between devices: 37.9 us -> 23 us  [swap(): return lax.ppermute(value, axis, [(i, i ^ bit) for i in range(size)])]
    pallas_call x23 -> x21, Pallas kernels: 51 us -> 43.4 us  [the longest x4 14.9 us: up(): call(kernel, 'up', [SMEM] + [VMEM] * (2 + n) + [HBM] * m + [ANY] * len(af...]
    ppermute x16 -> x20, starting transfers between devices: 19.2 us -> 22.5 us  [swap(): return lax.ppermute(value, axis, [(i, i ^ bit) for i in range(size)])]
    unnamed x4 -> x10, local copies, waits for them, and re-layouts: 1.68 us -> 0.02 us
  transfers between devices with their start and end apart: 16 -> 20, of which waited for: 12 -> 14; matrix products, arithmetic and copies ran while one was open for 0% -> 0% of each run, Pallas kernels for 29% -> 38%
where the time goes in v3:
time: 89.9 us; the launch traced here: 89.8 us
  Pallas kernels  43.4 us (48%)
  waiting for transfers between devices  23 us (26%)
  starting transfers between devices  22.5 us (25%)
    ppermute x20, waiting for transfers between devices, swap(): return lax.ppermute(value, axis, [(i, i ^ bit) for i in range(size)])  23 us
    ppermute x20, starting transfers between devices, swap(): return lax.ppermute(value, axis, [(i, i ^ bit) for i in range(size)])  22.5 us
    pallas_call x4, Pallas kernels, up(): call(kernel, 'up', [SMEM] + [VMEM] * (2 + n) + [HBM] * m + [ANY] * len(af...  14.9 us
    pallas_call x3, Pallas kernels, down(): call(kernel, 'down', [SMEM] + [VMEM] * (5 + len(prev)), shapes, [pltpu.VM...  14.3 us
    pallas_call x3, Pallas kernels, fetch(): call(kernel, 'fetch', [SMEM] + [HBM] * n + [ANY] * len(after), outs, [plt...  12.7 us
  transfers between devices with their start and end apart: 20, of which 14 were waited for; matrix products, arithmetic and copies ran while one was open for 0% of the time, Pallas kernels for 38%

profile of v3, /device:TPU:0, one launch (start us, length us, event | category | flops | bytes accessed | tf_op | source)
XLA Modules:
  0.0 89.8 jit_solution(11695531275642058247)
XLA Ops:
  0.6 4.1 %collective-permute-start = (bf16[10,2048]{1,0:T(8,128)(2,1)}, bf16[10,2048]{1,0:T(8,128)(2,1)S(1)}, u32[]{:S(2)}, u32[]{:S(2)}) collective-permute-start(bf16[10,2048]{1,0:T(8,128)(2,1)} %refs_0_.5), channel_id=1, source_target_pairs={{0,8},{4,12},{8,0},{12,4},{1,9},{5,13},{9,1},{13,5},{2,10},{6,14},... | collective-permute-start | bytes 122888 | tf_op jit(solution)/shard_map/ppermute | solution.py:21
  4.9 3.6 %fetch.3.refs_4_.refs_0_.gate_w = bf16[2048,1792]{1,0:T(8,128)(2,1)S(1)} custom-call(s32[2]{0:T(128)S(1)} %pad_add_fusion.where, bf16[2048,6656]{1,0:T(8,128)(2,1)} %refs_1_.3), custom_call_target="tpu_custom_call" | custom-call | bytes 7340032 | tf_op jit(solution)/shard_map/fetch/pallas_call | solution.py:85
  8.6 2.8 %collective-permute-done.1.refs_3_ = bf16[10,2048]{1,0:T(8,128)(2,1)S(1)} collective-permute-done((bf16[10,2048]{1,0:T(8,128)(2,1)}, bf16[10,2048]{1,0:T(8,128)(2,1)S(1)}, u32[]{:S(2)}, u32[]{:S(2)}) %collective-permute-start.1) | collective-permute-done | bytes 40992 | tf_op jit(solution)/shard_map/ppermute | solution.py:21
  12.2 3.6 %fetch.4.refs_2_.refs_1_.up_w = bf16[2048,1792]{1,0:T(8,128)(2,1)S(1)} custom-call(s32[2]{0:T(128)S(1)} %pad_add_fusion.where, bf16[2048,6656]{1,0:T(8,128)(2,1)} %refs_2_.2, bf16[2,20,2048]{2,1,0:T(8,128)(2,1)S(1)} %pack.2.refs_1_.refs_0_), custom_call_target="tpu_custom_call" | custom-call | bytes 7340032 | tf_op jit(solution)/shard_map/fetch/pallas_call | solution.py:85
  15.8 1.4 %collective-permute-done.2.refs_1_ = bf16[2,20,2048]{2,1,0:T(8,128)(2,1)S(1)} collective-permute-done((bf16[2,20,2048]{2,1,0:T(8,128)(2,1)S(1)}, bf16[2,20,2048]{2,1,0:T(8,128)(2,1)S(1)}, u32[]{:S(2)}, u32[]{:S(2)}) %collective-permute-start.2) | collective-permute-done | bytes 163872 | tf_op jit(solution)/shard_map/ppermute | solution.py:21
  17.3 2.7 %collective-permute-start.3 = (bf16[2,40,2048]{2,1,0:T(8,128)(2,1)S(1)}, bf16[2,40,2048]{2,1,0:T(8,128)(2,1)S(1)}, u32[]{:S(2)}, u32[]{:S(2)}) collective-permute-start(bf16[2,40,2048]{2,1,0:T(8,128)(2,1)S(1)} %pack.3.refs_2_.near), channel_id=1, source_target_pairs={{0,16},{16,0},{1,17},{17,1},{2,18},{18,2},{3,19},{19,3},{4,20},{20... | collective-permute-start | bytes 983048 | tf_op jit(solution)/shard_map/ppermute | solution.py:21
  20.0 5.4 %fetch.5 = (bf16[1792,2048]{1,0:T(8,128)(2,1)S(1)}, bf16[2048,1536]{1,0:T(8,128)(2,1)S(1)}) custom-call(s32[2]{0:T(128)S(1)} %pad_add_fusion.where, bf16[6656,2048]{1,0:T(8,128)(2,1)} %refs_2_.3, bf16[2048,6656]{1,0:T(8,128)(2,1)} %refs_1_.3, bf16[2,40,2048]{2,1,0:T(8,128)(2,1)S(1)} %pack.3.refs_2_.near), custom_call_target="tpu_custom_call" | custom-call | bytes 13631488 | tf_op jit(solution)/shard_map/fetch/pallas_call | solution.py:85
  26.8 4.1 %up.4 = (f32[40,1792]{1,0:T(8,128)S(1)}, f32[40,1792]{1,0:T(8,128)S(1)}, f32[40,1792]{1,0:T(8,128)S(1)}, f32[40,1792]{1,0:T(8,128)S(1)}, bf16[2048,1536]{1,0:T(8,128)(2,1)S(1)}) custom-call(s32[2]{0:T(128)S(1)} %pad_add_fusion.where, bf16[2,40,2048]{2,1,0:T(8,128)(2,1)S(1)} %pack.3.refs_2_.near, bf16[2,40,2048]{2,1,0:T(8,128)(2,1)S(1)} %collective-permute-done.3.far, ...), custom_call_target="tpu_custom_call" | custom-call | flops 3758096384 | bytes 14680064 | tf_op jit(solution)/shard_map/up/pallas_call | solution.py:154
  31.5 3.8 %up.5 = (f32[40,1792]{1,0:T(8,128)S(1)}, f32[40,1792]{1,0:T(8,128)S(1)}) custom-call(s32[2]{0:T(128)S(1)} %pad_add_fusion.where, bf16[2,40,2048]{2,1,0:T(8,128)(2,1)S(1)} %pack.3.refs_2_.near, bf16[2,40,2048]{2,1,0:T(8,128)(2,1)S(1)} %collective-permute-done.3.far, bf16[1792,2048]{1,0:T(8,128)(2,1)S(1)} %get-tuple-element.38.refs_0_.down_w), custom_call_target="tpu_custom_call" | custom-call | flops 1879048192 | bytes 7340032 | tf_op jit(solution)/shard_map/up/pallas_call | solution.py:154
  35.5 1.5 %collective-permute-done.6.refs_5_ = f32[40,1792]{1,0:T(8,128)S(1)} collective-permute-done((f32[40,1792]{1,0:T(8,128)S(1)}, f32[40,1792]{1,0:T(8,128)S(1)}, u32[]{:S(2)}, u32[]{:S(2)}) %collective-permute-start.6) | collective-permute-done | bytes 286752 | tf_op jit(solution)/shard_map/ppermute | solution.py:21
  37.1 1.8 %collective-permute-start.11 = (bf16[3,40,1792]{2,1,0:T(8,128)(2,1)S(1)}, bf16[3,40,1792]{2,1,0:T(8,128)(2,1)S(1)}, u32[]{:S(2)}, u32[]{:S(2)}) collective-permute-start(bf16[3,40,1792]{2,1,0:T(8,128)(2,1)S(1)} %get-tuple-element.43.refs_3_.refs_1_), channel_id=1, source_target_pairs={{0,2},{1,3},{2,0},{3,1},{4,6},{5,7},{6,4},{7,5},{8,10},{9,11},{10,... | collective-permute-start | bytes 1290248 | tf_op jit(solution)/shard_map/ppermute | solution.py:21
  38.9 3.6 %up.6 = (f32[40,1536]{1,0:T(8,128)S(1)}, f32[40,1536]{1,0:T(8,128)S(1)}, f32[40,1536]{1,0:T(8,128)S(1)}, f32[40,1536]{1,0:T(8,128)S(1)}, bf16[1536,2048]{1,0:T(8,128)(2,1)S(1)}) custom-call(s32[2]{0:T(128)S(1)} %pad_add_fusion.where, bf16[2,40,2048]{2,1,0:T(8,128)(2,1)S(1)} %pack.3.refs_2_.near, bf16[2,40,2048]{2,1,0:T(8,128)(2,1)S(1)} %collective-permute-done.3.far, ...), custom_call_target="tpu_custom_call" | custom-call | flops 3221225472 | bytes 12582912 | tf_op jit(solution)/shard_map/up/pallas_call | solution.py:154
  43.1 3.3 %up.7 = (f32[40,1536]{1,0:T(8,128)S(1)}, f32[40,1536]{1,0:T(8,128)S(1)}) custom-call(s32[2]{0:T(128)S(1)} %pad_add_fusion.where, bf16[2,40,2048]{2,1,0:T(8,128)(2,1)S(1)} %pack.3.refs_2_.near, bf16[2,40,2048]{2,1,0:T(8,128)(2,1)S(1)} %collective-permute-done.3.far, bf16[1536,2048]{1,0:T(8,128)(2,1)S(1)} %get-tuple-element.46.refs_0_.down_w, ...), custom_call_target="tpu_custom_call" | custom-call | flops 1610612736 | bytes 6291456 | tf_op jit(solution)/shard_map/up/pallas_call | solution.py:154
  49.4 1.8 %collective-permute-start.10 = (bf16[3,40,1536]{2,1,0:T(8,128)(2,1)S(1)}, bf16[3,40,1536]{2,1,0:T(8,128)(2,1)S(1)}, u32[]{:S(2)}, u32[]{:S(2)}) collective-permute-start(bf16[3,40,1536]{2,1,0:T(8,128)(2,1)S(1)} %get-tuple-element.52.rest_0_), channel_id=1, source_target_pairs={{0,2},{1,3},{2,0},{3,1},{4,6},{5,7},{6,4},{7,5},{8,10},{9,11},{10,... | collective-permute-start | bytes 1105928 | tf_op jit(solution)/shard_map/ppermute | solution.py:21
  51.3 6.9 %down.3.rest_0_ = f32[2,96,2048]{2,1,0:T(8,128)S(1)} custom-call(s32[2]{0:T(128)S(1)} %pad_add_fusion.where, bf16[3,48,1792]{2,1,0:T(8,128)(2,1)S(1)} %activate.2.own, bf16[3,48,1792]{2,1,0:T(8,128)(2,1)S(1)} %collective-permute-done.12.other, bf16[2048,1792]{1,0:T(8,128)(2,1)S(1)} %fetch.3.refs_4_.refs_0_.gate_w, ...), custom_call_target="tpu_custom_call" | custom-call | flops 5637144576 | bytes 22020096 | tf_op jit(solution)/shard_map/down/pallas_call | solution.py:265
  58.2 2.2 %collective-permute-done.10.got = bf16[3,40,1536]{2,1,0:T(8,128)(2,1)S(1)} collective-permute-done((bf16[3,40,1536]{2,1,0:T(8,128)(2,1)S(1)}, bf16[3,40,1536]{2,1,0:T(8,128)(2,1)S(1)}, u32[]{:S(2)}, u32[]{:S(2)}) %collective-permute-start.10) | collective-permute-done | bytes 368672 | tf_op jit(solution)/shard_map/ppermute | solution.py:21
  60.7 1.8 %collective-permute-done.13.other = bf16[3,48,1536]{2,1,0:T(8,128)(2,1)S(1)} collective-permute-done((bf16[3,48,1536]{2,1,0:T(8,128)(2,1)S(1)}, bf16[3,48,1536]{2,1,0:T(8,128)(2,1)S(1)}, u32[]{:S(2)}, u32[]{:S(2)}) %collective-permute-start.13) | collective-permute-done | bytes 442400 | tf_op jit(solution)/shard_map/ppermute | solution.py:21
  62.5 3.7 %down.5 = (f32[2,40,1024]{2,1,0:T(8,128)S(1)}, bf16[2,40,1024]{2,1,0:T(8,128)(2,1)S(1)}) custom-call(s32[2]{0:T(128)S(1)} %pad_add_fusion.where, bf16[3,48,1536]{2,1,0:T(8,128)(2,1)S(1)} %activate.3.own, bf16[3,48,1536]{2,1,0:T(8,128)(2,1)S(1)} %collective-permute-done.13.other, bf16[2048,1536]{1,0:T(8,128)(2,1)S(1)} %get-tuple-element.34.refs_0_.gate_w, ...), custom_call_target="tpu_custom_call" | custom-call | flops 2415919104 | bytes 9437184 | tf_op jit(solution)/shard_map/down/pallas_call | solution.py:265
  66.2 1.8 %collective-permute-start.16 = (bf16[2,40,1024]{2,1,0:T(8,128)(2,1)S(1)}, bf16[2,40,1024]{2,1,0:T(8,128)(2,1)S(1)}, u32[]{:S(2)}, u32[]{:S(2)}) collective-permute-start(bf16[2,40,1024]{2,1,0:T(8,128)(2,1)S(1)} %get-tuple-element.60), channel_id=1, source_target_pairs={{0,16},{16,0},{1,17},{17,1},{2,18},{18,2},{3,19},{19,3},{4,20},{20... | collective-permute-start | bytes 491528 | tf_op jit(solution)/shard_map/ppermute | solution.py:21
  68.0 3.7 %down.4 = (f32[2,40,1024]{2,1,0:T(8,128)S(1)}, bf16[2,40,1024]{2,1,0:T(8,128)(2,1)S(1)}) custom-call(s32[2]{0:T(128)S(1)} %pad_add_fusion.where, bf16[3,48,1536]{2,1,0:T(8,128)(2,1)S(1)} %activate.3.own, bf16[3,48,1536]{2,1,0:T(8,128)(2,1)S(1)} %collective-permute-done.13.other, bf16[2048,1536]{1,0:T(8,128)(2,1)S(1)} %get-tuple-element.34.refs_0_.gate_w, ...), custom_call_target="tpu_custom_call" | custom-call | flops 2415919104 | bytes 9437184 | tf_op jit(solution)/shard_map/down/pallas_call | solution.py:265
  73.7 4.0 %collective-permute-done.14.got = bf16[2,40,1024]{2,1,0:T(8,128)(2,1)S(1)} collective-permute-done((bf16[2,40,1024]{2,1,0:T(8,128)(2,1)S(1)}, bf16[2,40,1024]{2,1,0:T(8,128)(2,1)S(1)}, u32[]{:S(2)}, u32[]{:S(2)}) %collective-permute-start.14) | collective-permute-done | bytes 163872 | tf_op jit(solution)/shard_map/ppermute | solution.py:21
  78.7 3.3 %collective-permute-start.19 = (bf16[2,10,1024]{2,1,0:T(8,128)(2,1)S(1)}, bf16[2,10,1024]{2,1,0:T(8,128)(2,1)S(1)}, u32[]{:S(2)}, u32[]{:S(2)}) collective-permute-start(bf16[2,10,1024]{2,1,0:T(8,128)(2,1)S(1)} %get-tuple-element.65), channel_id=1, source_target_pairs={{0,8},{4,12},{8,0},{12,4},{1,9},{5,13},{9,1},{13,5},{2,10},{6,14},... | collective-permute-start | bytes 122888 | tf_op jit(solution)/shard_map/ppermute | solution.py:21
  83.1 2.1 %collective-permute-start.18 = (bf16[2,10,1024]{2,1,0:T(8,128)(2,1)S(1)}, bf16[2,10,1024]{2,1,0:T(8,128)(2,1)S(1)}, u32[]{:S(2)}, u32[]{:S(2)}) collective-permute-start(bf16[2,10,1024]{2,1,0:T(8,128)(2,1)S(1)} %get-tuple-element.64), channel_id=1, source_target_pairs={{0,8},{4,12},{8,0},{12,4},{1,9},{5,13},{9,1},{13,5},{2,10},{6,14},... | collective-permute-start | bytes 122888 | tf_op jit(solution)/shard_map/ppermute | solution.py:21
  85.3 3.8 %collective-permute-done.18.refs_2_ = bf16[2,10,1024]{2,1,0:T(8,128)(2,1)S(1)} collective-permute-done((bf16[2,10,1024]{2,1,0:T(8,128)(2,1)S(1)}, bf16[2,10,1024]{2,1,0:T(8,128)(2,1)S(1)}, u32[]{:S(2)}, u32[]{:S(2)}) %collective-permute-start.18) | collective-permute-done | bytes 40992 | tf_op jit(solution)/shard_map/ppermute | solution.py:21
  (49 shorter events, 12.1 us)
Async XLA Ops:
  0.6 8.0 %collective-permute-start = (bf16[10,2048]{1,0:T(8,128)(2,1)}, bf16[10,2048]{1,0:T(8,128)(2,1)S(1)}, u32[]{:S(2)}, u32[]{:S(2)}) collective-permute-start(bf16[10,2048]{1,0:T(8,128)(2,1)} %refs_0_.5), channel_id=1, source_target_pairs={{0,8},{4,12},{8,0},{12,4},{1,9},{5,13},{9,1},{13,5},{2,10},{6,14},... | collective-permute-start | bytes 122888 | tf_op jit(solution)/shard_map/ppermute | solution.py:21
  4.7 6.7 %collective-permute-start.1 = (bf16[10,2048]{1,0:T(8,128)(2,1)}, bf16[10,2048]{1,0:T(8,128)(2,1)S(1)}, u32[]{:S(2)}, u32[]{:S(2)}) collective-permute-start(bf16[10,2048]{1,0:T(8,128)(2,1)} %refs_1_.2), channel_id=1, source_target_pairs={{0,8},{4,12},{8,0},{12,4},{1,9},{5,13},{9,1},{13,5},{2,10},{6,14},... | collective-permute-start | bytes 122888 | tf_op jit(solution)/shard_map/ppermute | solution.py:21
  4.9 6.5 %copy-start.1 = (bf16[10,2048]{1,0:T(8,128)(2,1)S(1)}, bf16[10,2048]{1,0:T(8,128)(2,1)}, u32[]{:S(2)}) copy-start(bf16[10,2048]{1,0:T(8,128)(2,1)} %refs_0_.5) | copy-start | bytes 122884
  4.9 6.5 %copy-start.2 = (bf16[10,2048]{1,0:T(8,128)(2,1)S(1)}, bf16[10,2048]{1,0:T(8,128)(2,1)}, u32[]{:S(2)}) copy-start(bf16[10,2048]{1,0:T(8,128)(2,1)} %refs_1_.2) | copy-start | bytes 122884
  11.5 5.8 %collective-permute-start.2 = (bf16[2,20,2048]{2,1,0:T(8,128)(2,1)S(1)}, bf16[2,20,2048]{2,1,0:T(8,128)(2,1)S(1)}, u32[]{:S(2)}, u32[]{:S(2)}) collective-permute-start(bf16[2,20,2048]{2,1,0:T(8,128)(2,1)S(1)} %pack.2.refs_1_.refs_0_), channel_id=1, source_target_pairs={{0,4},{4,0},{8,12},{12,8},{1,5},{5,1},{9,13},{13,9},{2,6},{6,2},{1... | collective-permute-start | bytes 491528 | tf_op jit(solution)/shard_map/ppermute | solution.py:21
  17.3 9.5 %collective-permute-start.3 = (bf16[2,40,2048]{2,1,0:T(8,128)(2,1)S(1)}, bf16[2,40,2048]{2,1,0:T(8,128)(2,1)S(1)}, u32[]{:S(2)}, u32[]{:S(2)}) collective-permute-start(bf16[2,40,2048]{2,1,0:T(8,128)(2,1)S(1)} %pack.3.refs_2_.near), channel_id=1, source_target_pairs={{0,16},{16,0},{1,17},{17,1},{2,18},{18,2},{3,19},{19,3},{4,20},{20... | collective-permute-start | bytes 983048 | tf_op jit(solution)/shard_map/ppermute | solution.py:21
  31.0 4.5 %collective-permute-start.4 = (f32[40,1792]{1,0:T(8,128)S(1)}, f32[40,1792]{1,0:T(8,128)S(1)}, u32[]{:S(2)}, u32[]{:S(2)}) collective-permute-start(f32[40,1792]{1,0:T(8,128)S(1)} %get-tuple-element.40), channel_id=1, source_target_pairs={{0,1},{1,0},{2,3},{3,2},{4,5},{5,4},{6,7},{7,6},{8,9},{9,8},{10,11... | collective-permute-start | bytes 860168 | tf_op jit(solution)/shard_map/ppermute | solution.py:21
  31.0 4.5 %collective-permute-start.5 = (f32[40,1792]{1,0:T(8,128)S(1)}, f32[40,1792]{1,0:T(8,128)S(1)}, u32[]{:S(2)}, u32[]{:S(2)}) collective-permute-start(f32[40,1792]{1,0:T(8,128)S(1)} %get-tuple-element.41), channel_id=1, source_target_pairs={{0,1},{1,0},{2,3},{3,2},{4,5},{5,4},{6,7},{7,6},{8,9},{9,8},{10,11... | collective-permute-start | bytes 860168 | tf_op jit(solution)/shard_map/ppermute | solution.py:21
  35.3 1.6 %collective-permute-start.6 = (f32[40,1792]{1,0:T(8,128)S(1)}, f32[40,1792]{1,0:T(8,128)S(1)}, u32[]{:S(2)}, u32[]{:S(2)}) collective-permute-start(f32[40,1792]{1,0:T(8,128)S(1)} %get-tuple-element.42), channel_id=1, source_target_pairs={{0,1},{1,0},{2,3},{3,2},{4,5},{5,4},{6,7},{7,6},{8,9},{9,8},{10,11... | collective-permute-start | bytes 860168 | tf_op jit(solution)/shard_map/ppermute | solution.py:21
  37.1 12.0 %collective-permute-start.11 = (bf16[3,40,1792]{2,1,0:T(8,128)(2,1)S(1)}, bf16[3,40,1792]{2,1,0:T(8,128)(2,1)S(1)}, u32[]{:S(2)}, u32[]{:S(2)}) collective-permute-start(bf16[3,40,1792]{2,1,0:T(8,128)(2,1)S(1)} %get-tuple-element.43.refs_3_.refs_1_), channel_id=1, source_target_pairs={{0,2},{1,3},{2,0},{3,1},{4,6},{5,7},{6,4},{7,5},{8,10},{9,11},{10,... | collective-permute-start | bytes 1290248 | tf_op jit(solution)/shard_map/ppermute | solution.py:21
  38.9 12.4 %slice-start = ((s8[7340032]{0:T(1024)(128)(4,1)}), s8[4194304]{0:T(1024)(128)(4,1)S(1)}, s32[]{:S(2)}) async-start(s8[7340032]{0:T(1024)(128)(4,1)} %bitcast.2), calls=%async_computation | async-start | bytes 8388608
  38.9 12.4 %slice-start.1 = ((s8[7340032]{0:T(1024)(128)(4,1)}), s8[3145728]{0:T(1024)(128)(4,1)S(1)}, s32[]{:S(2)}) async-start(s8[7340032]{0:T(1024)(128)(4,1)} %bitcast.2), calls=%async_computation.1 | async-start | bytes 6291456
  42.5 4.1 %collective-permute-start.7 = (f32[40,1536]{1,0:T(8,128)S(1)}, f32[40,1536]{1,0:T(8,128)S(1)}, u32[]{:S(2)}, u32[]{:S(2)}) collective-permute-start(f32[40,1536]{1,0:T(8,128)S(1)} %get-tuple-element.48), channel_id=1, source_target_pairs={{0,1},{1,0},{2,3},{3,2},{4,5},{5,4},{6,7},{7,6},{8,9},{9,8},{10,11... | collective-permute-start | bytes 737288 | tf_op jit(solution)/shard_map/ppermute | solution.py:21
  42.6 4.0 %collective-permute-start.8 = (f32[40,1536]{1,0:T(8,128)S(1)}, f32[40,1536]{1,0:T(8,128)S(1)}, u32[]{:S(2)}, u32[]{:S(2)}) collective-permute-start(f32[40,1536]{1,0:T(8,128)S(1)} %get-tuple-element.49), channel_id=1, source_target_pairs={{0,1},{1,0},{2,3},{3,2},{4,5},{5,4},{6,7},{7,6},{8,9},{9,8},{10,11... | collective-permute-start | bytes 737288 | tf_op jit(solution)/shard_map/ppermute | solution.py:21
  46.4 1.6 %collective-permute-start.9 = (f32[40,1536]{1,0:T(8,128)S(1)}, f32[40,1536]{1,0:T(8,128)S(1)}, u32[]{:S(2)}, u32[]{:S(2)}) collective-permute-start(f32[40,1536]{1,0:T(8,128)S(1)} %get-tuple-element.50), channel_id=1, source_target_pairs={{0,1},{1,0},{2,3},{3,2},{4,5},{5,4},{6,7},{7,6},{8,9},{9,8},{10,11... | collective-permute-start | bytes 737288 | tf_op jit(solution)/shard_map/ppermute | solution.py:21
  49.3 2.0 %collective-permute-start.12 = (bf16[3,48,1792]{2,1,0:T(8,128)(2,1)S(1)}, bf16[3,48,1792]{2,1,0:T(8,128)(2,1)S(1)}, u32[]{:S(2)}, u32[]{:S(2)}) collective-permute-start(bf16[3,48,1792]{2,1,0:T(8,128)(2,1)S(1)} %activate.2.own), channel_id=1, source_target_pairs={{0,1},{1,0},{2,3},{3,2},{4,5},{5,4},{6,7},{7,6},{8,9},{9,8},{10,11... | collective-permute-start | bytes 1548296 | tf_op jit(solution)/shard_map/ppermute | solution.py:21
  49.4 11.0 %collective-permute-start.10 = (bf16[3,40,1536]{2,1,0:T(8,128)(2,1)S(1)}, bf16[3,40,1536]{2,1,0:T(8,128)(2,1)S(1)}, u32[]{:S(2)}, u32[]{:S(2)}) collective-permute-start(bf16[3,40,1536]{2,1,0:T(8,128)(2,1)S(1)} %get-tuple-element.52.rest_0_), channel_id=1, source_target_pairs={{0,2},{1,3},{2,0},{3,1},{4,6},{5,7},{6,4},{7,5},{8,10},{9,11},{10,... | collective-permute-start | bytes 1105928 | tf_op jit(solution)/shard_map/ppermute | solution.py:21
  60.6 1.9 %collective-permute-start.13 = (bf16[3,48,1536]{2,1,0:T(8,128)(2,1)S(1)}, bf16[3,48,1536]{2,1,0:T(8,128)(2,1)S(1)}, u32[]{:S(2)}, u32[]{:S(2)}) collective-permute-start(bf16[3,48,1536]{2,1,0:T(8,128)(2,1)S(1)} %activate.3.own), channel_id=1, source_target_pairs={{0,1},{1,0},{2,3},{3,2},{4,5},{5,4},{6,7},{7,6},{8,9},{9,8},{10,11... | collective-permute-start | bytes 1327112 | tf_op jit(solution)/shard_map/ppermute | solution.py:21
  66.2 6.3 %collective-permute-start.16 = (bf16[2,40,1024]{2,1,0:T(8,128)(2,1)S(1)}, bf16[2,40,1024]{2,1,0:T(8,128)(2,1)S(1)}, u32[]{:S(2)}, u32[]{:S(2)}) collective-permute-start(bf16[2,40,1024]{2,1,0:T(8,128)(2,1)S(1)} %get-tuple-element.60), channel_id=1, source_target_pairs={{0,16},{16,0},{1,17},{17,1},{2,18},{18,2},{3,19},{19,3},{4,20},{20... | collective-permute-start | bytes 491528 | tf_op jit(solution)/shard_map/ppermute | solution.py:21
  71.7 6.0 %collective-permute-start.14 = (bf16[2,40,1024]{2,1,0:T(8,128)(2,1)S(1)}, bf16[2,40,1024]{2,1,0:T(8,128)(2,1)S(1)}, u32[]{:S(2)}, u32[]{:S(2)}) collective-permute-start(bf16[2,40,1024]{2,1,0:T(8,128)(2,1)S(1)} %get-tuple-element.55), channel_id=1, source_target_pairs={{0,16},{16,0},{1,17},{17,1},{2,18},{18,2},{3,19},{19,3},{4,20},{20... | collective-permute-start | bytes 491528 | tf_op jit(solution)/shard_map/ppermute | solution.py:21
  72.5 6.2 %collective-permute-start.17 = (bf16[2,20,1024]{2,1,0:T(8,128)(2,1)S(1)}, bf16[2,20,1024]{2,1,0:T(8,128)(2,1)S(1)}, u32[]{:S(2)}, u32[]{:S(2)}) collective-permute-start(bf16[2,20,1024]{2,1,0:T(8,128)(2,1)S(1)} %get-tuple-element.62), channel_id=1, source_target_pairs={{0,4},{4,0},{8,12},{12,8},{1,5},{5,1},{9,13},{13,9},{2,6},{6,2},{1... | collective-permute-start | bytes 245768 | tf_op jit(solution)/shard_map/ppermute | solution.py:21
  77.7 5.4 %collective-permute-start.15 = (bf16[2,20,1024]{2,1,0:T(8,128)(2,1)S(1)}, bf16[2,20,1024]{2,1,0:T(8,128)(2,1)S(1)}, u32[]{:S(2)}, u32[]{:S(2)}) collective-permute-start(bf16[2,20,1024]{2,1,0:T(8,128)(2,1)S(1)} %get-tuple-element.57), channel_id=1, source_target_pairs={{0,4},{4,0},{8,12},{12,8},{1,5},{5,1},{9,13},{13,9},{2,6},{6,2},{1... | collective-permute-start | bytes 245768 | tf_op jit(solution)/shard_map/ppermute | solution.py:21
  78.7 6.5 %collective-permute-start.19 = (bf16[2,10,1024]{2,1,0:T(8,128)(2,1)S(1)}, bf16[2,10,1024]{2,1,0:T(8,128)(2,1)S(1)}, u32[]{:S(2)}, u32[]{:S(2)}) collective-permute-start(bf16[2,10,1024]{2,1,0:T(8,128)(2,1)S(1)} %get-tuple-element.65), channel_id=1, source_target_pairs={{0,8},{4,12},{8,0},{12,4},{1,9},{5,13},{9,1},{13,5},{2,10},{6,14},... | collective-permute-start | bytes 122888 | tf_op jit(solution)/shard_map/ppermute | solution.py:21
  83.1 5.9 %collective-permute-start.18 = (bf16[2,10,1024]{2,1,0:T(8,128)(2,1)S(1)}, bf16[2,10,1024]{2,1,0:T(8,128)(2,1)S(1)}, u32[]{:S(2)}, u32[]{:S(2)}) collective-permute-start(bf16[2,10,1024]{2,1,0:T(8,128)(2,1)S(1)} %get-tuple-element.64), channel_id=1, source_target_pairs={{0,8},{4,12},{8,0},{12,4},{1,9},{5,13},{9,1},{13,5},{2,10},{6,14},... | collective-permute-start | bytes 122888 | tf_op jit(solution)/shard_map/ppermute | solution.py:21
  (1 other events, 6.1 us)

commit v4 on v3

--- a/solution.py
+++ b/solution.py
@@ -11,6 +11,10 @@
 BF16 = jnp.bfloat16
 NT = (((1,), (1,)), ((), ()))
 MIB = 2**20
+WINDOWS = [["g0"], ["u0", "g1"], ["d0"]]
+BESIDE = {"b0": ["u1"], "gu0": [], "gu1": ["d1"], "b1": []}
+FIRST = 0.5
+PIECE = 0.5
 VMEM = pl.BlockSpec(memory_space=pltpu.VMEM)
 SMEM = pl.BlockSpec(memory_space=pltpu.SMEM)
 HBM = pl.BlockSpec(memory_space=pltpu.HBM)
@@ -93,28 +97,37 @@
 
 
 def pack(near, far, after):
-    n, feats = near[0].shape[-2:]
+    n, feats = near[0].shape
+    m = len(near)
 
     def kernel(*refs):
-        out, wide = refs[-2:]
-        for i in range(2):
-            a, b = (refs[i], refs[2 + i]) if len(near) == 2 else (refs[0].at[i], refs[1].at[i])
-            wide[i, :n, :] = a[...].astype(F32)
-            wide[i, n : 2 * n, :] = b[...].astype(F32)
-            out[i] = wide[i].astype(BF16)
+        outs, wide = refs[-m - 1 : -1], refs[-1]
+        for i in range(m):
+            wide[i, :n, :] = refs[i][...].astype(F32)
+            wide[i, n : 2 * n, :] = refs[m + i][...].astype(F32)
+            outs[i][...] = wide[i].astype(BF16)
 
     return call(
         kernel,
         "pack",
-        [VMEM] * (len(near) + len(far)) + [ANY] * len(after),
-        jax.ShapeDtypeStruct((2, 2 * n, feats), BF16),
-        [pltpu.VMEM((2, 2 * n, feats), F32)],
-        limit=4,
+        [VMEM] * (2 * m) + [ANY] * len(after),
+        [jax.ShapeDtypeStruct((2 * n, feats), BF16)] * m,
+        [pltpu.VMEM((m, 2 * n, feats), F32)],
+        limit=2,
     )(*near, *far, *after)
 
 
-def up(where, near, far, which, weights, transposed, block, wanted=(), after=()):
-    _, half, feats = near.shape
+def locate(block, order, count):
+    place = 0
+    for bit, hop in enumerate(order):
+        place += ((block >> hop) & 1) << bit
+    return place // (count // 2), place % (count // 2)
+
+
+def up(where, near, far, order, weights, transposed, block, wanted=(), after=()):
+    half, feats = near.shape
+    count = 2 ** len(order)
+    rows = 2 * half // count
     width = weights[0].shape[0 if transposed else 1]
     n, m = len(weights), len(wanted)
     specs = [s for _, s in wanted]
@@ -131,14 +144,17 @@
         for copy in made:
             copy.start()
         first = where[1] == 0
-        a, b = near[which].astype(F32), far[which].astype(F32)
-        wide[:half, :] = jnp.where(first, a, b)
-        wide[half:, :] = jnp.where(first, b, a)
+        both = (near[...].astype(F32), far[...].astype(F32))
+        run = half if order == sorted(order) else rows
+        for at in range(0, 2 * half, run):
+            picks = []
+            for start in (at, (at + half) % (2 * half)):
+                side, place = locate(start // rows, order, count)
+                picks.append(both[side][place * rows : place * rows + run])
+            wide[at : at + run, :] = jnp.where(first, *picks)
         lhs[...] = wide[...].astype(BF16)
 
-        @pl.loop(0, width // block)
-        def _(step):
-            cut = pl.ds(pl.multiple_of(step * block, block), block)
+        def tile(cut):
             for i, w in enumerate(ws):
                 if transposed:
                     value = lax.dot_general(lhs[...], w[cut, :], NT, preferred_element_type=F32)
@@ -147,6 +163,16 @@
                 outs[2 * i][:, cut] = value[:half]
                 outs[2 * i + 1][:, cut] = value[half:]
 
+        if made:
+            block2 = width // 2 if width % 256 == 0 else width
+
+            @pl.loop(0, width // block2)
+            def _(step):
+                tile(pl.ds(pl.multiple_of(step * block2, 128), block2))
+
+        else:
+            for step in range(width // block):
+                tile(slice(step * block, (step + 1) * block))
         for copy in made:
             copy.wait()
 
@@ -158,7 +184,7 @@
         [out] * (2 * n) + [fetched(w, s) for w, s in wanted],
         [pltpu.VMEM((2 * half, feats), F32), pltpu.VMEM((2 * half, feats), BF16)]
         + ([pltpu.SemaphoreType.DMA((m,))] if m else []),
-        limit=6,
+        limit=2,
         estimate=cost(2 * n * 256 * feats * width, 2 * n * feats * width),
     )(where, near, far, *[resident(w) for w in weights], *[in_hbm(w) for w, _ in wanted], *after)
     return got[: 2 * n : 2], got[1 : 2 * n : 2], got[2 * n :]
@@ -220,13 +246,14 @@
         "activate",
         [VMEM] * 2 + [ANY] * len(after),
         jax.ShapeDtypeStruct((3, padded, width), BF16),
-        limit=4,
+        limit=2,
     )(sums, got, *after)
 
 
-def down(where, own, other, weights, prev, half, part, last, block):
+def down(where, own, other, weights, prev, half, part, last):
     _, padded, width = own.shape
     start, feats = part
+    block = 256 if feats % 256 == 0 else 128
 
     def kernel(where, own, other, gate_w, up_w, down_w, *rest):
         lhs = rest[-1]
@@ -235,10 +262,9 @@
         lhs[:, :padded, :] = own[...]
         lhs[:, padded:, :] = other[...]
 
-        @pl.loop(0, feats // block)
-        def _(step):
-            cut = pl.ds(pl.multiple_of(step * block, block), block)
-            full = pl.ds(pl.multiple_of(start + step * block, block), block)
+        for step in range(feats // block):
+            cut = slice(step * block, (step + 1) * block)
+            full = slice(start + step * block, start + (step + 1) * block)
             mixed = jnp.dot(lhs[0], down_w[:, full], preferred_element_type=F32)
             grad = lax.dot_general(lhs[1], gate_w[full, :], NT, preferred_element_type=F32)
             grad += lax.dot_general(lhs[2], up_w[full, :], NT, preferred_element_type=F32)
@@ -268,7 +294,7 @@
         [SMEM] + [VMEM] * (5 + len(prev)),
         shapes,
         [pltpu.VMEM((3, 2 * padded, width), BF16)],
-        limit=6,
+        limit=2,
         estimate=cost(6 * 256 * feats * width, 6 * feats * width),
     )(where, own, other, *[resident(w) for w in weights], *prev)
 
@@ -293,20 +319,22 @@
 
 def finish(keeps, gots):
     n = len(keeps)
-    _, rows, feats = keeps[0].shape
+    rows = keeps[0].shape[1]
+    sizes = [k.shape[2] for k in keeps]
 
     def kernel(*refs):
         outs = refs[2 * n :]
-        for j in range(n):
+        for j, size in enumerate(sizes):
+            at = sum(sizes[:j])
             for i in range(2):
                 value = refs[j][i] + refs[n + j][i].astype(F32)
-                outs[i][:, j * feats : (j + 1) * feats] = value.astype(BF16)
+                outs[i][:, at : at + size] = value.astype(BF16)
 
     return call(
         kernel,
         "finish",
         [VMEM] * (2 * n),
-        [jax.ShapeDtypeStruct((rows, n * feats), BF16)] * 2,
+        [jax.ShapeDtypeStruct((rows, sum(sizes)), BF16)] * 2,
     )(*keeps, *gots)
 
 
@@ -317,9 +345,10 @@
     whole = units // grp if split else units
     block = 256 if whole % 256 == 0 else 128
     blocks = whole // block
-    cuts = [0, blocks - blocks // 2, blocks] if blocks > 1 else [0, blocks]
+    cuts = [0, int(blocks * FIRST), blocks] if blocks > 1 else [0, blocks]
     chunks = [(a * block, (b - a) * block) for a, b in zip(cuts, cuts[1:])]
-    down_block = 256 if feats % 256 == 0 else 128
+    lead = int(feats * PIECE) // 256 * 256
+    pieces = [(0, lead), (lead, feats - lead)] if lead else [(0, feats)]
 
     core = lax.axis_index("bulk") % 2
     group = lax.axis_index("grp") if split else jnp.int32(0)
@@ -329,53 +358,61 @@
     if split:
         hops += [("grp", grp, b) for b in bits(grp)]
 
-    gates, ups, downs = (
-        [(w, (dim, whole, start, size)) for start, size in chunks]
-        for w, dim in ((gate_weight, 1), (up_weight, 1), (down_weight, 0))
-    )
-    (gate0,) = fetch(where, [gates[0]])
-    near = (tokens, cotangent)
-    far = tuple(swap(v, *hops[0]) for v in near)
-    near = pack(near, far, (gate0,))
-    (up0,) = fetch(where, [ups[0]], (near,))
-    for hop in hops[1:-1]:
-        near = pack((near,), (swap(near, *hop),), (up0,))
-    far = swap(near, *hops[-1])
-    down0, *more = fetch(where, [downs[0]] + gates[1:], (near,))
-    half = near.shape[1]
+    sources = {"g": (gate_weight, 1), "u": (up_weight, 1), "d": (down_weight, 0)}
+    here = {}
+
+    def wanted(names):
+        found = []
+        for name in names:
+            if int(name[1]) < len(chunks):
+                weight, dim = sources[name[0]]
+                found.append((name, (weight, (dim, whole, *chunks[int(name[1])]))))
+        return [n for n, _ in found], [w for _, w in found]
+
+    n = len(hops)
+    orders = (list(range(n)), [n - 1, *range(n - 1)])
+    near, far = [tokens, cotangent], [None, None]
+    after = []
+    for step in range(n):
+        far = [swap(v, *hops[o[step]]) for v, o in zip(near, orders)]
+        names, parts = wanted(WINDOWS[2 if step == n - 1 else step] if step < 2 or step == n - 1 else [])
+        got = fetch(where, parts, after) if parts else []
+        here.update(zip(names, got))
+        if step < n - 1:
+            near = pack(near, far, got)
+            after = near
+    half = near[0].shape[0]
     padded = -(-half // 16) * 16
 
-    weights = [[gate0, up0, down0]] + [[g, None, None] for g in more]
     summed = []
     after = ()
-    for c, w in enumerate(weights):
-        later = ups[1:] if c == 0 else downs[c : c + 1]
-        keep, send, got = up(where, near, far, 0, w[:2], False, block, later, after)
-        if c == 0:
-            for v, value in zip(weights[1:], got):
-                v[1] = value
-        else:
-            w[2] = got[0]
-        keep_b, send_b, _ = up(where, near, far, 1, w[2:], True, block, (), after)
-        keep, send = [*keep, *keep_b], [*send, *send_b]
+    for c in range(len(chunks)):
+        out = {}
+        for kind, i in (("gu", 0), ("b", 1)) if c else (("b", 1), ("gu", 0)):
+            ws = [here[f"{w}{c}"] for w in ("d" if kind == "b" else "gu")]
+            names, parts = wanted(BESIDE[f"{kind}{c}"])
+            *out[kind], got = up(
+                where, near[i], far[i], orders[i], ws, kind == "b", block, parts, after
+            )
+            here.update(zip(names, got))
+        keep, send = ([*out["gu"][i], *out["b"][i]] for i in range(2))
         sums, rounded = gather(keep, [swap(v, "bulk", bulk, 1) for v in send])
         after = (rounded,)
         summed.append((sums, rounded))
 
     prev = ()
-    for c, (w, (sums, rounded)) in enumerate(zip(weights, summed)):
+    for c, (sums, rounded) in enumerate(summed):
         for b in bits(bulk, 2)[:-1]:
             sums, rounded = add(sums, swap(rounded, "bulk", bulk, b))
         got = swap(rounded, "bulk", bulk, bits(bulk, 2)[-1])
+        w = [here[f"{name}{c}"] for name in "gud"]
         own = activate(sums, got, padded, (*prev, *[r for _, r in summed[c + 1 :]]))
         other = swap(own, "bulk", bulk, 1)
         if c < len(chunks) - 1:
-            prev = down(where, own, other, w, prev, half, (0, feats), False, down_block)
-    pieces = 2 if feats % (2 * down_block) == 0 else 1
+            prev = down(where, own, other, w, prev, half, (0, feats), False)
     stays, gots = [], []
-    for p in range(pieces):
-        part = (p * feats // pieces, feats // pieces)
-        stay, send = down(where, own, other, w, prev, half, part, True, down_block)
+    for part in pieces:
+        stay, send = down(where, own, other, w, prev, half, part, True)
         for hop in reversed(hops[1:]):
             stay, send = fold(stay, swap(send, *hop))
         stays.append(stay)

time: 89.9 us -> 83.7 us (0.931)
  Pallas kernels: 43.4 us -> 38.5 us
  waiting for transfers between devices: 23 us -> 21.5 us
    pallas_call x3, Pallas kernels: 14.3 us -> 11.8 us  [down(): call(kernel, 'down', [SMEM] + [VMEM] * (5 + len(prev)), shapes, [pltpu.VM...]
    pallas_call x4, Pallas kernels: 14.9 us -> 13 us  [up(): call(kernel, 'up', [SMEM] + [VMEM] * (2 + n) + [HBM] * m + [ANY] * len(af...]
    ppermute x20 -> x22, waiting for transfers between devices: 23 us -> 21.5 us  [swap(): return lax.ppermute(value, axis, [(i, i ^ bit) for i in range(size)])]
    ppermute x20 -> x22, starting transfers between devices: 22.5 us -> 22.5 us  [swap(): return lax.ppermute(value, axis, [(i, i ^ bit) for i in range(size)])]
  transfers between devices with their start and end apart: 20 -> 22, of which waited for: 14 -> 11; matrix products, arithmetic and copies ran while one was open for 0% -> 0% of each run, Pallas kernels for 38% -> 41%
where the time goes in v4:
time: 83.7 us; the launch traced here: 83.4 us
  Pallas kernels  38.5 us (46%)
  starting transfers between devices  22.5 us (27%)
  waiting for transfers between devices  21.5 us (26%)
    ppermute x22, starting transfers between devices, swap(): return lax.ppermute(value, axis, [(i, i ^ bit) for i in range(size)])  22.5 us
    ppermute x22, waiting for transfers between devices, swap(): return lax.ppermute(value, axis, [(i, i ^ bit) for i in range(size)])  21.5 us
    pallas_call x4, Pallas kernels, up(): call(kernel, 'up', [SMEM] + [VMEM] * (2 + n) + [HBM] * m + [ANY] * len(af...  13 us
    pallas_call x3, Pallas kernels, fetch(): call(kernel, 'fetch', [SMEM] + [HBM] * n + [ANY] * len(after), outs, [plt...  12.2 us
    pallas_call x3, Pallas kernels, down(): call(kernel, 'down', [SMEM] + [VMEM] * (5 + len(prev)), shapes, [pltpu.VM...  11.8 us
  transfers between devices with their start and end apart: 22, of which 11 were waited for; matrix products, arithmetic and copies ran while one was open for 0% of the time, Pallas kernels for 41%

profile of v4, /device:TPU:0, one launch (start us, length us, event | category | flops | bytes accessed | tf_op | source)
XLA Modules:
  0.0 83.4 jit_solution(17775040707184800239)
XLA Ops:
  0.6 4.1 %collective-permute-start = (bf16[10,2048]{1,0:T(8,128)(2,1)}, bf16[10,2048]{1,0:T(8,128)(2,1)S(1)}, u32[]{:S(2)}, u32[]{:S(2)}) collective-permute-start(bf16[10,2048]{1,0:T(8,128)(2,1)} %refs_0_.5), channel_id=1, source_target_pairs={{0,8},{4,12},{8,0},{12,4},{1,9},{5,13},{9,1},{13,5},{2,10},{6,14},... | collective-permute-start | bytes 122888 | tf_op jit(solution)/shard_map/ppermute | solution.py:25
  4.7 1.5 %collective-permute-start.1 = (bf16[10,2048]{1,0:T(8,128)(2,1)}, bf16[10,2048]{1,0:T(8,128)(2,1)S(1)}, u32[]{:S(2)}, u32[]{:S(2)}) collective-permute-start(bf16[10,2048]{1,0:T(8,128)(2,1)} %refs_1_.3), channel_id=1, source_target_pairs={{0,16},{16,0},{1,17},{17,1},{2,18},{18,2},{3,19},{19,3},{4,20},{20... | collective-permute-start | bytes 122888 | tf_op jit(solution)/shard_map/ppermute | solution.py:25
  6.3 3.3 %fetch.3.refs_4_.refs_0_.gate_w = bf16[2048,1536]{1,0:T(8,128)(2,1)S(1)} custom-call(s32[2]{0:T(128)S(1)} %pad_add_fusion.where, bf16[2048,6656]{1,0:T(8,128)(2,1)} %refs_1_.4), custom_call_target="tpu_custom_call" | custom-call | bytes 6291456 | tf_op jit(solution)/shard_map/fetch/pallas_call | solution.py:89
  9.8 1.6 %collective-permute-start.2 = (bf16[20,2048]{1,0:T(8,128)(2,1)S(1)}, bf16[20,2048]{1,0:T(8,128)(2,1)S(1)}, u32[]{:S(2)}, u32[]{:S(2)}) collective-permute-start(bf16[20,2048]{1,0:T(8,128)(2,1)S(1)} %get-tuple-element.38.refs_2_.refs_0_), channel_id=1, source_target_pairs={{0,4},{4,0},{8,12},{12,8},{1,5},{5,1},{9,13},{13,9},{2,6},{6,2},{1... | collective-permute-start | bytes 245768 | tf_op jit(solution)/shard_map/ppermute | solution.py:25
  12.7 5.5 %fetch.4 = (bf16[2048,1536]{1,0:T(8,128)(2,1)S(1)}, bf16[2048,1792]{1,0:T(8,128)(2,1)S(1)}) custom-call(s32[2]{0:T(128)S(1)} %pad_add_fusion.where, bf16[2048,6656]{1,0:T(8,128)(2,1)} %refs_1_.5, bf16[2048,6656]{1,0:T(8,128)(2,1)} %refs_1_.4, bf16[20,2048]{1,0:T(8,128)(2,1)S(1)} %get-tuple-element.38.refs_2_.refs_0_, ...), custom_call_target="tpu_custom_call" | custom-call | bytes 13631488 | tf_op jit(solution)/shard_map/fetch/pallas_call | solution.py:89
  18.3 1.7 %collective-permute-start.4 = (bf16[40,2048]{1,0:T(8,128)(2,1)S(1)}, bf16[40,2048]{1,0:T(8,128)(2,1)S(1)}, u32[]{:S(2)}, u32[]{:S(2)}) collective-permute-start(bf16[40,2048]{1,0:T(8,128)(2,1)S(1)} %get-tuple-element.42.refs_1_.near), channel_id=1, source_target_pairs={{0,16},{16,0},{1,17},{17,1},{2,18},{18,2},{3,19},{19,3},{4,20},{20... | collective-permute-start | bytes 491528 | tf_op jit(solution)/shard_map/ppermute | solution.py:25
  20.0 3.3 %fetch.5.refs_0_.down_w = bf16[1536,2048]{1,0:T(8,128)(2,1)S(1)} custom-call(s32[2]{0:T(128)S(1)} %pad_add_fusion.where, bf16[6656,2048]{1,0:T(8,128)(2,1)} %refs_2_.1, bf16[40,2048]{1,0:T(8,128)(2,1)S(1)} %get-tuple-element.42.refs_1_.near, bf16[40,2048]{1,0:T(8,128)(2,1)S(1)} %get-tuple-element.43.refs_2_.near), custom_call_target="tpu_custom_call" | custom-call | bytes 6291456 | tf_op jit(solution)/shard_map/fetch/pallas_call | solution.py:89
  23.6 2.8 %up.5 = (f32[40,1536]{1,0:T(8,128)S(1)}, f32[40,1536]{1,0:T(8,128)S(1)}, f32[40,1536]{1,0:T(8,128)S(1)}, f32[40,1536]{1,0:T(8,128)S(1)}) custom-call(s32[2]{0:T(128)S(1)} %pad_add_fusion.where, bf16[40,2048]{1,0:T(8,128)(2,1)S(1)} %get-tuple-element.42.refs_1_.near, bf16[40,2048]{1,0:T(8,128)(2,1)S(1)} %collective-permute-done.4.far, ...), custom_call_target="tpu_custom_call" | custom-call | flops 3221225472 | bytes 12582912 | tf_op jit(solution)/shard_map/up/pallas_call | solution.py:180
  27.1 3.6 %up.4 = (f32[40,1536]{1,0:T(8,128)S(1)}, f32[40,1536]{1,0:T(8,128)S(1)}, bf16[2048,1792]{1,0:T(8,128)(2,1)S(1)}) custom-call(s32[2]{0:T(128)S(1)} %pad_add_fusion.where, bf16[40,2048]{1,0:T(8,128)(2,1)S(1)} %get-tuple-element.43.refs_2_.near, bf16[40,2048]{1,0:T(8,128)(2,1)S(1)} %collective-permute-done.5.far, bf16[1536,2048]{1,0:T(8,128)(2,1)S(1)} %fetch.5.refs_0_.down_w, ...), custom_call_target="tpu_custom_call" | custom-call | flops 1610612736 | bytes 6291456 | tf_op jit(solution)/shard_map/up/pallas_call | solution.py:180
  32.4 1.6 %collective-permute-start.13 = (bf16[3,40,1536]{2,1,0:T(8,128)(2,1)S(1)}, bf16[3,40,1536]{2,1,0:T(8,128)(2,1)S(1)}, u32[]{:S(2)}, u32[]{:S(2)}) collective-permute-start(bf16[3,40,1536]{2,1,0:T(8,128)(2,1)S(1)} %get-tuple-element.51.refs_3_.refs_1_), channel_id=1, source_target_pairs={{0,2},{1,3},{2,0},{3,1},{4,6},{5,7},{6,4},{7,5},{8,10},{9,11},{10,... | collective-permute-start | bytes 1105928 | tf_op jit(solution)/shard_map/ppermute | solution.py:25
  33.9 3.6 %up.6 = (f32[40,1792]{1,0:T(8,128)S(1)}, f32[40,1792]{1,0:T(8,128)S(1)}, f32[40,1792]{1,0:T(8,128)S(1)}, f32[40,1792]{1,0:T(8,128)S(1)}, bf16[1792,2048]{1,0:T(8,128)(2,1)S(1)}) custom-call(s32[2]{0:T(128)S(1)} %pad_add_fusion.where, bf16[40,2048]{1,0:T(8,128)(2,1)S(1)} %get-tuple-element.42.refs_1_.near, bf16[40,2048]{1,0:T(8,128)(2,1)S(1)} %collective-permute-done.4.far, ...), custom_call_target="tpu_custom_call" | custom-call | flops 3758096384 | bytes 14680064 | tf_op jit(solution)/shard_map/up/pallas_call | solution.py:180
  38.2 2.9 %up.7 = (f32[40,1792]{1,0:T(8,128)S(1)}, f32[40,1792]{1,0:T(8,128)S(1)}) custom-call(s32[2]{0:T(128)S(1)} %pad_add_fusion.where, bf16[40,2048]{1,0:T(8,128)(2,1)S(1)} %get-tuple-element.43.refs_2_.near, bf16[40,2048]{1,0:T(8,128)(2,1)S(1)} %collective-permute-done.5.far, bf16[1792,2048]{1,0:T(8,128)(2,1)S(1)} %get-tuple-element.54.refs_0_.down_w, ...), custom_call_target="tpu_custom_call" | custom-call | flops 1879048192 | bytes 7340032 | tf_op jit(solution)/shard_map/up/pallas_call | solution.py:180
  43.3 1.6 %collective-permute-start.12 = (bf16[3,40,1792]{2,1,0:T(8,128)(2,1)S(1)}, bf16[3,40,1792]{2,1,0:T(8,128)(2,1)S(1)}, u32[]{:S(2)}, u32[]{:S(2)}) collective-permute-start(bf16[3,40,1792]{2,1,0:T(8,128)(2,1)S(1)} %get-tuple-element.60.rest_0_), channel_id=1, source_target_pairs={{0,2},{1,3},{2,0},{3,1},{4,6},{5,7},{6,4},{7,5},{8,10},{9,11},{10,... | collective-permute-start | bytes 1290248 | tf_op jit(solution)/shard_map/ppermute | solution.py:25
  45.1 5.4 %down.3.rest_0_ = f32[2,96,2048]{2,1,0:T(8,128)S(1)} custom-call(s32[2]{0:T(128)S(1)} %pad_add_fusion.where, bf16[3,48,1536]{2,1,0:T(8,128)(2,1)S(1)} %activate.2.own, bf16[3,48,1536]{2,1,0:T(8,128)(2,1)S(1)} %collective-permute-done.14.other, bf16[2048,1536]{1,0:T(8,128)(2,1)S(1)} %fetch.3.refs_4_.refs_0_.gate_w, bf16[2048,1536]{1,0:T(8,128)(2,1)S(1)} %bitcast.3, ...), custom_call_target="tpu_custom_call" | custom-call | flops 4831838208 | bytes 18874368 | tf_op jit(solution)/shard_map/down/pallas_call | solution.py:291
  50.5 5.1 %collective-permute-done.12.got = bf16[3,40,1792]{2,1,0:T(8,128)(2,1)S(1)} collective-permute-done((bf16[3,40,1792]{2,1,0:T(8,128)(2,1)S(1)}, bf16[3,40,1792]{2,1,0:T(8,128)(2,1)S(1)}, u32[]{:S(2)}, u32[]{:S(2)}) %collective-permute-start.12) | collective-permute-done | bytes 430112 | tf_op jit(solution)/shard_map/ppermute | solution.py:25
  56.0 1.9 %collective-permute-done.15.other = bf16[3,48,1792]{2,1,0:T(8,128)(2,1)S(1)} collective-permute-done((bf16[3,48,1792]{2,1,0:T(8,128)(2,1)S(1)}, bf16[3,48,1792]{2,1,0:T(8,128)(2,1)S(1)}, u32[]{:S(2)}, u32[]{:S(2)}) %collective-permute-start.15) | collective-permute-done | bytes 516128 | tf_op jit(solution)/shard_map/ppermute | solution.py:25
  57.8 3.2 %down.5 = (f32[2,40,1024]{2,1,0:T(8,128)S(1)}, bf16[2,40,1024]{2,1,0:T(8,128)(2,1)S(1)}) custom-call(s32[2]{0:T(128)S(1)} %pad_add_fusion.where, bf16[3,48,1792]{2,1,0:T(8,128)(2,1)S(1)} %activate.3.own, bf16[3,48,1792]{2,1,0:T(8,128)(2,1)S(1)} %collective-permute-done.15.other, bf16[2048,1792]{1,0:T(8,128)(2,1)S(1)} %get-tuple-element.41.refs_5_.refs_0_.gate_w, ...), custom_call_target="tpu_custom_call" | custom-call | flops 2818572288 | bytes 11010048 | tf_op jit(solution)/shard_map/down/pallas_call | solution.py:291
  61.0 1.7 %collective-permute-start.18 = (bf16[2,40,1024]{2,1,0:T(8,128)(2,1)S(1)}, bf16[2,40,1024]{2,1,0:T(8,128)(2,1)S(1)}, u32[]{:S(2)}, u32[]{:S(2)}) collective-permute-start(bf16[2,40,1024]{2,1,0:T(8,128)(2,1)S(1)} %get-tuple-element.68), channel_id=1, source_target_pairs={{0,16},{16,0},{1,17},{17,1},{2,18},{18,2},{3,19},{19,3},{4,20},{20... | collective-permute-start | bytes 491528 | tf_op jit(solution)/shard_map/ppermute | solution.py:25
  62.7 3.2 %down.4 = (f32[2,40,1024]{2,1,0:T(8,128)S(1)}, bf16[2,40,1024]{2,1,0:T(8,128)(2,1)S(1)}) custom-call(s32[2]{0:T(128)S(1)} %pad_add_fusion.where, bf16[3,48,1792]{2,1,0:T(8,128)(2,1)S(1)} %activate.3.own, bf16[3,48,1792]{2,1,0:T(8,128)(2,1)S(1)} %collective-permute-done.15.other, bf16[2048,1792]{1,0:T(8,128)(2,1)S(1)} %get-tuple-element.41.refs_5_.refs_0_.gate_w, ...), custom_call_target="tpu_custom_call" | custom-call | flops 2818572288 | bytes 11010048 | tf_op jit(solution)/shard_map/down/pallas_call | solution.py:291
  67.4 1.8 %collective-permute-start.19 = (bf16[2,20,1024]{2,1,0:T(8,128)(2,1)S(1)}, bf16[2,20,1024]{2,1,0:T(8,128)(2,1)S(1)}, u32[]{:S(2)}, u32[]{:S(2)}) collective-permute-start(bf16[2,20,1024]{2,1,0:T(8,128)(2,1)S(1)} %get-tuple-element.70), channel_id=1, source_target_pairs={{0,4},{4,0},{8,12},{12,8},{1,5},{5,1},{9,13},{13,9},{2,6},{6,2},{1... | collective-permute-start | bytes 245768 | tf_op jit(solution)/shard_map/ppermute | solution.py:25
  69.1 2.8 %collective-permute-done.16.got = bf16[2,40,1024]{2,1,0:T(8,128)(2,1)S(1)} collective-permute-done((bf16[2,40,1024]{2,1,0:T(8,128)(2,1)S(1)}, bf16[2,40,1024]{2,1,0:T(8,128)(2,1)S(1)}, u32[]{:S(2)}, u32[]{:S(2)}) %collective-permute-start.16) | collective-permute-done | bytes 163872 | tf_op jit(solution)/shard_map/ppermute | solution.py:25
  72.7 1.6 %collective-permute-start.21 = (bf16[2,10,1024]{2,1,0:T(8,128)(2,1)S(1)}, bf16[2,10,1024]{2,1,0:T(8,128)(2,1)S(1)}, u32[]{:S(2)}, u32[]{:S(2)}) collective-permute-start(bf16[2,10,1024]{2,1,0:T(8,128)(2,1)S(1)} %get-tuple-element.73), channel_id=1, source_target_pairs={{0,8},{4,12},{8,0},{12,4},{1,9},{5,13},{9,1},{13,5},{2,10},{6,14},... | collective-permute-start | bytes 122888 | tf_op jit(solution)/shard_map/ppermute | solution.py:25
  74.3 2.5 %collective-permute-done.17.got = bf16[2,20,1024]{2,1,0:T(8,128)(2,1)S(1)} collective-permute-done((bf16[2,20,1024]{2,1,0:T(8,128)(2,1)S(1)}, bf16[2,20,1024]{2,1,0:T(8,128)(2,1)S(1)}, u32[]{:S(2)}, u32[]{:S(2)}) %collective-permute-start.17) | collective-permute-done | bytes 81952 | tf_op jit(solution)/shard_map/ppermute | solution.py:25
  78.2 4.5 %collective-permute-done.20.refs_2_ = bf16[2,10,1024]{2,1,0:T(8,128)(2,1)S(1)} collective-permute-done((bf16[2,10,1024]{2,1,0:T(8,128)(2,1)S(1)}, bf16[2,10,1024]{2,1,0:T(8,128)(2,1)S(1)}, u32[]{:S(2)}, u32[]{:S(2)}) %collective-permute-start.20) | collective-permute-done | bytes 40992 | tf_op jit(solution)/shard_map/ppermute | solution.py:25
  (53 shorter events, 11.8 us)
Async XLA Ops:
  0.6 9.1 %collective-permute-start = (bf16[10,2048]{1,0:T(8,128)(2,1)}, bf16[10,2048]{1,0:T(8,128)(2,1)S(1)}, u32[]{:S(2)}, u32[]{:S(2)}) collective-permute-start(bf16[10,2048]{1,0:T(8,128)(2,1)} %refs_0_.5), channel_id=1, source_target_pairs={{0,8},{4,12},{8,0},{12,4},{1,9},{5,13},{9,1},{13,5},{2,10},{6,14},... | collective-permute-start | bytes 122888 | tf_op jit(solution)/shard_map/ppermute | solution.py:25
  4.7 5.0 %collective-permute-start.1 = (bf16[10,2048]{1,0:T(8,128)(2,1)}, bf16[10,2048]{1,0:T(8,128)(2,1)S(1)}, u32[]{:S(2)}, u32[]{:S(2)}) collective-permute-start(bf16[10,2048]{1,0:T(8,128)(2,1)} %refs_1_.3), channel_id=1, source_target_pairs={{0,16},{16,0},{1,17},{17,1},{2,18},{18,2},{3,19},{19,3},{4,20},{20... | collective-permute-start | bytes 122888 | tf_op jit(solution)/shard_map/ppermute | solution.py:25
  9.8 8.4 %collective-permute-start.2 = (bf16[20,2048]{1,0:T(8,128)(2,1)S(1)}, bf16[20,2048]{1,0:T(8,128)(2,1)S(1)}, u32[]{:S(2)}, u32[]{:S(2)}) collective-permute-start(bf16[20,2048]{1,0:T(8,128)(2,1)S(1)} %get-tuple-element.38.refs_2_.refs_0_), channel_id=1, source_target_pairs={{0,4},{4,0},{8,12},{12,8},{1,5},{5,1},{9,13},{13,9},{2,6},{6,2},{1... | collective-permute-start | bytes 245768 | tf_op jit(solution)/shard_map/ppermute | solution.py:25
  11.4 6.8 %collective-permute-start.3 = (bf16[20,2048]{1,0:T(8,128)(2,1)S(1)}, bf16[20,2048]{1,0:T(8,128)(2,1)S(1)}, u32[]{:S(2)}, u32[]{:S(2)}) collective-permute-start(bf16[20,2048]{1,0:T(8,128)(2,1)S(1)} %get-tuple-element.39.refs_3_.refs_1_), channel_id=1, source_target_pairs={{0,8},{4,12},{8,0},{12,4},{1,9},{5,13},{9,1},{13,5},{2,10},{6,14},... | collective-permute-start | bytes 245768 | tf_op jit(solution)/shard_map/ppermute | solution.py:25
  18.3 5.4 %collective-permute-start.4 = (bf16[40,2048]{1,0:T(8,128)(2,1)S(1)}, bf16[40,2048]{1,0:T(8,128)(2,1)S(1)}, u32[]{:S(2)}, u32[]{:S(2)}) collective-permute-start(bf16[40,2048]{1,0:T(8,128)(2,1)S(1)} %get-tuple-element.42.refs_1_.near), channel_id=1, source_target_pairs={{0,16},{16,0},{1,17},{17,1},{2,18},{18,2},{3,19},{19,3},{4,20},{20... | collective-permute-start | bytes 491528 | tf_op jit(solution)/shard_map/ppermute | solution.py:25
  19.9 7.1 %collective-permute-start.5 = (bf16[40,2048]{1,0:T(8,128)(2,1)S(1)}, bf16[40,2048]{1,0:T(8,128)(2,1)S(1)}, u32[]{:S(2)}, u32[]{:S(2)}) collective-permute-start(bf16[40,2048]{1,0:T(8,128)(2,1)S(1)} %get-tuple-element.43.refs_2_.near), channel_id=1, source_target_pairs={{0,4},{4,0},{8,12},{12,8},{1,5},{5,1},{9,13},{13,9},{2,6},{6,2},{1... | collective-permute-start | bytes 491528 | tf_op jit(solution)/shard_map/ppermute | solution.py:25
  26.5 4.4 %collective-permute-start.6 = (f32[40,1536]{1,0:T(8,128)S(1)}, f32[40,1536]{1,0:T(8,128)S(1)}, u32[]{:S(2)}, u32[]{:S(2)}) collective-permute-start(f32[40,1536]{1,0:T(8,128)S(1)} %get-tuple-element.48), channel_id=1, source_target_pairs={{0,1},{1,0},{2,3},{3,2},{4,5},{5,4},{6,7},{7,6},{8,9},{9,8},{10,11... | collective-permute-start | bytes 737288 | tf_op jit(solution)/shard_map/ppermute | solution.py:25
  26.6 4.3 %collective-permute-start.7 = (f32[40,1536]{1,0:T(8,128)S(1)}, f32[40,1536]{1,0:T(8,128)S(1)}, u32[]{:S(2)}, u32[]{:S(2)}) collective-permute-start(f32[40,1536]{1,0:T(8,128)S(1)} %get-tuple-element.49), channel_id=1, source_target_pairs={{0,1},{1,0},{2,3},{3,2},{4,5},{5,4},{6,7},{7,6},{8,9},{9,8},{10,11... | collective-permute-start | bytes 737288 | tf_op jit(solution)/shard_map/ppermute | solution.py:25
  30.7 1.6 %collective-permute-start.8 = (f32[40,1536]{1,0:T(8,128)S(1)}, f32[40,1536]{1,0:T(8,128)S(1)}, u32[]{:S(2)}, u32[]{:S(2)}) collective-permute-start(f32[40,1536]{1,0:T(8,128)S(1)} %get-tuple-element.50), channel_id=1, source_target_pairs={{0,1},{1,0},{2,3},{3,2},{4,5},{5,4},{6,7},{7,6},{8,9},{9,8},{10,11... | collective-permute-start | bytes 737288 | tf_op jit(solution)/shard_map/ppermute | solution.py:25
  32.4 10.7 %collective-permute-start.13 = (bf16[3,40,1536]{2,1,0:T(8,128)(2,1)S(1)}, bf16[3,40,1536]{2,1,0:T(8,128)(2,1)S(1)}, u32[]{:S(2)}, u32[]{:S(2)}) collective-permute-start(bf16[3,40,1536]{2,1,0:T(8,128)(2,1)S(1)} %get-tuple-element.51.refs_3_.refs_1_), channel_id=1, source_target_pairs={{0,2},{1,3},{2,0},{3,1},{4,6},{5,7},{6,4},{7,5},{8,10},{9,11},{10,... | collective-permute-start | bytes 1105928 | tf_op jit(solution)/shard_map/ppermute | solution.py:25
  37.6 7.5 %slice-start = ((s8[6291456]{0:T(1024)(128)(4,1)}), s8[4194304]{0:T(1024)(128)(4,1)S(1)}, s32[]{:S(2)}) async-start(s8[6291456]{0:T(1024)(128)(4,1)} %bitcast.2), calls=%async_computation | async-start | bytes 8388608
  37.6 3.6 %collective-permute-start.9 = (f32[40,1792]{1,0:T(8,128)S(1)}, f32[40,1792]{1,0:T(8,128)S(1)}, u32[]{:S(2)}, u32[]{:S(2)}) collective-permute-start(f32[40,1792]{1,0:T(8,128)S(1)} %get-tuple-element.56), channel_id=1, source_target_pairs={{0,1},{1,0},{2,3},{3,2},{4,5},{5,4},{6,7},{7,6},{8,9},{9,8},{10,11... | collective-permute-start | bytes 860168 | tf_op jit(solution)/shard_map/ppermute | solution.py:25
  37.7 3.5 %collective-permute-start.10 = (f32[40,1792]{1,0:T(8,128)S(1)}, f32[40,1792]{1,0:T(8,128)S(1)}, u32[]{:S(2)}, u32[]{:S(2)}) collective-permute-start(f32[40,1792]{1,0:T(8,128)S(1)} %get-tuple-element.57), channel_id=1, source_target_pairs={{0,1},{1,0},{2,3},{3,2},{4,5},{5,4},{6,7},{7,6},{8,9},{9,8},{10,11... | collective-permute-start | bytes 860168 | tf_op jit(solution)/shard_map/ppermute | solution.py:25
  38.2 7.0 %slice-start.1 = ((s8[6291456]{0:T(1024)(128)(4,1)}), s8[2097152]{0:T(1024)(128)(4,1)S(1)}, s32[]{:S(2)}) async-start(s8[6291456]{0:T(1024)(128)(4,1)} %bitcast.2), calls=%async_computation.1 | async-start | bytes 4194304
  41.0 1.6 %collective-permute-start.11 = (f32[40,1792]{1,0:T(8,128)S(1)}, f32[40,1792]{1,0:T(8,128)S(1)}, u32[]{:S(2)}, u32[]{:S(2)}) collective-permute-start(f32[40,1792]{1,0:T(8,128)S(1)} %get-tuple-element.58), channel_id=1, source_target_pairs={{0,1},{1,0},{2,3},{3,2},{4,5},{5,4},{6,7},{7,6},{8,9},{9,8},{10,11... | collective-permute-start | bytes 860168 | tf_op jit(solution)/shard_map/ppermute | solution.py:25
  43.3 1.9 %collective-permute-start.14 = (bf16[3,48,1536]{2,1,0:T(8,128)(2,1)S(1)}, bf16[3,48,1536]{2,1,0:T(8,128)(2,1)S(1)}, u32[]{:S(2)}, u32[]{:S(2)}) collective-permute-start(bf16[3,48,1536]{2,1,0:T(8,128)(2,1)S(1)} %activate.2.own), channel_id=1, source_target_pairs={{0,1},{1,0},{2,3},{3,2},{4,5},{5,4},{6,7},{7,6},{8,9},{9,8},{10,11... | collective-permute-start | bytes 1327112 | tf_op jit(solution)/shard_map/ppermute | solution.py:25
  43.3 12.3 %collective-permute-start.12 = (bf16[3,40,1792]{2,1,0:T(8,128)(2,1)S(1)}, bf16[3,40,1792]{2,1,0:T(8,128)(2,1)S(1)}, u32[]{:S(2)}, u32[]{:S(2)}) collective-permute-start(bf16[3,40,1792]{2,1,0:T(8,128)(2,1)S(1)} %get-tuple-element.60.rest_0_), channel_id=1, source_target_pairs={{0,2},{1,3},{2,0},{3,1},{4,6},{5,7},{6,4},{7,5},{8,10},{9,11},{10,... | collective-permute-start | bytes 1290248 | tf_op jit(solution)/shard_map/ppermute | solution.py:25
  55.9 2.0 %collective-permute-start.15 = (bf16[3,48,1792]{2,1,0:T(8,128)(2,1)S(1)}, bf16[3,48,1792]{2,1,0:T(8,128)(2,1)S(1)}, u32[]{:S(2)}, u32[]{:S(2)}) collective-permute-start(bf16[3,48,1792]{2,1,0:T(8,128)(2,1)S(1)} %activate.3.own), channel_id=1, source_target_pairs={{0,1},{1,0},{2,3},{3,2},{4,5},{5,4},{6,7},{7,6},{8,9},{9,8},{10,11... | collective-permute-start | bytes 1548296 | tf_op jit(solution)/shard_map/ppermute | solution.py:25
  61.0 6.3 %collective-permute-start.18 = (bf16[2,40,1024]{2,1,0:T(8,128)(2,1)S(1)}, bf16[2,40,1024]{2,1,0:T(8,128)(2,1)S(1)}, u32[]{:S(2)}, u32[]{:S(2)}) collective-permute-start(bf16[2,40,1024]{2,1,0:T(8,128)(2,1)S(1)} %get-tuple-element.68), channel_id=1, source_target_pairs={{0,16},{16,0},{1,17},{17,1},{2,18},{18,2},{3,19},{19,3},{4,20},{20... | collective-permute-start | bytes 491528 | tf_op jit(solution)/shard_map/ppermute | solution.py:25
  65.9 6.0 %collective-permute-start.16 = (bf16[2,40,1024]{2,1,0:T(8,128)(2,1)S(1)}, bf16[2,40,1024]{2,1,0:T(8,128)(2,1)S(1)}, u32[]{:S(2)}, u32[]{:S(2)}) collective-permute-start(bf16[2,40,1024]{2,1,0:T(8,128)(2,1)S(1)} %get-tuple-element.63), channel_id=1, source_target_pairs={{0,16},{16,0},{1,17},{17,1},{2,18},{18,2},{3,19},{19,3},{4,20},{20... | collective-permute-start | bytes 491528 | tf_op jit(solution)/shard_map/ppermute | solution.py:25
  67.4 5.2 %collective-permute-start.19 = (bf16[2,20,1024]{2,1,0:T(8,128)(2,1)S(1)}, bf16[2,20,1024]{2,1,0:T(8,128)(2,1)S(1)}, u32[]{:S(2)}, u32[]{:S(2)}) collective-permute-start(bf16[2,20,1024]{2,1,0:T(8,128)(2,1)S(1)} %get-tuple-element.70), channel_id=1, source_target_pairs={{0,4},{4,0},{8,12},{12,8},{1,5},{5,1},{9,13},{13,9},{2,6},{6,2},{1... | collective-permute-start | bytes 245768 | tf_op jit(solution)/shard_map/ppermute | solution.py:25
  71.9 4.8 %collective-permute-start.17 = (bf16[2,20,1024]{2,1,0:T(8,128)(2,1)S(1)}, bf16[2,20,1024]{2,1,0:T(8,128)(2,1)S(1)}, u32[]{:S(2)}, u32[]{:S(2)}) collective-permute-start(bf16[2,20,1024]{2,1,0:T(8,128)(2,1)S(1)} %get-tuple-element.65), channel_id=1, source_target_pairs={{0,4},{4,0},{8,12},{12,8},{1,5},{5,1},{9,13},{13,9},{2,6},{6,2},{1... | collective-permute-start | bytes 245768 | tf_op jit(solution)/shard_map/ppermute | solution.py:25
  72.7 5.5 %collective-permute-start.21 = (bf16[2,10,1024]{2,1,0:T(8,128)(2,1)S(1)}, bf16[2,10,1024]{2,1,0:T(8,128)(2,1)S(1)}, u32[]{:S(2)}, u32[]{:S(2)}) collective-permute-start(bf16[2,10,1024]{2,1,0:T(8,128)(2,1)S(1)} %get-tuple-element.73), channel_id=1, source_target_pairs={{0,8},{4,12},{8,0},{12,4},{1,9},{5,13},{9,1},{13,5},{2,10},{6,14},... | collective-permute-start | bytes 122888 | tf_op jit(solution)/shard_map/ppermute | solution.py:25
  76.8 5.9 %collective-permute-start.20 = (bf16[2,10,1024]{2,1,0:T(8,128)(2,1)S(1)}, bf16[2,10,1024]{2,1,0:T(8,128)(2,1)S(1)}, u32[]{:S(2)}, u32[]{:S(2)}) collective-permute-start(bf16[2,10,1024]{2,1,0:T(8,128)(2,1)S(1)} %get-tuple-element.72), channel_id=1, source_target_pairs={{0,8},{4,12},{8,0},{12,4},{1,9},{5,13},{9,1},{13,5},{2,10},{6,14},... | collective-permute-start | bytes 122888 | tf_op jit(solution)/shard_map/ppermute | solution.py:25
  (3 other events, 12.3 us)

commit v5 on v4

--- a/solution.py
+++ b/solution.py
@@ -13,8 +13,12 @@
 MIB = 2**20
 WINDOWS = [["g0"], ["u0", "g1"], ["d0"]]
 BESIDE = {"b0": ["u1"], "gu0": [], "gu1": ["d1"], "b1": []}
-FIRST = 0.5
-PIECE = 0.5
+FIRST = 0.62
+EST = 1
+PARTS = [1, 1]
+ORDER = 0
+SPLITS = [0.5]
+SENDS = [1, 2]
 VMEM = pl.BlockSpec(memory_space=pltpu.VMEM)
 SMEM = pl.BlockSpec(memory_space=pltpu.SMEM)
 HBM = pl.BlockSpec(memory_space=pltpu.HBM)
@@ -124,7 +128,7 @@
     return place // (count // 2), place % (count // 2)
 
 
-def up(where, near, far, order, weights, transposed, block, wanted=(), after=()):
+def up(where, near, far, order, weights, transposed, block, cuts, wanted=(), after=()):
     half, feats = near.shape
     count = 2 ** len(order)
     rows = 2 * half // count
@@ -137,7 +141,7 @@
         ws = [refs.pop(0) for _ in range(n)]
         srcs = [refs.pop(0) for _ in range(m)]
         del refs[: len(after)]
-        outs = [refs.pop(0) for _ in range(2 * n)]
+        outs = [[refs.pop(0) for _ in range(len(cuts))] for _ in range(n)]
         dsts = [refs.pop(0) for _ in range(m)]
         wide, lhs = refs[:2]
         made = copies(where, specs, srcs, dsts, refs[2]) if m else []
@@ -160,8 +164,8 @@
                     value = lax.dot_general(lhs[...], w[cut, :], NT, preferred_element_type=F32)
                 else:
                     value = jnp.dot(lhs[...], w[:, cut], preferred_element_type=F32)
-                outs[2 * i][:, cut] = value[:half]
-                outs[2 * i + 1][:, cut] = value[half:]
+                for out, (start, size) in zip(outs[i], cuts):
+                    out[:, cut] = value[start : start + size]
 
         if made:
             block2 = width // 2 if width % 256 == 0 else width
@@ -176,37 +180,45 @@
         for copy in made:
             copy.wait()
 
-    out = jax.ShapeDtypeStruct((half, width), F32)
+    shapes = [jax.ShapeDtypeStruct((size, width), F32) for _, size in cuts] * n
     got = call(
         kernel,
         "up",
         [SMEM] + [VMEM] * (2 + n) + [HBM] * m + [ANY] * len(after),
-        [out] * (2 * n) + [fetched(w, s) for w, s in wanted],
+        shapes + [fetched(w, s) for w, s in wanted],
         [pltpu.VMEM((2 * half, feats), F32), pltpu.VMEM((2 * half, feats), BF16)]
         + ([pltpu.SemaphoreType.DMA((m,))] if m else []),
         limit=2,
         estimate=cost(2 * n * 256 * feats * width, 2 * n * feats * width),
     )(where, near, far, *[resident(w) for w in weights], *[in_hbm(w) for w, _ in wanted], *after)
-    return got[: 2 * n : 2], got[1 : 2 * n : 2], got[2 * n :]
-
-
-def gather(keeps, gots):
-    n = len(keeps)
-    shape = (n,) + keeps[0].shape
+    k = len(cuts)
+    return [got[i * k : (i + 1) * k] for i in range(n)], got[n * k :]
+
+
+def gather(keeps, gots, cuts):
+    n, m = len(keeps), len(gots[0])
+    rows = keeps[0].shape[0]
 
     def kernel(*refs):
-        total, rounded = refs[-2:]
-        for i in range(n):
-            value = refs[i][...] + refs[n + i][...]
-            total[i] = value
-            rounded[i] = value.astype(BF16)
-
-    return call(
+        outs = refs[n + n * m :]
+        for k, (start, width) in enumerate(cuts):
+            at = slice(start, start + width)
+            for i in range(n):
+                top = 0
+                for got in refs[n + i * m : n + (i + 1) * m]:
+                    run = slice(top, top + got.shape[0])
+                    value = refs[i][run, at] + got[:, at]
+                    outs[2 * k][i, run] = value
+                    outs[2 * k + 1][i, run] = value.astype(BF16)
+                    top += got.shape[0]
+
+    outs = call(
         kernel,
         "gather",
-        [VMEM] * (2 * n),
-        [jax.ShapeDtypeStruct(shape, F32), jax.ShapeDtypeStruct(shape, BF16)],
-    )(*keeps, *gots)
+        [VMEM] * (n + n * m),
+        [jax.ShapeDtypeStruct((n, rows, w), t) for _, w in cuts for t in (F32, BF16)],
+    )(*keeps, *[v for got in gots for v in got])
+    return list(zip(outs[::2], outs[1::2]))
 
 
 def add(a, b):
@@ -227,7 +239,7 @@
     _, half, width = sums.shape
 
     def kernel(sums, got, *rest):
-        out = rest[-1]
+        outs = rest[-3:]
         gate = sums[0] + got[0].astype(F32)
         upward = sums[1] + got[1].astype(F32)
         back = sums[2] + got[2].astype(F32)
@@ -235,39 +247,42 @@
         hidden = gate * sigma * upward
         d_up = back * gate * sigma
         d_gate = back * upward * sigma * (1.0 + gate * (1.0 - sigma))
-        for i, value in enumerate((hidden, d_gate, d_up)):
+        for out, value in zip(outs, (hidden, d_gate, d_up)):
             if padded > half:
                 empty = jnp.zeros((padded - half, width), F32)
                 value = jnp.concatenate([value, empty], axis=0)
-            out[i] = value.astype(BF16)
+            out[...] = value.astype(BF16)
 
     return call(
         kernel,
         "activate",
         [VMEM] * 2 + [ANY] * len(after),
-        jax.ShapeDtypeStruct((3, padded, width), BF16),
+        [jax.ShapeDtypeStruct((padded, width), BF16)] * 3,
         limit=2,
     )(sums, got, *after)
 
 
-def down(where, own, other, weights, prev, half, part, last):
-    _, padded, width = own.shape
+def down(where, own, other, weights, units, prev, half, part, last):
+    padded, width = own[0].shape
     start, feats = part
+    units = slice(units[0], units[0] + units[1])
     block = 256 if feats % 256 == 0 else 128
 
-    def kernel(where, own, other, gate_w, up_w, down_w, *rest):
+    def kernel(where, *rest):
+        own, other, (gate_w, up_w, down_w), rest = rest[:3], rest[3:6], rest[6:9], rest[9:]
         lhs = rest[-1]
         outs = rest[len(prev) : -1]
         first = where[1] == 0
-        lhs[:, :padded, :] = own[...]
-        lhs[:, padded:, :] = other[...]
+        for i in range(3):
+            lhs[i, :padded, :] = own[i][...]
+            lhs[i, padded:, :] = other[i][...]
 
         for step in range(feats // block):
             cut = slice(step * block, (step + 1) * block)
             full = slice(start + step * block, start + (step + 1) * block)
-            mixed = jnp.dot(lhs[0], down_w[:, full], preferred_element_type=F32)
-            grad = lax.dot_general(lhs[1], gate_w[full, :], NT, preferred_element_type=F32)
-            grad += lax.dot_general(lhs[2], up_w[full, :], NT, preferred_element_type=F32)
+            mixed = jnp.dot(lhs[0], down_w[units, full], preferred_element_type=F32)
+            grad = lax.dot_general(lhs[1], gate_w[full, units], NT, preferred_element_type=F32)
+            grad += lax.dot_general(lhs[2], up_w[full, units], NT, preferred_element_type=F32)
             for i, value in enumerate((mixed, grad)):
                 if prev:
                     value += prev_ref(rest)[i, :, full]
@@ -291,19 +306,20 @@
     return call(
         kernel,
         "down",
-        [SMEM] + [VMEM] * (5 + len(prev)),
+        [SMEM] + [VMEM] * (9 + len(prev)),
         shapes,
         [pltpu.VMEM((3, 2 * padded, width), BF16)],
         limit=2,
-        estimate=cost(6 * 256 * feats * width, 6 * feats * width),
-    )(where, own, other, *[resident(w) for w in weights], *prev)
-
-
-def fold(keep, got):
+        estimate=cost(6 * 256 * feats * width, 6 * feats * width) if last else cost(EST, EST),
+    )(where, *own, *other, *[resident(w) for w in weights], *prev)
+
+
+def fold(keep, got, after):
     _, n, feats = keep.shape
     half = n // 2
 
-    def kernel(keep, got, stay, send):
+    def kernel(keep, got, *rest):
+        stay, send = rest[-2:]
         for i in range(2):
             value = keep[i] + got[i].astype(F32)
             stay[i] = value[:half]
@@ -312,9 +328,9 @@
     return call(
         kernel,
         "fold",
-        [VMEM] * 2,
+        [VMEM] * 2 + [ANY] * len(after),
         [jax.ShapeDtypeStruct((2, half, feats), F32), jax.ShapeDtypeStruct((2, half, feats), BF16)],
-    )(keep, got)
+    )(keep, got, *after)
 
 
 def finish(keeps, gots):
@@ -347,8 +363,8 @@
     blocks = whole // block
     cuts = [0, int(blocks * FIRST), blocks] if blocks > 1 else [0, blocks]
     chunks = [(a * block, (b - a) * block) for a, b in zip(cuts, cuts[1:])]
-    lead = int(feats * PIECE) // 256 * 256
-    pieces = [(0, lead), (lead, feats - lead)] if lead else [(0, feats)]
+    ends = [0, *[int(feats * v) // 256 * 256 for v in SPLITS], feats]
+    pieces = [(a, b - a) for a, b in zip(ends, ends[1:]) if b > a]
 
     core = lax.axis_index("bulk") % 2
     group = lax.axis_index("grp") if split else jnp.int32(0)
@@ -370,7 +386,7 @@
         return [n for n, _ in found], [w for _, w in found]
 
     n = len(hops)
-    orders = (list(range(n)), [n - 1, *range(n - 1)])
+    orders = (list(range(n)), [[n - 1, *range(n - 1)], [0, n - 1, *range(1, n - 1)]][ORDER])
     near, far = [tokens, cotangent], [None, None]
     after = []
     for step in range(n):
@@ -388,33 +404,42 @@
     after = ()
     for c in range(len(chunks)):
         out = {}
+        top = -(-half // 32) * 16 if SENDS[c] == 2 else half
+        runs = [(0, half), (half, top)] + ([(half + top, half - top)] if top < half else [])
         for kind, i in (("gu", 0), ("b", 1)) if c else (("b", 1), ("gu", 0)):
             ws = [here[f"{w}{c}"] for w in ("d" if kind == "b" else "gu")]
             names, parts = wanted(BESIDE[f"{kind}{c}"])
-            *out[kind], got = up(
-                where, near[i], far[i], orders[i], ws, kind == "b", block, parts, after
+            out[kind], got = up(
+                where, near[i], far[i], orders[i], ws, kind == "b", block, runs, parts, after
             )
             here.update(zip(names, got))
-        keep, send = ([*out["gu"][i], *out["b"][i]] for i in range(2))
-        sums, rounded = gather(keep, [swap(v, "bulk", bulk, 1) for v in send])
-        after = (rounded,)
-        summed.append((sums, rounded))
+        out = out["gu"] + out["b"]
+        size = chunks[c][1]
+        parts = PARTS[c] if size % (128 * PARTS[c]) == 0 else 1
+        cuts = [(i * size // parts, size // parts) for i in range(parts)]
+        sums = gather(
+            [v[0] for v in out], [[swap(r, "bulk", bulk, 1) for r in v[1:]] for v in out], cuts
+        )
+        after = tuple(rounded for _, rounded in sums)
+        summed += [(c, cut, *pair) for cut, pair in zip(cuts, sums)]
 
     prev = ()
-    for c, (sums, rounded) in enumerate(summed):
+    for step, (c, cut, sums, rounded) in enumerate(summed):
         for b in bits(bulk, 2)[:-1]:
             sums, rounded = add(sums, swap(rounded, "bulk", bulk, b))
         got = swap(rounded, "bulk", bulk, bits(bulk, 2)[-1])
         w = [here[f"{name}{c}"] for name in "gud"]
-        own = activate(sums, got, padded, (*prev, *[r for _, r in summed[c + 1 :]]))
-        other = swap(own, "bulk", bulk, 1)
-        if c < len(chunks) - 1:
-            prev = down(where, own, other, w, prev, half, (0, feats), False)
+        own = activate(sums, got, padded, (*prev, *[v[-1] for v in summed[step + 1 :]]))
+        other = [swap(v, "bulk", bulk, 1) for v in own]
+        if step < len(summed) - 1:
+            prev = down(where, own, other, w, cut, prev, half, (0, feats), False)
+    made = [down(where, own, other, w, cut, prev, half, part, True) for part in pieces]
     stays, gots = [], []
-    for part in pieces:
-        stay, send = down(where, own, other, w, prev, half, part, True)
+    for p, (stay, send) in enumerate(made):
+        late = made[p + 1][1:] if p + 1 < len(made) else ()
         for hop in reversed(hops[1:]):
-            stay, send = fold(stay, swap(send, *hop))
+            stay, send = fold(stay, swap(send, *hop), late)
+            late = ()
         stays.append(stay)
         gots.append(swap(send, *hops[0]))
     return tuple(finish(stays, gots))

time: 83.7 us -> 81.8 us (0.977)
  waiting for transfers between devices: 21.5 us -> 15.7 us
  starting transfers between devices: 22.5 us -> 25.4 us
  Pallas kernels: 38.5 us -> 39.6 us
    ppermute x22 -> x29, waiting for transfers between devices: 21.5 us -> 15.7 us  [swap(): return lax.ppermute(value, axis, [(i, i ^ bit) for i in range(size)])]
    ppermute x22 -> x29, starting transfers between devices: 22.5 us -> 25.4 us  [swap(): return lax.ppermute(value, axis, [(i, i ^ bit) for i in range(size)])]
    pallas_call x3, Pallas kernels: 12.2 us -> 13.5 us  [fetch(): call(kernel, 'fetch', [SMEM] + [HBM] * n + [ANY] * len(after), outs, [plt...]
  transfers between devices with their start and end apart: 22 -> 29, of which waited for: 11 -> 18; matrix products, arithmetic and copies ran while one was open for 0% -> 0% of each run, Pallas kernels for 41% -> 44%
where the time goes in v5:
time: 81.8 us; the launch traced here: 81.6 us
  Pallas kernels  39.6 us (48%)
  starting transfers between devices  25.4 us (31%)
  waiting for transfers between devices  15.7 us (19%)
  between operations  0.82 us (1%)
    ppermute x29, starting transfers between devices, swap(): return lax.ppermute(value, axis, [(i, i ^ bit) for i in range(size)])  25.4 us
    ppermute x29, waiting for transfers between devices, swap(): return lax.ppermute(value, axis, [(i, i ^ bit) for i in range(size)])  15.7 us
    pallas_call x3, Pallas kernels, fetch(): call(kernel, 'fetch', [SMEM] + [HBM] * n + [ANY] * len(after), outs, [plt...  13.5 us
    pallas_call x4, Pallas kernels, up(): call(kernel, 'up', [SMEM] + [VMEM] * (2 + n) + [HBM] * m + [ANY] * len(af...  12.5 us
    pallas_call x3, Pallas kernels, down(): call(kernel, 'down', [SMEM] + [VMEM] * (9 + len(prev)), shapes, [pltpu.VM...  12.1 us
  transfers between devices with their start and end apart: 29, of which 18 were waited for; matrix products, arithmetic and copies ran while one was open for 0% of the time, Pallas kernels for 44%

profile of v5, /device:TPU:0, one launch (start us, length us, event | category | flops | bytes accessed | tf_op | source)
XLA Modules:
  0.0 81.6 jit_solution(2707360035114874402)
XLA Ops:
  0.6 4.1 %collective-permute-start = (bf16[10,2048]{1,0:T(8,128)(2,1)}, bf16[10,2048]{1,0:T(8,128)(2,1)S(1)}, u32[]{:S(2)}, u32[]{:S(2)}) collective-permute-start(bf16[10,2048]{1,0:T(8,128)(2,1)} %refs_0_.5), channel_id=1, source_target_pairs={{0,8},{4,12},{8,0},{12,4},{1,9},{5,13},{9,1},{13,5},{2,10},{6,14},... | collective-permute-start | bytes 122888 | tf_op jit(solution)/shard_map/ppermute | solution.py:29
  4.7 1.5 %collective-permute-start.1 = (bf16[10,2048]{1,0:T(8,128)(2,1)}, bf16[10,2048]{1,0:T(8,128)(2,1)S(1)}, u32[]{:S(2)}, u32[]{:S(2)}) collective-permute-start(bf16[10,2048]{1,0:T(8,128)(2,1)} %refs_1_.3), channel_id=1, source_target_pairs={{0,16},{16,0},{1,17},{17,1},{2,18},{18,2},{3,19},{19,3},{4,20},{20... | collective-permute-start | bytes 122888 | tf_op jit(solution)/shard_map/ppermute | solution.py:29
  6.3 3.9 %fetch.3.refs_4_.refs_0_.rest_6_ = bf16[2048,2048]{1,0:T(8,128)(2,1)S(1)} custom-call(s32[2]{0:T(128)S(1)} %pad_add_fusion.where, bf16[2048,6656]{1,0:T(8,128)(2,1)} %refs_1_.4), custom_call_target="tpu_custom_call" | custom-call | bytes 8388608 | tf_op jit(solution)/shard_map/fetch/pallas_call | solution.py:93
  10.4 1.6 %collective-permute-start.2 = (bf16[20,2048]{1,0:T(8,128)(2,1)S(1)}, bf16[20,2048]{1,0:T(8,128)(2,1)S(1)}, u32[]{:S(2)}, u32[]{:S(2)}) collective-permute-start(bf16[20,2048]{1,0:T(8,128)(2,1)S(1)} %get-tuple-element.47.refs_2_.refs_0_), channel_id=1, source_target_pairs={{0,4},{4,0},{8,12},{12,8},{1,5},{5,1},{9,13},{13,9},{2,6},{6,2},{1... | collective-permute-start | bytes 245768 | tf_op jit(solution)/shard_map/ppermute | solution.py:29
  12.7 5.6 %fetch.4 = (bf16[2048,2048]{1,0:T(8,128)(2,1)S(1)}, bf16[2048,1280]{1,0:T(8,128)(2,1)S(1)}) custom-call(s32[2]{0:T(128)S(1)} %pad_add_fusion.where, bf16[2048,6656]{1,0:T(8,128)(2,1)} %refs_1_.5, bf16[2048,6656]{1,0:T(8,128)(2,1)} %refs_1_.4, bf16[20,2048]{1,0:T(8,128)(2,1)S(1)} %get-tuple-element.47.refs_2_.refs_0_, ...), custom_call_target="tpu_custom_call" | custom-call | bytes 13631488 | tf_op jit(solution)/shard_map/fetch/pallas_call | solution.py:93
  18.7 1.2 %collective-permute-start.4 = (bf16[40,2048]{1,0:T(8,128)(2,1)S(1)}, bf16[40,2048]{1,0:T(8,128)(2,1)S(1)}, u32[]{:S(2)}, u32[]{:S(2)}) collective-permute-start(bf16[40,2048]{1,0:T(8,128)(2,1)S(1)} %get-tuple-element.51.refs_1_.near), channel_id=1, source_target_pairs={{0,16},{16,0},{1,17},{17,1},{2,18},{18,2},{3,19},{19,3},{4,20},{20... | collective-permute-start | bytes 491528 | tf_op jit(solution)/shard_map/ppermute | solution.py:29
  20.0 3.9 %fetch.5.refs_0_.rest_8_ = bf16[2048,2048]{1,0:T(8,128)(2,1)S(1)} custom-call(s32[2]{0:T(128)S(1)} %pad_add_fusion.where, bf16[6656,2048]{1,0:T(8,128)(2,1)} %refs_2_.1, bf16[40,2048]{1,0:T(8,128)(2,1)S(1)} %get-tuple-element.51.refs_1_.near, bf16[40,2048]{1,0:T(8,128)(2,1)S(1)} %get-tuple-element.52.refs_2_.near), custom_call_target="tpu_custom_call" | custom-call | bytes 8388608 | tf_op jit(solution)/shard_map/fetch/pallas_call | solution.py:93
  24.1 3.6 %up.5 = (f32[40,2048]{1,0:T(8,128)S(1)}, f32[40,2048]{1,0:T(8,128)S(1)}, f32[40,2048]{1,0:T(8,128)S(1)}, f32[40,2048]{1,0:T(8,128)S(1)}) custom-call(s32[2]{0:T(128)S(1)} %pad_add_fusion.where, bf16[40,2048]{1,0:T(8,128)(2,1)S(1)} %get-tuple-element.51.refs_1_.near, bf16[40,2048]{1,0:T(8,128)(2,1)S(1)} %collective-permute-done.4.far, ...), custom_call_target="tpu_custom_call" | custom-call | flops 4294967296 | bytes 16777216 | tf_op jit(solution)/shard_map/up/pallas_call | solution.py:184
  28.3 3.6 %up.4 = (f32[40,2048]{1,0:T(8,128)S(1)}, f32[40,2048]{1,0:T(8,128)S(1)}, bf16[2048,1280]{1,0:T(8,128)(2,1)S(1)}) custom-call(s32[2]{0:T(128)S(1)} %pad_add_fusion.where, bf16[40,2048]{1,0:T(8,128)(2,1)S(1)} %get-tuple-element.52.refs_2_.near, bf16[40,2048]{1,0:T(8,128)(2,1)S(1)} %collective-permute-done.5.far, bf16[2048,2048]{1,0:T(8,128)(2,1)S(1)} %fetch.5.refs_0_.rest_8_, ...), custom_call_target="tpu_custom_call" | custom-call | flops 2147483648 | bytes 8388608 | tf_op jit(solution)/shard_map/up/pallas_call | solution.py:184
  32.0 1.5 %collective-permute-done.8.refs_5_ = f32[40,2048]{1,0:T(8,128)S(1)} collective-permute-done((f32[40,2048]{1,0:T(8,128)S(1)}, f32[40,2048]{1,0:T(8,128)S(1)}, u32[]{:S(2)}, u32[]{:S(2)}) %collective-permute-start.8) | collective-permute-done | bytes 327712 | tf_op jit(solution)/shard_map/ppermute | solution.py:29
  33.7 1.6 %collective-permute-start.16 = (bf16[3,40,2048]{2,1,0:T(8,128)(2,1)S(1)}, bf16[3,40,2048]{2,1,0:T(8,128)(2,1)S(1)}, u32[]{:S(2)}, u32[]{:S(2)}) collective-permute-start(bf16[3,40,2048]{2,1,0:T(8,128)(2,1)S(1)} %get-tuple-element.60.refs_3_.refs_1_), channel_id=1, source_target_pairs={{0,2},{1,3},{2,0},{3,1},{4,6},{5,7},{6,4},{7,5},{8,10},{9,11},{10,... | collective-permute-start | bytes 1474568 | tf_op jit(solution)/shard_map/ppermute | solution.py:29
  35.2 3.0 %up.6 = (f32[40,1280]{1,0:T(8,128)S(1)}, f32[32,1280]{1,0:T(8,128)S(1)}, f32[8,1280]{1,0:T(8,128)S(1)}, f32[40,1280]{1,0:T(8,128)S(1)}, f32[32,1280]{1,0:T(8,128...) custom-call(s32[2]{0:T(128)S(1)} %pad_add_fusion.where, ...), custom_call_target="tpu_custom_call" | custom-call | flops 2684354560 | bytes 10485760 | tf_op jit(solution)/shard_map/up/pallas_call | solution.py:184
  38.8 2.3 %up.7 = (f32[40,1280]{1,0:T(8,128)S(1)}, f32[32,1280]{1,0:T(8,128)S(1)}, f32[8,1280]{1,0:T(8,128)S(1)}) custom-call(s32[2]{0:T(128)S(1)} %pad_add_fusion.where, bf16[40,2048]{1,0:T(8,128)(2,1)S(1)} %get-tuple-element.52.refs_2_.near, bf16[40,2048]{1,0:T(8,128)(2,1)S(1)} %collective-permute-done.5.far, ...), custom_call_target="tpu_custom_call" | custom-call | flops 1342177280 | bytes 5242880 | tf_op jit(solution)/shard_map/up/pallas_call | solution.py:184
  49.3 7.1 %down.3.rest_0_.rest_9_ = f32[2,96,2048]{2,1,0:T(8,128)S(1)} custom-call(s32[2]{0:T(128)S(1)} %pad_add_fusion.where, bf16[48,2048]{1,0:T(8,128)(2,1)S(1)} %get-tuple-element.74.rest_0_, bf16[48,2048]{1,0:T(8,128)(2,1)S(1)} %get-tuple-element.75.rest_1_, bf16[48,2048]{1,0:T(8,128)(2,1)S(1)} %get-tuple-element.76.rest_2_, ...), custom_call_target="tpu_custom_call" | custom-call | flops 1 | bytes 1 | tf_op jit(solution)/shard_map/down/pallas_call | solution.py:306
  58.5 2.5 %down.4 = (f32[2,40,1024]{2,1,0:T(8,128)S(1)}, bf16[2,40,1024]{2,1,0:T(8,128)(2,1)S(1)}) custom-call(s32[2]{0:T(128)S(1)} %pad_add_fusion.where, bf16[48,1280]{1,0:T(8,128)(2,1)S(1)} %get-tuple-element.77.rest_0_, bf16[48,1280]{1,0:T(8,128)(2,1)S(1)} %get-tuple-element.78.rest_1_, bf16[48,1280]{1,0:T(8,128)(2,1)S(1)} %get-tuple-element.79.rest_2_, ...), custom_call_target="tpu_custom_call" | custom-call | flops 2013265920 | bytes 7864320 | tf_op jit(solution)/shard_map/down/pallas_call | solution.py:306
  61.0 1.2 %collective-permute-start.23 = (bf16[2,40,1024]{2,1,0:T(8,128)(2,1)S(1)}, bf16[2,40,1024]{2,1,0:T(8,128)(2,1)S(1)}, u32[]{:S(2)}, u32[]{:S(2)}) collective-permute-start(bf16[2,40,1024]{2,1,0:T(8,128)(2,1)S(1)} %get-tuple-element.81), channel_id=1, source_target_pairs={{0,16},{16,0},{1,17},{17,1},{2,18},{18,2},{3,19},{19,3},{4,20},{20... | collective-permute-start | bytes 491528 | tf_op jit(solution)/shard_map/ppermute | solution.py:29
  62.2 2.5 %down.5 = (f32[2,40,1024]{2,1,0:T(8,128)S(1)}, bf16[2,40,1024]{2,1,0:T(8,128)(2,1)S(1)}) custom-call(s32[2]{0:T(128)S(1)} %pad_add_fusion.where, bf16[48,1280]{1,0:T(8,128)(2,1)S(1)} %get-tuple-element.77.rest_0_, bf16[48,1280]{1,0:T(8,128)(2,1)S(1)} %get-tuple-element.78.rest_1_, bf16[48,1280]{1,0:T(8,128)(2,1)S(1)} %get-tuple-element.79.rest_2_, ...), custom_call_target="tpu_custom_call" | custom-call | flops 2013265920 | bytes 7864320 | tf_op jit(solution)/shard_map/down/pallas_call | solution.py:306
  65.6 1.7 %collective-permute-done.23.got = bf16[2,40,1024]{2,1,0:T(8,128)(2,1)S(1)} collective-permute-done((bf16[2,40,1024]{2,1,0:T(8,128)(2,1)S(1)}, bf16[2,40,1024]{2,1,0:T(8,128)(2,1)S(1)}, u32[]{:S(2)}, u32[]{:S(2)}) %collective-permute-start.23) | collective-permute-done | bytes 163872 | tf_op jit(solution)/shard_map/ppermute | solution.py:29
  67.4 2.2 %collective-permute-start.24 = (bf16[2,20,1024]{2,1,0:T(8,128)(2,1)S(1)}, bf16[2,20,1024]{2,1,0:T(8,128)(2,1)S(1)}, u32[]{:S(2)}, u32[]{:S(2)}) collective-permute-start(bf16[2,20,1024]{2,1,0:T(8,128)(2,1)S(1)} %get-tuple-element.84), channel_id=1, source_target_pairs={{0,4},{4,0},{8,12},{12,8},{1,5},{5,1},{9,13},{13,9},{2,6},{6,2},{1... | collective-permute-start | bytes 245768 | tf_op jit(solution)/shard_map/ppermute | solution.py:29
  69.7 1.2 %collective-permute-done.25.got = bf16[2,40,1024]{2,1,0:T(8,128)(2,1)S(1)} collective-permute-done((bf16[2,40,1024]{2,1,0:T(8,128)(2,1)S(1)}, bf16[2,40,1024]{2,1,0:T(8,128)(2,1)S(1)}, u32[]{:S(2)}, u32[]{:S(2)}) %collective-permute-start.25) | collective-permute-done | bytes 163872 | tf_op jit(solution)/shard_map/ppermute | solution.py:29
  71.0 1.9 %collective-permute-start.26 = (bf16[2,20,1024]{2,1,0:T(8,128)(2,1)S(1)}, bf16[2,20,1024]{2,1,0:T(8,128)(2,1)S(1)}, u32[]{:S(2)}, u32[]{:S(2)}) collective-permute-start(bf16[2,20,1024]{2,1,0:T(8,128)(2,1)S(1)} %get-tuple-element.88), channel_id=1, source_target_pairs={{0,4},{4,0},{8,12},{12,8},{1,5},{5,1},{9,13},{13,9},{2,6},{6,2},{1... | collective-permute-start | bytes 245768 | tf_op jit(solution)/shard_map/ppermute | solution.py:29
  72.9 1.6 %collective-permute-start.27 = (bf16[2,10,1024]{2,1,0:T(8,128)(2,1)S(1)}, bf16[2,10,1024]{2,1,0:T(8,128)(2,1)S(1)}, u32[]{:S(2)}, u32[]{:S(2)}) collective-permute-start(bf16[2,10,1024]{2,1,0:T(8,128)(2,1)S(1)} %get-tuple-element.90), channel_id=1, source_target_pairs={{0,8},{4,12},{8,0},{12,4},{1,9},{5,13},{9,1},{13,5},{2,10},{6,14},... | collective-permute-start | bytes 122888 | tf_op jit(solution)/shard_map/ppermute | solution.py:29
  75.7 2.3 %collective-permute-start.28 = (bf16[2,10,1024]{2,1,0:T(8,128)(2,1)S(1)}, bf16[2,10,1024]{2,1,0:T(8,128)(2,1)S(1)}, u32[]{:S(2)}, u32[]{:S(2)}) collective-permute-start(bf16[2,10,1024]{2,1,0:T(8,128)(2,1)S(1)} %get-tuple-element.91), channel_id=1, source_target_pairs={{0,8},{4,12},{8,0},{12,4},{1,9},{5,13},{9,1},{13,5},{2,10},{6,14},... | collective-permute-start | bytes 122888 | tf_op jit(solution)/shard_map/ppermute | solution.py:29
  78.0 2.1 %collective-permute-done.27.refs_2_ = bf16[2,10,1024]{2,1,0:T(8,128)(2,1)S(1)} collective-permute-done((bf16[2,10,1024]{2,1,0:T(8,128)(2,1)S(1)}, bf16[2,10,1024]{2,1,0:T(8,128)(2,1)S(1)}, u32[]{:S(2)}, u32[]{:S(2)}) %collective-permute-start.27) | collective-permute-done | bytes 40992 | tf_op jit(solution)/shard_map/ppermute | solution.py:29
  (60 shorter events, 16.9 us)
Async XLA Ops:
  0.6 9.6 %collective-permute-start = (bf16[10,2048]{1,0:T(8,128)(2,1)}, bf16[10,2048]{1,0:T(8,128)(2,1)S(1)}, u32[]{:S(2)}, u32[]{:S(2)}) collective-permute-start(bf16[10,2048]{1,0:T(8,128)(2,1)} %refs_0_.5), channel_id=1, source_target_pairs={{0,8},{4,12},{8,0},{12,4},{1,9},{5,13},{9,1},{13,5},{2,10},{6,14},... | collective-permute-start | bytes 122888 | tf_op jit(solution)/shard_map/ppermute | solution.py:29
  4.7 5.6 %collective-permute-start.1 = (bf16[10,2048]{1,0:T(8,128)(2,1)}, bf16[10,2048]{1,0:T(8,128)(2,1)S(1)}, u32[]{:S(2)}, u32[]{:S(2)}) collective-permute-start(bf16[10,2048]{1,0:T(8,128)(2,1)} %refs_1_.3), channel_id=1, source_target_pairs={{0,16},{16,0},{1,17},{17,1},{2,18},{18,2},{3,19},{19,3},{4,20},{20... | collective-permute-start | bytes 122888 | tf_op jit(solution)/shard_map/ppermute | solution.py:29
  10.4 7.9 %collective-permute-start.2 = (bf16[20,2048]{1,0:T(8,128)(2,1)S(1)}, bf16[20,2048]{1,0:T(8,128)(2,1)S(1)}, u32[]{:S(2)}, u32[]{:S(2)}) collective-permute-start(bf16[20,2048]{1,0:T(8,128)(2,1)S(1)} %get-tuple-element.47.refs_2_.refs_0_), channel_id=1, source_target_pairs={{0,4},{4,0},{8,12},{12,8},{1,5},{5,1},{9,13},{13,9},{2,6},{6,2},{1... | collective-permute-start | bytes 245768 | tf_op jit(solution)/shard_map/ppermute | solution.py:29
  12.0 6.6 %collective-permute-start.3 = (bf16[20,2048]{1,0:T(8,128)(2,1)S(1)}, bf16[20,2048]{1,0:T(8,128)(2,1)S(1)}, u32[]{:S(2)}, u32[]{:S(2)}) collective-permute-start(bf16[20,2048]{1,0:T(8,128)(2,1)S(1)} %get-tuple-element.48.refs_3_.refs_1_), channel_id=1, source_target_pairs={{0,8},{4,12},{8,0},{12,4},{1,9},{5,13},{9,1},{13,5},{2,10},{6,14},... | collective-permute-start | bytes 245768 | tf_op jit(solution)/shard_map/ppermute | solution.py:29
  18.7 5.4 %collective-permute-start.4 = (bf16[40,2048]{1,0:T(8,128)(2,1)S(1)}, bf16[40,2048]{1,0:T(8,128)(2,1)S(1)}, u32[]{:S(2)}, u32[]{:S(2)}) collective-permute-start(bf16[40,2048]{1,0:T(8,128)(2,1)S(1)} %get-tuple-element.51.refs_1_.near), channel_id=1, source_target_pairs={{0,16},{16,0},{1,17},{17,1},{2,18},{18,2},{3,19},{19,3},{4,20},{20... | collective-permute-start | bytes 491528 | tf_op jit(solution)/shard_map/ppermute | solution.py:29
  19.9 8.3 %collective-permute-start.5 = (bf16[40,2048]{1,0:T(8,128)(2,1)S(1)}, bf16[40,2048]{1,0:T(8,128)(2,1)S(1)}, u32[]{:S(2)}, u32[]{:S(2)}) collective-permute-start(bf16[40,2048]{1,0:T(8,128)(2,1)S(1)} %get-tuple-element.52.refs_2_.near), channel_id=1, source_target_pairs={{0,4},{4,0},{8,12},{12,8},{1,5},{5,1},{9,13},{13,9},{2,6},{6,2},{1... | collective-permute-start | bytes 491528 | tf_op jit(solution)/shard_map/ppermute | solution.py:29
  27.7 4.3 %collective-permute-start.6 = (f32[40,2048]{1,0:T(8,128)S(1)}, f32[40,2048]{1,0:T(8,128)S(1)}, u32[]{:S(2)}, u32[]{:S(2)}) collective-permute-start(f32[40,2048]{1,0:T(8,128)S(1)} %get-tuple-element.57), channel_id=1, source_target_pairs={{0,1},{1,0},{2,3},{3,2},{4,5},{5,4},{6,7},{7,6},{8,9},{9,8},{10,11... | collective-permute-start | bytes 983048 | tf_op jit(solution)/shard_map/ppermute | solution.py:29
  27.8 4.2 %collective-permute-start.7 = (f32[40,2048]{1,0:T(8,128)S(1)}, f32[40,2048]{1,0:T(8,128)S(1)}, u32[]{:S(2)}, u32[]{:S(2)}) collective-permute-start(f32[40,2048]{1,0:T(8,128)S(1)} %get-tuple-element.58), channel_id=1, source_target_pairs={{0,1},{1,0},{2,3},{3,2},{4,5},{5,4},{6,7},{7,6},{8,9},{9,8},{10,11... | collective-permute-start | bytes 983048 | tf_op jit(solution)/shard_map/ppermute | solution.py:29
  31.8 1.7 %collective-permute-start.8 = (f32[40,2048]{1,0:T(8,128)S(1)}, f32[40,2048]{1,0:T(8,128)S(1)}, u32[]{:S(2)}, u32[]{:S(2)}) collective-permute-start(f32[40,2048]{1,0:T(8,128)S(1)} %get-tuple-element.59), channel_id=1, source_target_pairs={{0,1},{1,0},{2,3},{3,2},{4,5},{5,4},{6,7},{7,6},{8,9},{9,8},{10,11... | collective-permute-start | bytes 983048 | tf_op jit(solution)/shard_map/ppermute | solution.py:29
  33.7 13.3 %collective-permute-start.16 = (bf16[3,40,2048]{2,1,0:T(8,128)(2,1)S(1)}, bf16[3,40,2048]{2,1,0:T(8,128)(2,1)S(1)}, u32[]{:S(2)}, u32[]{:S(2)}) collective-permute-start(bf16[3,40,2048]{2,1,0:T(8,128)(2,1)S(1)} %get-tuple-element.60.refs_3_.refs_1_), channel_id=1, source_target_pairs={{0,2},{1,3},{2,0},{3,1},{4,6},{5,7},{6,4},{7,5},{8,10},{9,11},{10,... | collective-permute-start | bytes 1474568 | tf_op jit(solution)/shard_map/ppermute | solution.py:29
  38.3 6.8 %collective-permute-start.9 = (f32[32,1280]{1,0:T(8,128)S(1)}, f32[32,1280]{1,0:T(8,128)S(1)}, u32[]{:S(2)}, u32[]{:S(2)}) collective-permute-start(f32[32,1280]{1,0:T(8,128)S(1)} %get-tuple-element.65), channel_id=1, source_target_pairs={{0,1},{1,0},{2,3},{3,2},{4,5},{5,4},{6,7},{7,6},{8,9},{9,8},{10,11... | collective-permute-start | bytes 491528 | tf_op jit(solution)/shard_map/ppermute | solution.py:29
  38.3 6.7 %collective-permute-start.11 = (f32[32,1280]{1,0:T(8,128)S(1)}, f32[32,1280]{1,0:T(8,128)S(1)}, u32[]{:S(2)}, u32[]{:S(2)}) collective-permute-start(f32[32,1280]{1,0:T(8,128)S(1)} %get-tuple-element.67), channel_id=1, source_target_pairs={{0,1},{1,0},{2,3},{3,2},{4,5},{5,4},{6,7},{7,6},{8,9},{9,8},{10,11... | collective-permute-start | bytes 491528 | tf_op jit(solution)/shard_map/ppermute | solution.py:29
  41.1 4.0 %collective-permute-start.13 = (f32[32,1280]{1,0:T(8,128)S(1)}, f32[32,1280]{1,0:T(8,128)S(1)}, u32[]{:S(2)}, u32[]{:S(2)}) collective-permute-start(f32[32,1280]{1,0:T(8,128)S(1)} %get-tuple-element.69), channel_id=1, source_target_pairs={{0,1},{1,0},{2,3},{3,2},{4,5},{5,4},{6,7},{7,6},{8,9},{9,8},{10,11... | collective-permute-start | bytes 491528 | tf_op jit(solution)/shard_map/ppermute | solution.py:29
  45.2 11.2 %collective-permute-start.15 = (bf16[3,40,1280]{2,1,0:T(8,128)(2,1)S(1)}, bf16[3,40,1280]{2,1,0:T(8,128)(2,1)S(1)}, u32[]{:S(2)}, u32[]{:S(2)}) collective-permute-start(bf16[3,40,1280]{2,1,0:T(8,128)(2,1)S(1)} %get-tuple-element.72.rest_0_), channel_id=1, source_target_pairs={{0,2},{1,3},{2,0},{3,1},{4,6},{5,7},{6,4},{7,5},{8,10},{9,11},{10,... | collective-permute-start | bytes 921608 | tf_op jit(solution)/shard_map/ppermute | solution.py:29
  47.2 1.5 %collective-permute-start.17 = (bf16[48,2048]{1,0:T(8,128)(2,1)S(1)}, bf16[48,2048]{1,0:T(8,128)(2,1)S(1)}, u32[]{:S(2)}, u32[]{:S(2)}) collective-permute-start(bf16[48,2048]{1,0:T(8,128)(2,1)S(1)} %get-tuple-element.74.rest_0_), channel_id=1, source_target_pairs={{0,1},{1,0},{2,3},{3,2},{4,5},{5,4},{6,7},{7,6},{8,9},{9,8},{10,11... | collective-permute-start | bytes 589832 | tf_op jit(solution)/shard_map/ppermute | solution.py:29
  47.3 1.7 %collective-permute-start.18 = (bf16[48,2048]{1,0:T(8,128)(2,1)S(1)}, bf16[48,2048]{1,0:T(8,128)(2,1)S(1)}, u32[]{:S(2)}, u32[]{:S(2)}) collective-permute-start(bf16[48,2048]{1,0:T(8,128)(2,1)S(1)} %get-tuple-element.75.rest_1_), channel_id=1, source_target_pairs={{0,1},{1,0},{2,3},{3,2},{4,5},{5,4},{6,7},{7,6},{8,9},{9,8},{10,11... | collective-permute-start | bytes 589832 | tf_op jit(solution)/shard_map/ppermute | solution.py:29
  47.8 1.5 %collective-permute-start.19 = (bf16[48,2048]{1,0:T(8,128)(2,1)S(1)}, bf16[48,2048]{1,0:T(8,128)(2,1)S(1)}, u32[]{:S(2)}, u32[]{:S(2)}) collective-permute-start(bf16[48,2048]{1,0:T(8,128)(2,1)S(1)} %get-tuple-element.76.rest_2_), channel_id=1, source_target_pairs={{0,1},{1,0},{2,3},{3,2},{4,5},{5,4},{6,7},{7,6},{8,9},{9,8},{10,11... | collective-permute-start | bytes 589832 | tf_op jit(solution)/shard_map/ppermute | solution.py:29
  56.6 1.4 %collective-permute-start.20 = (bf16[48,1280]{1,0:T(8,128)(2,1)S(1)}, bf16[48,1280]{1,0:T(8,128)(2,1)S(1)}, u32[]{:S(2)}, u32[]{:S(2)}) collective-permute-start(bf16[48,1280]{1,0:T(8,128)(2,1)S(1)} %get-tuple-element.77.rest_0_), channel_id=1, source_target_pairs={{0,1},{1,0},{2,3},{3,2},{4,5},{5,4},{6,7},{7,6},{8,9},{9,8},{10,11... | collective-permute-start | bytes 368648 | tf_op jit(solution)/shard_map/ppermute | solution.py:29
  61.0 6.4 %collective-permute-start.23 = (bf16[2,40,1024]{2,1,0:T(8,128)(2,1)S(1)}, bf16[2,40,1024]{2,1,0:T(8,128)(2,1)S(1)}, u32[]{:S(2)}, u32[]{:S(2)}) collective-permute-start(bf16[2,40,1024]{2,1,0:T(8,128)(2,1)S(1)} %get-tuple-element.81), channel_id=1, source_target_pairs={{0,16},{16,0},{1,17},{17,1},{2,18},{18,2},{3,19},{19,3},{4,20},{20... | collective-permute-start | bytes 491528 | tf_op jit(solution)/shard_map/ppermute | solution.py:29
  64.7 6.2 %collective-permute-start.25 = (bf16[2,40,1024]{2,1,0:T(8,128)(2,1)S(1)}, bf16[2,40,1024]{2,1,0:T(8,128)(2,1)S(1)}, u32[]{:S(2)}, u32[]{:S(2)}) collective-permute-start(bf16[2,40,1024]{2,1,0:T(8,128)(2,1)S(1)} %get-tuple-element.82.rest_0_), channel_id=1, source_target_pairs={{0,16},{16,0},{1,17},{17,1},{2,18},{18,2},{3,19},{19,3},{4,20},{20... | collective-permute-start | bytes 491528 | tf_op jit(solution)/shard_map/ppermute | solution.py:29
  67.4 5.4 %collective-permute-start.24 = (bf16[2,20,1024]{2,1,0:T(8,128)(2,1)S(1)}, bf16[2,20,1024]{2,1,0:T(8,128)(2,1)S(1)}, u32[]{:S(2)}, u32[]{:S(2)}) collective-permute-start(bf16[2,20,1024]{2,1,0:T(8,128)(2,1)S(1)} %get-tuple-element.84), channel_id=1, source_target_pairs={{0,4},{4,0},{8,12},{12,8},{1,5},{5,1},{9,13},{13,9},{2,6},{6,2},{1... | collective-permute-start | bytes 245768 | tf_op jit(solution)/shard_map/ppermute | solution.py:29
  71.0 4.7 %collective-permute-start.26 = (bf16[2,20,1024]{2,1,0:T(8,128)(2,1)S(1)}, bf16[2,20,1024]{2,1,0:T(8,128)(2,1)S(1)}, u32[]{:S(2)}, u32[]{:S(2)}) collective-permute-start(bf16[2,20,1024]{2,1,0:T(8,128)(2,1)S(1)} %get-tuple-element.88), channel_id=1, source_target_pairs={{0,4},{4,0},{8,12},{12,8},{1,5},{5,1},{9,13},{13,9},{2,6},{6,2},{1... | collective-permute-start | bytes 245768 | tf_op jit(solution)/shard_map/ppermute | solution.py:29
  72.9 7.1 %collective-permute-start.27 = (bf16[2,10,1024]{2,1,0:T(8,128)(2,1)S(1)}, bf16[2,10,1024]{2,1,0:T(8,128)(2,1)S(1)}, u32[]{:S(2)}, u32[]{:S(2)}) collective-permute-start(bf16[2,10,1024]{2,1,0:T(8,128)(2,1)S(1)} %get-tuple-element.90), channel_id=1, source_target_pairs={{0,8},{4,12},{8,0},{12,4},{1,9},{5,13},{9,1},{13,5},{2,10},{6,14},... | collective-permute-start | bytes 122888 | tf_op jit(solution)/shard_map/ppermute | solution.py:29
  75.7 5.3 %collective-permute-start.28 = (bf16[2,10,1024]{2,1,0:T(8,128)(2,1)S(1)}, bf16[2,10,1024]{2,1,0:T(8,128)(2,1)S(1)}, u32[]{:S(2)}, u32[]{:S(2)}) collective-permute-start(bf16[2,10,1024]{2,1,0:T(8,128)(2,1)S(1)} %get-tuple-element.91), channel_id=1, source_target_pairs={{0,8},{4,12},{8,0},{12,4},{1,9},{5,13},{9,1},{13,5},{2,10},{6,14},... | collective-permute-start | bytes 122888 | tf_op jit(solution)/shard_map/ppermute | solution.py:29
  (7 other events, 14.4 us)

commit v6 on v5

--- a/solution.py
+++ b/solution.py
@@ -12,12 +12,14 @@
 NT = (((1,), (1,)), ((), ()))
 MIB = 2**20
 WINDOWS = [["g0"], ["u0", "g1"], ["d0"]]
-BESIDE = {"b0": ["u1"], "gu0": [], "gu1": ["d1"], "b1": []}
-FIRST = 0.62
+BESIDE = [[["d", ["u1"]], ["gu", ["d1"]]], [["gud", []]]]
+UPLIM = 3
+INNER = True
+FIRST = 0.54
 EST = 1
-PARTS = [1, 1]
+PARTS = [1, 2]
 ORDER = 0
-SPLITS = [0.5]
+SPLITS = [0.38]
 SENDS = [1, 2]
 VMEM = pl.BlockSpec(memory_space=pltpu.VMEM)
 SMEM = pl.BlockSpec(memory_space=pltpu.SMEM)
@@ -128,51 +130,58 @@
     return place // (count // 2), place % (count // 2)
 
 
-def up(where, near, far, order, weights, transposed, block, cuts, wanted=(), after=()):
-    half, feats = near.shape
-    count = 2 ** len(order)
+def up(where, kinds, nears, fars, orders, weights, block, cuts, wanted=(), after=()):
+    sides = sorted({int(kind == "d") for kind in kinds})
+    nears, fars, orders = ([v[i] for i in sides] for v in (nears, fars, orders))
+    n, k = len(sides), len(kinds)
+    half, feats = nears[0].shape
+    count = 2 ** len(orders[0])
     rows = 2 * half // count
-    width = weights[0].shape[0 if transposed else 1]
-    n, m = len(weights), len(wanted)
+    width = weights[0].shape[0 if kinds[0] == "d" else 1]
+    m = len(wanted)
     specs = [s for _, s in wanted]
 
-    def kernel(where, near, far, *refs):
+    def kernel(where, *refs):
         refs = list(refs)
-        ws = [refs.pop(0) for _ in range(n)]
+        near, far = ([refs.pop(0) for _ in sides] for _ in range(2))
+        ws = [refs.pop(0) for _ in kinds]
         srcs = [refs.pop(0) for _ in range(m)]
         del refs[: len(after)]
-        outs = [[refs.pop(0) for _ in range(len(cuts))] for _ in range(n)]
+        outs = [[refs.pop(0) for _ in cuts] for _ in kinds]
         dsts = [refs.pop(0) for _ in range(m)]
         wide, lhs = refs[:2]
         made = copies(where, specs, srcs, dsts, refs[2]) if m else []
         for copy in made:
             copy.start()
         first = where[1] == 0
-        both = (near[...].astype(F32), far[...].astype(F32))
-        run = half if order == sorted(order) else rows
-        for at in range(0, 2 * half, run):
-            picks = []
-            for start in (at, (at + half) % (2 * half)):
-                side, place = locate(start // rows, order, count)
-                picks.append(both[side][place * rows : place * rows + run])
-            wide[at : at + run, :] = jnp.where(first, *picks)
-        lhs[...] = wide[...].astype(BF16)
+        for i, order in enumerate(orders):
+            both = (near[i][...].astype(F32), far[i][...].astype(F32))
+            run = half if order == sorted(order) else rows
+            for at in range(0, 2 * half, run):
+                picks = []
+                for start in (at, (at + half) % (2 * half)):
+                    side, place = locate(start // rows, order, count)
+                    picks.append(both[side][place * rows : place * rows + run])
+                wide[at : at + run, :] = jnp.where(first, *picks)
+            lhs[i] = wide[...].astype(BF16)
 
         def tile(cut):
-            for i, w in enumerate(ws):
-                if transposed:
-                    value = lax.dot_general(lhs[...], w[cut, :], NT, preferred_element_type=F32)
+            for kind, w, out in zip(kinds, ws, outs):
+                if kind == "d":
+                    value = lax.dot_general(
+                        lhs[n - 1], w[cut, :], NT, preferred_element_type=F32
+                    )
                 else:
-                    value = jnp.dot(lhs[...], w[:, cut], preferred_element_type=F32)
-                for out, (start, size) in zip(outs[i], cuts):
-                    out[:, cut] = value[start : start + size]
+                    value = jnp.dot(lhs[0], w[:, cut], preferred_element_type=F32)
+                for ref, (start, size) in zip(out, cuts):
+                    ref[:, cut] = value[start : start + size]
 
         if made:
-            block2 = width // 2 if width % 256 == 0 else width
-
-            @pl.loop(0, width // block2)
+            large = width // 2 if width % 256 == 0 else width
+
+            @pl.loop(0, width // large)
             def _(step):
-                tile(pl.ds(pl.multiple_of(step * block2, 128), block2))
+                tile(pl.ds(pl.multiple_of(step * large, 128), large))
 
         else:
             for step in range(width // block):
@@ -180,19 +189,26 @@
         for copy in made:
             copy.wait()
 
-    shapes = [jax.ShapeDtypeStruct((size, width), F32) for _, size in cuts] * n
+    shapes = [jax.ShapeDtypeStruct((size, width), F32) for _, size in cuts] * k
     got = call(
         kernel,
         "up",
-        [SMEM] + [VMEM] * (2 + n) + [HBM] * m + [ANY] * len(after),
+        [SMEM] + [VMEM] * (2 * n + k) + [HBM] * m + [ANY] * len(after),
         shapes + [fetched(w, s) for w, s in wanted],
-        [pltpu.VMEM((2 * half, feats), F32), pltpu.VMEM((2 * half, feats), BF16)]
+        [pltpu.VMEM((2 * half, feats), F32), pltpu.VMEM((n, 2 * half, feats), BF16)]
         + ([pltpu.SemaphoreType.DMA((m,))] if m else []),
-        limit=2,
-        estimate=cost(2 * n * 256 * feats * width, 2 * n * feats * width),
-    )(where, near, far, *[resident(w) for w in weights], *[in_hbm(w) for w, _ in wanted], *after)
-    k = len(cuts)
-    return [got[i * k : (i + 1) * k] for i in range(n)], got[n * k :]
+        limit=UPLIM,
+        estimate=cost(2 * k * 256 * feats * width, 2 * k * feats * width),
+    )(
+        where,
+        *nears,
+        *fars,
+        *[resident(w) for w in weights],
+        *[in_hbm(w) for w, _ in wanted],
+        *after,
+    )
+    r = len(cuts)
+    return [got[i * r : (i + 1) * r] for i in range(k)], got[k * r :]
 
 
 def gather(keeps, gots, cuts):
@@ -235,43 +251,43 @@
     )(a, b)
 
 
-def activate(sums, got, padded, after):
-    _, half, width = sums.shape
-
-    def kernel(sums, got, *rest):
-        outs = rest[-3:]
-        gate = sums[0] + got[0].astype(F32)
-        upward = sums[1] + got[1].astype(F32)
-        back = sums[2] + got[2].astype(F32)
-        sigma = jax.nn.sigmoid(gate)
-        hidden = gate * sigma * upward
-        d_up = back * gate * sigma
-        d_gate = back * upward * sigma * (1.0 + gate * (1.0 - sigma))
-        for out, value in zip(outs, (hidden, d_gate, d_up)):
-            if padded > half:
-                empty = jnp.zeros((padded - half, width), F32)
-                value = jnp.concatenate([value, empty], axis=0)
-            out[...] = value.astype(BF16)
+def activate(sums, gots, padded, after):
+    n, half = len(sums), sums[0].shape[1]
+    widths = [v.shape[2] for v in sums]
+
+    def kernel(*refs):
+        outs = refs[-3:]
+        for p, width in enumerate(widths):
+            gate, upward, back = (refs[p][i] + refs[n + p][i].astype(F32) for i in range(3))
+            sigma = jax.nn.sigmoid(gate)
+            hidden = gate * sigma * upward
+            d_up = back * gate * sigma
+            d_gate = back * upward * sigma * (1.0 + gate * (1.0 - sigma))
+            at = sum(widths[:p])
+            for out, value in zip(outs, (hidden, d_gate, d_up)):
+                if padded > half:
+                    empty = jnp.zeros((padded - half, width), F32)
+                    value = jnp.concatenate([value, empty], axis=0)
+                out[:, at : at + width] = value.astype(BF16)
 
     return call(
         kernel,
         "activate",
-        [VMEM] * 2 + [ANY] * len(after),
-        [jax.ShapeDtypeStruct((padded, width), BF16)] * 3,
-        limit=2,
-    )(sums, got, *after)
-
-
-def down(where, own, other, weights, units, prev, half, part, last):
+        [VMEM] * (2 * n) + [ANY] * len(after),
+        [jax.ShapeDtypeStruct((padded, sum(widths)), BF16)] * 3,
+        limit=3,
+    )(*sums, *gots, *after)
+
+
+def down(where, own, other, weights, prev, half, part, last, inner=False):
     padded, width = own[0].shape
     start, feats = part
-    units = slice(units[0], units[0] + units[1])
     block = 256 if feats % 256 == 0 else 128
 
     def kernel(where, *rest):
         own, other, (gate_w, up_w, down_w), rest = rest[:3], rest[3:6], rest[6:9], rest[9:]
-        lhs = rest[-1]
-        outs = rest[len(prev) : -1]
+        lhs, swapped = rest[-2:]
+        outs = rest[len(prev) : -2]
         first = where[1] == 0
         for i in range(3):
             lhs[i, :padded, :] = own[i][...]
@@ -280,16 +296,24 @@
         for step in range(feats // block):
             cut = slice(step * block, (step + 1) * block)
             full = slice(start + step * block, start + (step + 1) * block)
-            mixed = jnp.dot(lhs[0], down_w[units, full], preferred_element_type=F32)
-            grad = lax.dot_general(lhs[1], gate_w[full, units], NT, preferred_element_type=F32)
-            grad += lax.dot_general(lhs[2], up_w[full, units], NT, preferred_element_type=F32)
+            mixed = jnp.dot(lhs[0], down_w[:, full], preferred_element_type=F32)
+            grad = lax.dot_general(lhs[1], gate_w[full, :], NT, preferred_element_type=F32)
+            grad += lax.dot_general(lhs[2], up_w[full, :], NT, preferred_element_type=F32)
             for i, value in enumerate((mixed, grad)):
                 if prev:
                     value += prev_ref(rest)[i, :, full]
                 if last:
                     a, b = value[:half], value[padded : padded + half]
-                    outs[0][i, :, cut] = jnp.where(first, a, b)
-                    outs[1][i, :, cut] = jnp.where(first, b, a).astype(BF16)
+                    a, b = jnp.where(first, a, b), jnp.where(first, b, a)
+                    if inner:
+                        q = half // 2
+                        for at, rows in ((0, a), (q, b)):
+                            outs[0][i, at : at + q, cut] = rows[:q]
+                            swapped[i, at : at + q, :] = rows[q:]
+                        outs[1][i, :, cut] = swapped[i].astype(BF16)
+                    else:
+                        outs[0][i, :, cut] = a
+                        outs[1][i, :, cut] = b.astype(BF16)
                 else:
                     outs[0][i, :, cut] = value
 
@@ -308,7 +332,7 @@
         "down",
         [SMEM] + [VMEM] * (9 + len(prev)),
         shapes,
-        [pltpu.VMEM((3, 2 * padded, width), BF16)],
+        [pltpu.VMEM((3, 2 * padded, width), BF16), pltpu.VMEM((2, half, block), F32)],
         limit=2,
         estimate=cost(6 * 256 * feats * width, 6 * feats * width) if last else cost(EST, EST),
     )(where, *own, *other, *[resident(w) for w in weights], *prev)
@@ -403,17 +427,16 @@
     summed = []
     after = ()
     for c in range(len(chunks)):
+        step = -(-half // (8 * SENDS[c])) * 8
+        runs = [(0, half)] + [(half + t, min(step, half - t)) for t in range(0, half, step)]
         out = {}
-        top = -(-half // 32) * 16 if SENDS[c] == 2 else half
-        runs = [(0, half), (half, top)] + ([(half + top, half - top)] if top < half else [])
-        for kind, i in (("gu", 0), ("b", 1)) if c else (("b", 1), ("gu", 0)):
-            ws = [here[f"{w}{c}"] for w in ("d" if kind == "b" else "gu")]
-            names, parts = wanted(BESIDE[f"{kind}{c}"])
-            out[kind], got = up(
-                where, near[i], far[i], orders[i], ws, kind == "b", block, runs, parts, after
-            )
+        for kinds, beside in BESIDE[c]:
+            ws = [here[f"{w}{c}"] for w in kinds]
+            names, parts = wanted(beside)
+            made, got = up(where, kinds, near, far, orders, ws, block, runs, parts, after)
             here.update(zip(names, got))
-        out = out["gu"] + out["b"]
+            out.update(zip(kinds, made))
+        out = [out[kind] for kind in "gud"]
         size = chunks[c][1]
         parts = PARTS[c] if size % (128 * PARTS[c]) == 0 else 1
         cuts = [(i * size // parts, size // parts) for i in range(parts)]
@@ -421,27 +444,37 @@
             [v[0] for v in out], [[swap(r, "bulk", bulk, 1) for r in v[1:]] for v in out], cuts
         )
         after = tuple(rounded for _, rounded in sums)
-        summed += [(c, cut, *pair) for cut, pair in zip(cuts, sums)]
+        summed.append(sums)
 
     prev = ()
-    for step, (c, cut, sums, rounded) in enumerate(summed):
-        for b in bits(bulk, 2)[:-1]:
-            sums, rounded = add(sums, swap(rounded, "bulk", bulk, b))
-        got = swap(rounded, "bulk", bulk, bits(bulk, 2)[-1])
+    for c, pairs in enumerate(summed):
+        sums, gots = [], []
+        for total, rounded in pairs:
+            for b in bits(bulk, 2)[:-1]:
+                total, rounded = add(total, swap(rounded, "bulk", bulk, b))
+            sums.append(total)
+            gots.append(swap(rounded, "bulk", bulk, bits(bulk, 2)[-1]))
         w = [here[f"{name}{c}"] for name in "gud"]
-        own = activate(sums, got, padded, (*prev, *[v[-1] for v in summed[step + 1 :]]))
+        late = [r for later in summed[c + 1 :] for _, r in later]
+        own = activate(sums, gots, padded, (*prev, *late))
         other = [swap(v, "bulk", bulk, 1) for v in own]
-        if step < len(summed) - 1:
-            prev = down(where, own, other, w, cut, prev, half, (0, feats), False)
-    made = [down(where, own, other, w, cut, prev, half, part, True) for part in pieces]
+        if c < len(chunks) - 1:
+            prev = down(where, own, other, w, prev, half, (0, feats), False)
+    made = [
+        down(where, own, other, w, prev, half, part, True, INNER and p == 1)
+        for p, part in enumerate(pieces)
+    ]
     stays, gots = [], []
     for p, (stay, send) in enumerate(made):
         late = made[p + 1][1:] if p + 1 < len(made) else ()
-        for hop in reversed(hops[1:]):
+        path = hops[::-1]
+        if INNER and p == 1:
+            path = [path[1], path[0], *path[2:]]
+        for hop in path[:-1]:
             stay, send = fold(stay, swap(send, *hop), late)
             late = ()
         stays.append(stay)
-        gots.append(swap(send, *hops[0]))
+        gots.append(swap(send, *path[-1]))
     return tuple(finish(stays, gots))
 
 

time: 81.8 us -> 80.9 us (0.989)
  Pallas kernels: 39.6 us -> 38 us
  waiting for transfers between devices: 15.7 us -> 17 us
    ppermute x29 -> x30, waiting for transfers between devices: 15.7 us -> 17 us  [swap(): return lax.ppermute(value, axis, [(i, i ^ bit) for i in range(size)])]
    pallas_call x6 -> x5, Pallas kernels: 12.9 us -> 11.8 us  [the longest x3 11.4 us: up(): call(kernel, 'up', [SMEM] + [VMEM] * (2 * n + k) + [HBM] * m + [ANY] * le...]
    ppermute x29 -> x30, starting transfers between devices: 25.4 us -> 24.8 us  [swap(): return lax.ppermute(value, axis, [(i, i ^ bit) for i in range(size)])]
  transfers between devices with their start and end apart: 29 -> 30, of which waited for: 18 -> 16; matrix products, arithmetic and copies ran while one was open for 0% -> 0% of each run, Pallas kernels for 44% -> 41%
where the time goes in v6:
time: 80.9 us; the launch traced here: 80.7 us
  Pallas kernels  38 us (47%)
  starting transfers between devices  24.8 us (31%)
  waiting for transfers between devices  17 us (21%)
  between operations  0.84 us (1%)
    ppermute x30, starting transfers between devices, swap(): return lax.ppermute(value, axis, [(i, i ^ bit) for i in range(size)])  24.8 us
    ppermute x30, waiting for transfers between devices, swap(): return lax.ppermute(value, axis, [(i, i ^ bit) for i in range(size)])  17 us
    pallas_call x3, Pallas kernels, fetch(): call(kernel, 'fetch', [SMEM] + [HBM] * n + [ANY] * len(after), outs, [plt...  12.7 us
    pallas_call x3, Pallas kernels, down(): call(kernel, 'down', [SMEM] + [VMEM] * (9 + len(prev)), shapes, [pltpu.VM...  12.3 us
    pallas_call x3, Pallas kernels, up(): call(kernel, 'up', [SMEM] + [VMEM] * (2 * n + k) + [HBM] * m + [ANY] * le...  11.4 us
  transfers between devices with their start and end apart: 30, of which 16 were waited for; matrix products, arithmetic and copies ran while one was open for 0% of the time, Pallas kernels for 41%

profile of v6, /device:TPU:0, one launch (start us, length us, event | category | flops | bytes accessed | tf_op | source)
XLA Modules:
  0.0 80.7 jit_solution(16905810869348484976)
XLA Ops:
  0.6 4.1 %collective-permute-start = (bf16[10,2048]{1,0:T(8,128)(2,1)}, bf16[10,2048]{1,0:T(8,128)(2,1)S(1)}, u32[]{:S(2)}, u32[]{:S(2)}) collective-permute-start(bf16[10,2048]{1,0:T(8,128)(2,1)} %refs_0_.5), channel_id=1, source_target_pairs={{0,8},{4,12},{8,0},{12,4},{1,9},{5,13},{9,1},{13,5},{2,10},{6,14},... | collective-permute-start | bytes 122888 | tf_op jit(solution)/shard_map/ppermute | solution.py:31
  4.7 1.5 %collective-permute-start.1 = (bf16[10,2048]{1,0:T(8,128)(2,1)}, bf16[10,2048]{1,0:T(8,128)(2,1)S(1)}, u32[]{:S(2)}, u32[]{:S(2)}) collective-permute-start(bf16[10,2048]{1,0:T(8,128)(2,1)} %refs_1_.2), channel_id=1, source_target_pairs={{0,16},{16,0},{1,17},{17,1},{2,18},{18,2},{3,19},{19,3},{4,20},{20... | collective-permute-start | bytes 122888 | tf_op jit(solution)/shard_map/ppermute | solution.py:31
  6.3 3.6 %fetch.3.refs_4_.refs_2_.rest_6_ = bf16[2048,1792]{1,0:T(8,128)(2,1)S(1)} custom-call(s32[2]{0:T(128)S(1)} %pad_add_fusion.where, bf16[2048,6656]{1,0:T(8,128)(2,1)} %refs_1_.3), custom_call_target="tpu_custom_call" | custom-call | bytes 7340032 | tf_op jit(solution)/shard_map/fetch/pallas_call | solution.py:95
  10.1 1.6 %collective-permute-start.2 = (bf16[20,2048]{1,0:T(8,128)(2,1)S(1)}, bf16[20,2048]{1,0:T(8,128)(2,1)S(1)}, u32[]{:S(2)}, u32[]{:S(2)}) collective-permute-start(bf16[20,2048]{1,0:T(8,128)(2,1)S(1)} %get-tuple-element.49.refs_2_.refs_0_), channel_id=1, source_target_pairs={{0,4},{4,0},{8,12},{12,8},{1,5},{5,1},{9,13},{13,9},{2,6},{6,2},{1... | collective-permute-start | bytes 245768 | tf_op jit(solution)/shard_map/ppermute | solution.py:31
  12.7 5.5 %fetch.4 = (bf16[2048,1792]{1,0:T(8,128)(2,1)S(1)}, bf16[2048,1536]{1,0:T(8,128)(2,1)S(1)}) custom-call(s32[2]{0:T(128)S(1)} %pad_add_fusion.where, bf16[2048,6656]{1,0:T(8,128)(2,1)} %refs_3_.1, bf16[2048,6656]{1,0:T(8,128)(2,1)} %refs_1_.3, bf16[20,2048]{1,0:T(8,128)(2,1)S(1)} %get-tuple-element.49.refs_2_.refs_0_, ...), custom_call_target="tpu_custom_call" | custom-call | bytes 13631488 | tf_op jit(solution)/shard_map/fetch/pallas_call | solution.py:95
  18.5 1.7 %collective-permute-start.4 = (bf16[40,2048]{1,0:T(8,128)(2,1)S(1)}, bf16[40,2048]{1,0:T(8,128)(2,1)S(1)}, u32[]{:S(2)}, u32[]{:S(2)}) collective-permute-start(bf16[40,2048]{1,0:T(8,128)(2,1)S(1)} %get-tuple-element.53.refs_1_.refs_0_), channel_id=1, source_target_pairs={{0,16},{16,0},{1,17},{17,1},{2,18},{18,2},{3,19},{19,3},{4,20},{20... | collective-permute-start | bytes 491528 | tf_op jit(solution)/shard_map/ppermute | solution.py:31
  20.1 3.6 %fetch.5.refs_2_.rest_8_ = bf16[1792,2048]{1,0:T(8,128)(2,1)S(1)} custom-call(s32[2]{0:T(128)S(1)} %pad_add_fusion.where, bf16[6656,2048]{1,0:T(8,128)(2,1)} %refs_4_.1, bf16[40,2048]{1,0:T(8,128)(2,1)S(1)} %get-tuple-element.53.refs_1_.refs_0_, bf16[40,2048]{1,0:T(8,128)(2,1)S(1)} %get-tuple-element.54.refs_2_.refs_0_.refs_1_), custom_call_target="tpu_custom_call" | custom-call | bytes 7340032 | tf_op jit(solution)/shard_map/fetch/pallas_call | solution.py:95
  23.8 3.3 %up.3 = (f32[40,1792]{1,0:T(8,128)S(1)}, f32[40,1792]{1,0:T(8,128)S(1)}, bf16[2048,1536]{1,0:T(8,128)(2,1)S(1)}) custom-call(s32[2]{0:T(128)S(1)} %pad_add_fusion.where, bf16[40,2048]{1,0:T(8,128)(2,1)S(1)} %get-tuple-element.54.refs_2_.refs_0_.refs_1_, bf16[40,2048]{1,0:T(8,128)(2,1)S(1)} %collective-permute-done.5.refs_1_.refs_3_, ...), custom_call_target="tpu_custom_call" | custom-call | flops 1879048192 | bytes 7340032 | tf_op jit(solution)/shard_map/up/pallas_call | solution.py:193
  27.2 3.5 %up.4 = (f32[40,1792]{1,0:T(8,128)S(1)}, f32[40,1792]{1,0:T(8,128)S(1)}, f32[40,1792]{1,0:T(8,128)S(1)}, f32[40,1792]{1,0:T(8,128)S(1)}, bf16[1536,2048]{1,0:T(8,128)(2,1)S(1)}) custom-call(s32[2]{0:T(128)S(1)} %pad_add_fusion.where, bf16[40,2048]{1,0:T(8,128)(2,1)S(1)} %get-tuple-element.53.refs_1_.refs_0_, ...), custom_call_target="tpu_custom_call" | custom-call | flops 3758096384 | bytes 14680064 | tf_op jit(solution)/shard_map/up/pallas_call | solution.py:193
  31.4 1.1 %collective-permute-done.6.refs_3_ = f32[40,1792]{1,0:T(8,128)S(1)} collective-permute-done((f32[40,1792]{1,0:T(8,128)S(1)}, f32[40,1792]{1,0:T(8,128)S(1)}, u32[]{:S(2)}, u32[]{:S(2)}) %collective-permute-start.6) | collective-permute-done | bytes 286752 | tf_op jit(solution)/shard_map/ppermute | solution.py:31
  33.0 1.6 %collective-permute-start.17 = (bf16[3,40,1792]{2,1,0:T(8,128)(2,1)S(1)}, bf16[3,40,1792]{2,1,0:T(8,128)(2,1)S(1)}, u32[]{:S(2)}, u32[]{:S(2)}) collective-permute-start(bf16[3,40,1792]{2,1,0:T(8,128)(2,1)S(1)} %get-tuple-element.63.refs_7_), channel_id=1, source_target_pairs={{0,2},{1,3},{2,0},{3,1},{4,6},{5,7},{6,4},{7,5},{8,10},{9,11},{10,... | collective-permute-start | bytes 1290248 | tf_op jit(solution)/shard_map/ppermute | solution.py:31
  34.6 4.5 %up.5 = (f32[40,1536]{1,0:T(8,128)S(1)}, f32[24,1536]{1,0:T(8,128)S(1)}, f32[16,1536]{1,0:T(8,128)S(1)}, f32[40,1536]{1,0:T(8,128)S(1)}, f32[24,1536]{1,0:T(8,12...) custom-call(s32[2]{0:T(128)S(1)} %pad_add_fusion.where, ...), custom_call_target="tpu_custom_call" | custom-call | flops 4831838208 | bytes 18874368 | tf_op jit(solution)/shard_map/up/pallas_call | solution.py:193
  42.8 1.5 %collective-permute-start.16 = (bf16[3,40,768]{2,1,0:T(8,128)(2,1)S(1)}, bf16[3,40,768]{2,1,0:T(8,128)(2,1)S(1)}, u32[]{:S(2)}, u32[]{:S(2)}) collective-permute-start(bf16[3,40,768]{2,1,0:T(8,128)(2,1)S(1)} %get-tuple-element.76.refs_3_), channel_id=1, source_target_pairs={{0,2},{1,3},{2,0},{3,1},{4,6},{5,7},{6,4},{7,5},{8,10},{9,11},{10,... | collective-permute-start | bytes 552968 | tf_op jit(solution)/shard_map/ppermute | solution.py:31
  44.2 1.2 %collective-permute-done.17.refs_1_ = bf16[3,40,1792]{2,1,0:T(8,128)(2,1)S(1)} collective-permute-done((bf16[3,40,1792]{2,1,0:T(8,128)(2,1)S(1)}, bf16[3,40,1792]{2,1,0:T(8,128)(2,1)S(1)}, u32[]{:S(2)}, u32[]{:S(2)}) %collective-permute-start.17) | collective-permute-done | bytes 430112 | tf_op jit(solution)/shard_map/ppermute | solution.py:31
  47.6 6.2 %down.3.refs_4_.rest_9_ = f32[2,96,2048]{2,1,0:T(8,128)S(1)} custom-call(s32[2]{0:T(128)S(1)} %pad_add_fusion.where, bf16[48,1792]{1,0:T(8,128)(2,1)S(1)} %get-tuple-element.78.rest_0_, bf16[48,1792]{1,0:T(8,128)(2,1)S(1)} %get-tuple-element.79.rest_1_, bf16[48,1792]{1,0:T(8,128)(2,1)S(1)} %get-tuple-element.80.rest_2_, ...), custom_call_target="tpu_custom_call" | custom-call | flops 1 | bytes 1 | tf_op jit(solution)/shard_map/down/pallas_call | solution.py:330
  56.0 3.6 %down.5 = (f32[2,40,1280]{2,1,0:T(8,128)S(1)}, bf16[2,40,1280]{2,1,0:T(8,128)(2,1)S(1)}) custom-call(s32[2]{0:T(128)S(1)} %pad_add_fusion.where, bf16[48,1536]{1,0:T(8,128)(2,1)S(1)} %get-tuple-element.81.rest_0_, bf16[48,1536]{1,0:T(8,128)(2,1)S(1)} %get-tuple-element.82.rest_1_, bf16[48,1536]{1,0:T(8,128)(2,1)S(1)} %get-tuple-element.83.rest_2_, ...), custom_call_target="tpu_custom_call" | custom-call | flops 3019898880 | bytes 11796480 | tf_op jit(solution)/shard_map/down/pallas_call | solution.py:330
  59.7 2.0 %collective-permute-start.26 = (bf16[2,40,1280]{2,1,0:T(8,128)(2,1)S(1)}, bf16[2,40,1280]{2,1,0:T(8,128)(2,1)S(1)}, u32[]{:S(2)}, u32[]{:S(2)}) collective-permute-start(bf16[2,40,1280]{2,1,0:T(8,128)(2,1)S(1)} %get-tuple-element.86.rest_0_), channel_id=1, source_target_pairs={{0,4},{4,0},{8,12},{12,8},{1,5},{5,1},{9,13},{13,9},{2,6},{6,2},{1... | collective-permute-start | bytes 614408 | tf_op jit(solution)/shard_map/ppermute | solution.py:31
  61.7 2.4 %down.4 = (f32[2,40,768]{2,1,0:T(8,128)S(1)}, bf16[2,40,768]{2,1,0:T(8,128)(2,1)S(1)}) custom-call(s32[2]{0:T(128)S(1)} %pad_add_fusion.where, bf16[48,1536]{1,0:T(8,128)(2,1)S(1)} %get-tuple-element.81.rest_0_, bf16[48,1536]{1,0:T(8,128)(2,1)S(1)} %get-tuple-element.82.rest_1_, bf16[48,1536]{1,0:T(8,128)(2,1)S(1)} %get-tuple-element.83.rest_2_, ...), custom_call_target="tpu_custom_call" | custom-call | flops 1811939328 | bytes 7077888 | tf_op jit(solution)/shard_map/down/pallas_call | solution.py:330
  64.6 2.6 %collective-permute-done.26.got = bf16[2,40,1280]{2,1,0:T(8,128)(2,1)S(1)} collective-permute-done((bf16[2,40,1280]{2,1,0:T(8,128)(2,1)S(1)}, bf16[2,40,1280]{2,1,0:T(8,128)(2,1)S(1)}, u32[]{:S(2)}, u32[]{:S(2)}) %collective-permute-start.26) | collective-permute-done | bytes 204832 | tf_op jit(solution)/shard_map/ppermute | solution.py:31
  67.3 1.4 %collective-permute-start.27 = (bf16[2,20,1280]{2,1,0:T(8,128)(2,1)S(1)}, bf16[2,20,1280]{2,1,0:T(8,128)(2,1)S(1)}, u32[]{:S(2)}, u32[]{:S(2)}) collective-permute-start(bf16[2,20,1280]{2,1,0:T(8,128)(2,1)S(1)} %get-tuple-element.92), channel_id=1, source_target_pairs={{0,16},{16,0},{1,17},{17,1},{2,18},{18,2},{3,19},{19,3},{4,20},{20... | collective-permute-start | bytes 307208 | tf_op jit(solution)/shard_map/ppermute | solution.py:31
  69.8 2.5 %collective-permute-done.27.got = bf16[2,20,1280]{2,1,0:T(8,128)(2,1)S(1)} collective-permute-done((bf16[2,20,1280]{2,1,0:T(8,128)(2,1)S(1)}, bf16[2,20,1280]{2,1,0:T(8,128)(2,1)S(1)}, u32[]{:S(2)}, u32[]{:S(2)}) %collective-permute-start.27) | collective-permute-done | bytes 102432 | tf_op jit(solution)/shard_map/ppermute | solution.py:31
  72.3 1.6 %collective-permute-start.29 = (bf16[2,10,1280]{2,1,0:T(8,128)(2,1)S(1)}, bf16[2,10,1280]{2,1,0:T(8,128)(2,1)S(1)}, u32[]{:S(2)}, u32[]{:S(2)}) collective-permute-start(bf16[2,10,1280]{2,1,0:T(8,128)(2,1)S(1)} %get-tuple-element.95), channel_id=1, source_target_pairs={{0,8},{4,12},{8,0},{12,4},{1,9},{5,13},{9,1},{13,5},{2,10},{6,14},... | collective-permute-start | bytes 153608 | tf_op jit(solution)/shard_map/ppermute | solution.py:31
  73.9 1.4 %collective-permute-start.28 = (bf16[2,10,768]{2,1,0:T(8,128)(2,1)S(1)}, bf16[2,10,768]{2,1,0:T(8,128)(2,1)S(1)}, u32[]{:S(2)}, u32[]{:S(2)}) collective-permute-start(bf16[2,10,768]{2,1,0:T(8,128)(2,1)S(1)} %get-tuple-element.94), channel_id=1, source_target_pairs={{0,8},{4,12},{8,0},{12,4},{1,9},{5,13},{9,1},{13,5},{2,10},{6,14},... | collective-permute-start | bytes 92168 | tf_op jit(solution)/shard_map/ppermute | solution.py:31
  75.4 4.7 %collective-permute-done.28.refs_2_ = bf16[2,10,768]{2,1,0:T(8,128)(2,1)S(1)} collective-permute-done((bf16[2,10,768]{2,1,0:T(8,128)(2,1)S(1)}, bf16[2,10,768]{2,1,0:T(8,128)(2,1)S(1)}, u32[]{:S(2)}, u32[]{:S(2)}) %collective-permute-start.28) | collective-permute-done | bytes 30752 | tf_op jit(solution)/shard_map/ppermute | solution.py:31
  (61 shorter events, 13.0 us)
Async XLA Ops:
  0.6 9.3 %collective-permute-start = (bf16[10,2048]{1,0:T(8,128)(2,1)}, bf16[10,2048]{1,0:T(8,128)(2,1)S(1)}, u32[]{:S(2)}, u32[]{:S(2)}) collective-permute-start(bf16[10,2048]{1,0:T(8,128)(2,1)} %refs_0_.5), channel_id=1, source_target_pairs={{0,8},{4,12},{8,0},{12,4},{1,9},{5,13},{9,1},{13,5},{2,10},{6,14},... | collective-permute-start | bytes 122888 | tf_op jit(solution)/shard_map/ppermute | solution.py:31
  4.7 5.3 %collective-permute-start.1 = (bf16[10,2048]{1,0:T(8,128)(2,1)}, bf16[10,2048]{1,0:T(8,128)(2,1)S(1)}, u32[]{:S(2)}, u32[]{:S(2)}) collective-permute-start(bf16[10,2048]{1,0:T(8,128)(2,1)} %refs_1_.2), channel_id=1, source_target_pairs={{0,16},{16,0},{1,17},{17,1},{2,18},{18,2},{3,19},{19,3},{4,20},{20... | collective-permute-start | bytes 122888 | tf_op jit(solution)/shard_map/ppermute | solution.py:31
  10.1 8.1 %collective-permute-start.2 = (bf16[20,2048]{1,0:T(8,128)(2,1)S(1)}, bf16[20,2048]{1,0:T(8,128)(2,1)S(1)}, u32[]{:S(2)}, u32[]{:S(2)}) collective-permute-start(bf16[20,2048]{1,0:T(8,128)(2,1)S(1)} %get-tuple-element.49.refs_2_.refs_0_), channel_id=1, source_target_pairs={{0,4},{4,0},{8,12},{12,8},{1,5},{5,1},{9,13},{13,9},{2,6},{6,2},{1... | collective-permute-start | bytes 245768 | tf_op jit(solution)/shard_map/ppermute | solution.py:31
  11.7 6.6 %collective-permute-start.3 = (bf16[20,2048]{1,0:T(8,128)(2,1)S(1)}, bf16[20,2048]{1,0:T(8,128)(2,1)S(1)}, u32[]{:S(2)}, u32[]{:S(2)}) collective-permute-start(bf16[20,2048]{1,0:T(8,128)(2,1)S(1)} %get-tuple-element.50.refs_3_.refs_1_), channel_id=1, source_target_pairs={{0,8},{4,12},{8,0},{12,4},{1,9},{5,13},{9,1},{13,5},{2,10},{6,14},... | collective-permute-start | bytes 245768 | tf_op jit(solution)/shard_map/ppermute | solution.py:31
  18.4 5.4 %collective-permute-start.5 = (bf16[40,2048]{1,0:T(8,128)(2,1)S(1)}, bf16[40,2048]{1,0:T(8,128)(2,1)S(1)}, u32[]{:S(2)}, u32[]{:S(2)}) collective-permute-start(bf16[40,2048]{1,0:T(8,128)(2,1)S(1)} %get-tuple-element.54.refs_2_.refs_0_.refs_1_), channel_id=1, source_target_pairs={{0,4},{4,0},{8,12},{12,8},{1,5},{5,1},{9,13},{13,9},{2,6},{6,2},{1... | collective-permute-start | bytes 491528 | tf_op jit(solution)/shard_map/ppermute | solution.py:31
  18.5 8.7 %collective-permute-start.4 = (bf16[40,2048]{1,0:T(8,128)(2,1)S(1)}, bf16[40,2048]{1,0:T(8,128)(2,1)S(1)}, u32[]{:S(2)}, u32[]{:S(2)}) collective-permute-start(bf16[40,2048]{1,0:T(8,128)(2,1)S(1)} %get-tuple-element.53.refs_1_.refs_0_), channel_id=1, source_target_pairs={{0,16},{16,0},{1,17},{17,1},{2,18},{18,2},{3,19},{19,3},{4,20},{20... | collective-permute-start | bytes 491528 | tf_op jit(solution)/shard_map/ppermute | solution.py:31
  27.1 4.2 %collective-permute-start.8 = (f32[40,1792]{1,0:T(8,128)S(1)}, f32[40,1792]{1,0:T(8,128)S(1)}, u32[]{:S(2)}, u32[]{:S(2)}) collective-permute-start(f32[40,1792]{1,0:T(8,128)S(1)} %get-tuple-element.62), channel_id=1, source_target_pairs={{0,1},{1,0},{2,3},{3,2},{4,5},{5,4},{6,7},{7,6},{8,9},{9,8},{10,11... | collective-permute-start | bytes 860168 | tf_op jit(solution)/shard_map/ppermute | solution.py:31
  30.7 1.8 %collective-permute-start.6 = (f32[40,1792]{1,0:T(8,128)S(1)}, f32[40,1792]{1,0:T(8,128)S(1)}, u32[]{:S(2)}, u32[]{:S(2)}) collective-permute-start(f32[40,1792]{1,0:T(8,128)S(1)} %get-tuple-element.60), channel_id=1, source_target_pairs={{0,1},{1,0},{2,3},{3,2},{4,5},{5,4},{6,7},{7,6},{8,9},{9,8},{10,11... | collective-permute-start | bytes 860168 | tf_op jit(solution)/shard_map/ppermute | solution.py:31
  31.3 1.6 %collective-permute-start.7 = (f32[40,1792]{1,0:T(8,128)S(1)}, f32[40,1792]{1,0:T(8,128)S(1)}, u32[]{:S(2)}, u32[]{:S(2)}) collective-permute-start(f32[40,1792]{1,0:T(8,128)S(1)} %get-tuple-element.61), channel_id=1, source_target_pairs={{0,1},{1,0},{2,3},{3,2},{4,5},{5,4},{6,7},{7,6},{8,9},{9,8},{10,11... | collective-permute-start | bytes 860168 | tf_op jit(solution)/shard_map/ppermute | solution.py:31
  33.0 12.4 %collective-permute-start.17 = (bf16[3,40,1792]{2,1,0:T(8,128)(2,1)S(1)}, bf16[3,40,1792]{2,1,0:T(8,128)(2,1)S(1)}, u32[]{:S(2)}, u32[]{:S(2)}) collective-permute-start(bf16[3,40,1792]{2,1,0:T(8,128)(2,1)S(1)} %get-tuple-element.63.refs_7_), channel_id=1, source_target_pairs={{0,2},{1,3},{2,0},{3,1},{4,6},{5,7},{6,4},{7,5},{8,10},{9,11},{10,... | collective-permute-start | bytes 1290248 | tf_op jit(solution)/shard_map/ppermute | solution.py:31
  39.7 2.3 %collective-permute-start.9 = (f32[24,1536]{1,0:T(8,128)S(1)}, f32[24,1536]{1,0:T(8,128)S(1)}, u32[]{:S(2)}, u32[]{:S(2)}) collective-permute-start(f32[24,1536]{1,0:T(8,128)S(1)} %get-tuple-element.67), channel_id=1, source_target_pairs={{0,1},{1,0},{2,3},{3,2},{4,5},{5,4},{6,7},{7,6},{8,9},{9,8},{10,11... | collective-permute-start | bytes 442376 | tf_op jit(solution)/shard_map/ppermute | solution.py:31
  39.8 2.2 %collective-permute-start.11 = (f32[24,1536]{1,0:T(8,128)S(1)}, f32[24,1536]{1,0:T(8,128)S(1)}, u32[]{:S(2)}, u32[]{:S(2)}) collective-permute-start(f32[24,1536]{1,0:T(8,128)S(1)} %get-tuple-element.69), channel_id=1, source_target_pairs={{0,1},{1,0},{2,3},{3,2},{4,5},{5,4},{6,7},{7,6},{8,9},{9,8},{10,11... | collective-permute-start | bytes 442376 | tf_op jit(solution)/shard_map/ppermute | solution.py:31
  40.5 1.5 %collective-permute-start.13 = (f32[24,1536]{1,0:T(8,128)S(1)}, f32[24,1536]{1,0:T(8,128)S(1)}, u32[]{:S(2)}, u32[]{:S(2)}) collective-permute-start(f32[24,1536]{1,0:T(8,128)S(1)} %get-tuple-element.71), channel_id=1, source_target_pairs={{0,1},{1,0},{2,3},{3,2},{4,5},{5,4},{6,7},{7,6},{8,9},{9,8},{10,11... | collective-permute-start | bytes 442376 | tf_op jit(solution)/shard_map/ppermute | solution.py:31
  42.2 11.7 %collective-permute-start.15 = (bf16[3,40,768]{2,1,0:T(8,128)(2,1)S(1)}, bf16[3,40,768]{2,1,0:T(8,128)(2,1)S(1)}, u32[]{:S(2)}, u32[]{:S(2)}) collective-permute-start(bf16[3,40,768]{2,1,0:T(8,128)(2,1)S(1)} %get-tuple-element.75.refs_2_), channel_id=1, source_target_pairs={{0,2},{1,3},{2,0},{3,1},{4,6},{5,7},{6,4},{7,5},{8,10},{9,11},{10,... | collective-permute-start | bytes 552968 | tf_op jit(solution)/shard_map/ppermute | solution.py:31
  42.8 11.1 %collective-permute-start.16 = (bf16[3,40,768]{2,1,0:T(8,128)(2,1)S(1)}, bf16[3,40,768]{2,1,0:T(8,128)(2,1)S(1)}, u32[]{:S(2)}, u32[]{:S(2)}) collective-permute-start(bf16[3,40,768]{2,1,0:T(8,128)(2,1)S(1)} %get-tuple-element.76.refs_3_), channel_id=1, source_target_pairs={{0,2},{1,3},{2,0},{3,1},{4,6},{5,7},{6,4},{7,5},{8,10},{9,11},{10,... | collective-permute-start | bytes 552968 | tf_op jit(solution)/shard_map/ppermute | solution.py:31
  45.6 1.5 %collective-permute-start.18 = (bf16[48,1792]{1,0:T(8,128)(2,1)S(1)}, bf16[48,1792]{1,0:T(8,128)(2,1)S(1)}, u32[]{:S(2)}, u32[]{:S(2)}) collective-permute-start(bf16[48,1792]{1,0:T(8,128)(2,1)S(1)} %get-tuple-element.78.rest_0_), channel_id=1, source_target_pairs={{0,1},{1,0},{2,3},{3,2},{4,5},{5,4},{6,7},{7,6},{8,9},{9,8},{10,11... | collective-permute-start | bytes 516104 | tf_op jit(solution)/shard_map/ppermute | solution.py:31
  45.7 1.6 %collective-permute-start.19 = (bf16[48,1792]{1,0:T(8,128)(2,1)S(1)}, bf16[48,1792]{1,0:T(8,128)(2,1)S(1)}, u32[]{:S(2)}, u32[]{:S(2)}) collective-permute-start(bf16[48,1792]{1,0:T(8,128)(2,1)S(1)} %get-tuple-element.79.rest_1_), channel_id=1, source_target_pairs={{0,1},{1,0},{2,3},{3,2},{4,5},{5,4},{6,7},{7,6},{8,9},{9,8},{10,11... | collective-permute-start | bytes 516104 | tf_op jit(solution)/shard_map/ppermute | solution.py:31
  54.1 1.4 %collective-permute-start.21 = (bf16[48,1536]{1,0:T(8,128)(2,1)S(1)}, bf16[48,1536]{1,0:T(8,128)(2,1)S(1)}, u32[]{:S(2)}, u32[]{:S(2)}) collective-permute-start(bf16[48,1536]{1,0:T(8,128)(2,1)S(1)} %get-tuple-element.81.rest_0_), channel_id=1, source_target_pairs={{0,1},{1,0},{2,3},{3,2},{4,5},{5,4},{6,7},{7,6},{8,9},{9,8},{10,11... | collective-permute-start | bytes 442376 | tf_op jit(solution)/shard_map/ppermute | solution.py:31
  59.7 7.5 %collective-permute-start.26 = (bf16[2,40,1280]{2,1,0:T(8,128)(2,1)S(1)}, bf16[2,40,1280]{2,1,0:T(8,128)(2,1)S(1)}, u32[]{:S(2)}, u32[]{:S(2)}) collective-permute-start(bf16[2,40,1280]{2,1,0:T(8,128)(2,1)S(1)} %get-tuple-element.86.rest_0_), channel_id=1, source_target_pairs={{0,4},{4,0},{8,12},{12,8},{1,5},{5,1},{9,13},{13,9},{2,6},{6,2},{1... | collective-permute-start | bytes 614408 | tf_op jit(solution)/shard_map/ppermute | solution.py:31
  64.1 5.3 %collective-permute-start.24 = (bf16[2,40,768]{2,1,0:T(8,128)(2,1)S(1)}, bf16[2,40,768]{2,1,0:T(8,128)(2,1)S(1)}, u32[]{:S(2)}, u32[]{:S(2)}) collective-permute-start(bf16[2,40,768]{2,1,0:T(8,128)(2,1)S(1)} %get-tuple-element.85), channel_id=1, source_target_pairs={{0,16},{16,0},{1,17},{17,1},{2,18},{18,2},{3,19},{19,3},{4,20},{20... | collective-permute-start | bytes 368648 | tf_op jit(solution)/shard_map/ppermute | solution.py:31
  67.3 5.0 %collective-permute-start.27 = (bf16[2,20,1280]{2,1,0:T(8,128)(2,1)S(1)}, bf16[2,20,1280]{2,1,0:T(8,128)(2,1)S(1)}, u32[]{:S(2)}, u32[]{:S(2)}) collective-permute-start(bf16[2,20,1280]{2,1,0:T(8,128)(2,1)S(1)} %get-tuple-element.92), channel_id=1, source_target_pairs={{0,16},{16,0},{1,17},{17,1},{2,18},{18,2},{3,19},{19,3},{4,20},{20... | collective-permute-start | bytes 307208 | tf_op jit(solution)/shard_map/ppermute | solution.py:31
  69.4 4.5 %collective-permute-start.25 = (bf16[2,20,768]{2,1,0:T(8,128)(2,1)S(1)}, bf16[2,20,768]{2,1,0:T(8,128)(2,1)S(1)}, u32[]{:S(2)}, u32[]{:S(2)}) collective-permute-start(bf16[2,20,768]{2,1,0:T(8,128)(2,1)S(1)} %get-tuple-element.88), channel_id=1, source_target_pairs={{0,4},{4,0},{8,12},{12,8},{1,5},{5,1},{9,13},{13,9},{2,6},{6,2},{1... | collective-permute-start | bytes 184328 | tf_op jit(solution)/shard_map/ppermute | solution.py:31
  72.3 7.7 %collective-permute-start.29 = (bf16[2,10,1280]{2,1,0:T(8,128)(2,1)S(1)}, bf16[2,10,1280]{2,1,0:T(8,128)(2,1)S(1)}, u32[]{:S(2)}, u32[]{:S(2)}) collective-permute-start(bf16[2,10,1280]{2,1,0:T(8,128)(2,1)S(1)} %get-tuple-element.95), channel_id=1, source_target_pairs={{0,8},{4,12},{8,0},{12,4},{1,9},{5,13},{9,1},{13,5},{2,10},{6,14},... | collective-permute-start | bytes 153608 | tf_op jit(solution)/shard_map/ppermute | solution.py:31
  73.9 6.1 %collective-permute-start.28 = (bf16[2,10,768]{2,1,0:T(8,128)(2,1)S(1)}, bf16[2,10,768]{2,1,0:T(8,128)(2,1)S(1)}, u32[]{:S(2)}, u32[]{:S(2)}) collective-permute-start(bf16[2,10,768]{2,1,0:T(8,128)(2,1)S(1)} %get-tuple-element.94), channel_id=1, source_target_pairs={{0,8},{4,12},{8,0},{12,4},{1,9},{5,13},{9,1},{13,5},{2,10},{6,14},... | collective-permute-start | bytes 92168 | tf_op jit(solution)/shard_map/ppermute | solution.py:31
  (8 other events, 15.6 us)

commit v7 on v6

--- a/solution.py
+++ b/solution.py
@@ -18,7 +18,6 @@
 FIRST = 0.54
 EST = 1
 PARTS = [1, 2]
-ORDER = 0
 SPLITS = [0.38]
 SENDS = [1, 2]
 VMEM = pl.BlockSpec(memory_space=pltpu.VMEM)
@@ -223,10 +222,9 @@
                 top = 0
                 for got in refs[n + i * m : n + (i + 1) * m]:
                     run = slice(top, top + got.shape[0])
-                    value = refs[i][run, at] + got[:, at]
-                    outs[2 * k][i, run] = value
-                    outs[2 * k + 1][i, run] = value.astype(BF16)
+                    outs[2 * k][i, run] = refs[i][run, at] + got[:, at]
                     top += got.shape[0]
+                outs[2 * k + 1][i] = outs[2 * k][i].astype(BF16)
 
     outs = call(
         kernel,
@@ -410,7 +408,7 @@
         return [n for n, _ in found], [w for _, w in found]
 
     n = len(hops)
-    orders = (list(range(n)), [[n - 1, *range(n - 1)], [0, n - 1, *range(1, n - 1)]][ORDER])
+    orders = (list(range(n)), [n - 1, *range(n - 1)])
     near, far = [tokens, cotangent], [None, None]
     after = []
     for step in range(n):

time: 80.9 us -> 80.9 us (level)
  no operation moved by 1% of the time
where the time goes in v7:
time: 80.9 us; the launch traced here: 80.7 us
  Pallas kernels  38 us (47%)
  starting transfers between devices  24.7 us (31%)
  waiting for transfers between devices  17 us (21%)
  between operations  0.85 us (1%)
    ppermute x30, starting transfers between devices, swap(): return lax.ppermute(value, axis, [(i, i ^ bit) for i in range(size)])  24.7 us
    ppermute x30, waiting for transfers between devices, swap(): return lax.ppermute(value, axis, [(i, i ^ bit) for i in range(size)])  17 us
    pallas_call x3, Pallas kernels, fetch(): call(kernel, 'fetch', [SMEM] + [HBM] * n + [ANY] * len(after), outs, [plt...  12.7 us
    pallas_call x3, Pallas kernels, down(): call(kernel, 'down', [SMEM] + [VMEM] * (9 + len(prev)), shapes, [pltpu.VM...  12.3 us
    pallas_call x3, Pallas kernels, up(): call(kernel, 'up', [SMEM] + [VMEM] * (2 * n + k) + [HBM] * m + [ANY] * le...  11.4 us
  transfers between devices with their start and end apart: 30, of which 16 were waited for; matrix products, arithmetic and copies ran while one was open for 0% of the time, Pallas kernels for 41%

profile of v7, /device:TPU:0, one launch (start us, length us, event | category | flops | bytes accessed | tf_op | source)
XLA Modules:
  0.0 80.7 jit_solution(8963565279408332046)
XLA Ops:
  0.6 4.1 %collective-permute-start = (bf16[10,2048]{1,0:T(8,128)(2,1)}, bf16[10,2048]{1,0:T(8,128)(2,1)S(1)}, u32[]{:S(2)}, u32[]{:S(2)}) collective-permute-start(bf16[10,2048]{1,0:T(8,128)(2,1)} %refs_0_.5), channel_id=1, source_target_pairs={{0,8},{4,12},{8,0},{12,4},{1,9},{5,13},{9,1},{13,5},{2,10},{6,14},... | collective-permute-start | bytes 122888 | tf_op jit(solution)/shard_map/ppermute | solution.py:30
  4.7 1.5 %collective-permute-start.1 = (bf16[10,2048]{1,0:T(8,128)(2,1)}, bf16[10,2048]{1,0:T(8,128)(2,1)S(1)}, u32[]{:S(2)}, u32[]{:S(2)}) collective-permute-start(bf16[10,2048]{1,0:T(8,128)(2,1)} %refs_1_.2), channel_id=1, source_target_pairs={{0,16},{16,0},{1,17},{17,1},{2,18},{18,2},{3,19},{19,3},{4,20},{20... | collective-permute-start | bytes 122888 | tf_op jit(solution)/shard_map/ppermute | solution.py:30
  6.3 3.6 %fetch.3.refs_4_.refs_2_.rest_6_ = bf16[2048,1792]{1,0:T(8,128)(2,1)S(1)} custom-call(s32[2]{0:T(128)S(1)} %pad_add_fusion.where, bf16[2048,6656]{1,0:T(8,128)(2,1)} %refs_1_.3), custom_call_target="tpu_custom_call" | custom-call | bytes 7340032 | tf_op jit(solution)/shard_map/fetch/pallas_call | solution.py:94
  10.1 1.6 %collective-permute-start.2 = (bf16[20,2048]{1,0:T(8,128)(2,1)S(1)}, bf16[20,2048]{1,0:T(8,128)(2,1)S(1)}, u32[]{:S(2)}, u32[]{:S(2)}) collective-permute-start(bf16[20,2048]{1,0:T(8,128)(2,1)S(1)} %get-tuple-element.49.refs_2_.refs_0_), channel_id=1, source_target_pairs={{0,4},{4,0},{8,12},{12,8},{1,5},{5,1},{9,13},{13,9},{2,6},{6,2},{1... | collective-permute-start | bytes 245768 | tf_op jit(solution)/shard_map/ppermute | solution.py:30
  12.7 5.5 %fetch.4 = (bf16[2048,1792]{1,0:T(8,128)(2,1)S(1)}, bf16[2048,1536]{1,0:T(8,128)(2,1)S(1)}) custom-call(s32[2]{0:T(128)S(1)} %pad_add_fusion.where, bf16[2048,6656]{1,0:T(8,128)(2,1)} %refs_3_.1, bf16[2048,6656]{1,0:T(8,128)(2,1)} %refs_1_.3, bf16[20,2048]{1,0:T(8,128)(2,1)S(1)} %get-tuple-element.49.refs_2_.refs_0_, ...), custom_call_target="tpu_custom_call" | custom-call | bytes 13631488 | tf_op jit(solution)/shard_map/fetch/pallas_call | solution.py:94
  18.5 1.7 %collective-permute-start.4 = (bf16[40,2048]{1,0:T(8,128)(2,1)S(1)}, bf16[40,2048]{1,0:T(8,128)(2,1)S(1)}, u32[]{:S(2)}, u32[]{:S(2)}) collective-permute-start(bf16[40,2048]{1,0:T(8,128)(2,1)S(1)} %get-tuple-element.53.refs_1_.refs_0_), channel_id=1, source_target_pairs={{0,16},{16,0},{1,17},{17,1},{2,18},{18,2},{3,19},{19,3},{4,20},{20... | collective-permute-start | bytes 491528 | tf_op jit(solution)/shard_map/ppermute | solution.py:30
  20.1 3.6 %fetch.5.refs_2_.rest_8_ = bf16[1792,2048]{1,0:T(8,128)(2,1)S(1)} custom-call(s32[2]{0:T(128)S(1)} %pad_add_fusion.where, bf16[6656,2048]{1,0:T(8,128)(2,1)} %refs_4_.1, bf16[40,2048]{1,0:T(8,128)(2,1)S(1)} %get-tuple-element.53.refs_1_.refs_0_, bf16[40,2048]{1,0:T(8,128)(2,1)S(1)} %get-tuple-element.54.refs_2_.refs_0_.refs_1_), custom_call_target="tpu_custom_call" | custom-call | bytes 7340032 | tf_op jit(solution)/shard_map/fetch/pallas_call | solution.py:94
  23.8 3.3 %up.3 = (f32[40,1792]{1,0:T(8,128)S(1)}, f32[40,1792]{1,0:T(8,128)S(1)}, bf16[2048,1536]{1,0:T(8,128)(2,1)S(1)}) custom-call(s32[2]{0:T(128)S(1)} %pad_add_fusion.where, bf16[40,2048]{1,0:T(8,128)(2,1)S(1)} %get-tuple-element.54.refs_2_.refs_0_.refs_1_, bf16[40,2048]{1,0:T(8,128)(2,1)S(1)} %collective-permute-done.5.refs_1_.refs_3_, ...), custom_call_target="tpu_custom_call" | custom-call | flops 1879048192 | bytes 7340032 | tf_op jit(solution)/shard_map/up/pallas_call | solution.py:192
  27.2 3.5 %up.4 = (f32[40,1792]{1,0:T(8,128)S(1)}, f32[40,1792]{1,0:T(8,128)S(1)}, f32[40,1792]{1,0:T(8,128)S(1)}, f32[40,1792]{1,0:T(8,128)S(1)}, bf16[1536,2048]{1,0:T(8,128)(2,1)S(1)}) custom-call(s32[2]{0:T(128)S(1)} %pad_add_fusion.where, bf16[40,2048]{1,0:T(8,128)(2,1)S(1)} %get-tuple-element.53.refs_1_.refs_0_, ...), custom_call_target="tpu_custom_call" | custom-call | flops 3758096384 | bytes 14680064 | tf_op jit(solution)/shard_map/up/pallas_call | solution.py:192
  31.4 1.1 %collective-permute-done.6.refs_3_ = f32[40,1792]{1,0:T(8,128)S(1)} collective-permute-done((f32[40,1792]{1,0:T(8,128)S(1)}, f32[40,1792]{1,0:T(8,128)S(1)}, u32[]{:S(2)}, u32[]{:S(2)}) %collective-permute-start.6) | collective-permute-done | bytes 286752 | tf_op jit(solution)/shard_map/ppermute | solution.py:30
  33.0 1.6 %collective-permute-start.17 = (bf16[3,40,1792]{2,1,0:T(8,128)(2,1)S(1)}, bf16[3,40,1792]{2,1,0:T(8,128)(2,1)S(1)}, u32[]{:S(2)}, u32[]{:S(2)}) collective-permute-start(bf16[3,40,1792]{2,1,0:T(8,128)(2,1)S(1)} %get-tuple-element.63.refs_7_), channel_id=1, source_target_pairs={{0,2},{1,3},{2,0},{3,1},{4,6},{5,7},{6,4},{7,5},{8,10},{9,11},{10,... | collective-permute-start | bytes 1290248 | tf_op jit(solution)/shard_map/ppermute | solution.py:30
  34.6 4.5 %up.5 = (f32[40,1536]{1,0:T(8,128)S(1)}, f32[24,1536]{1,0:T(8,128)S(1)}, f32[16,1536]{1,0:T(8,128)S(1)}, f32[40,1536]{1,0:T(8,128)S(1)}, f32[24,1536]{1,0:T(8,12...) custom-call(s32[2]{0:T(128)S(1)} %pad_add_fusion.where, ...), custom_call_target="tpu_custom_call" | custom-call | flops 4831838208 | bytes 18874368 | tf_op jit(solution)/shard_map/up/pallas_call | solution.py:192
  42.7 1.5 %collective-permute-start.16 = (bf16[3,40,768]{2,1,0:T(8,128)(2,1)S(1)}, bf16[3,40,768]{2,1,0:T(8,128)(2,1)S(1)}, u32[]{:S(2)}, u32[]{:S(2)}) collective-permute-start(bf16[3,40,768]{2,1,0:T(8,128)(2,1)S(1)} %get-tuple-element.76.refs_3_), channel_id=1, source_target_pairs={{0,2},{1,3},{2,0},{3,1},{4,6},{5,7},{6,4},{7,5},{8,10},{9,11},{10,... | collective-permute-start | bytes 552968 | tf_op jit(solution)/shard_map/ppermute | solution.py:30
  44.2 1.2 %collective-permute-done.17.refs_1_ = bf16[3,40,1792]{2,1,0:T(8,128)(2,1)S(1)} collective-permute-done((bf16[3,40,1792]{2,1,0:T(8,128)(2,1)S(1)}, bf16[3,40,1792]{2,1,0:T(8,128)(2,1)S(1)}, u32[]{:S(2)}, u32[]{:S(2)}) %collective-permute-start.17) | collective-permute-done | bytes 430112 | tf_op jit(solution)/shard_map/ppermute | solution.py:30
  47.6 6.2 %down.3.refs_4_.rest_9_ = f32[2,96,2048]{2,1,0:T(8,128)S(1)} custom-call(s32[2]{0:T(128)S(1)} %pad_add_fusion.where, bf16[48,1792]{1,0:T(8,128)(2,1)S(1)} %get-tuple-element.78.rest_0_, bf16[48,1792]{1,0:T(8,128)(2,1)S(1)} %get-tuple-element.79.rest_1_, bf16[48,1792]{1,0:T(8,128)(2,1)S(1)} %get-tuple-element.80.rest_2_, ...), custom_call_target="tpu_custom_call" | custom-call | flops 1 | bytes 1 | tf_op jit(solution)/shard_map/down/pallas_call | solution.py:328
  56.0 3.6 %down.5 = (f32[2,40,1280]{2,1,0:T(8,128)S(1)}, bf16[2,40,1280]{2,1,0:T(8,128)(2,1)S(1)}) custom-call(s32[2]{0:T(128)S(1)} %pad_add_fusion.where, bf16[48,1536]{1,0:T(8,128)(2,1)S(1)} %get-tuple-element.81.rest_0_, bf16[48,1536]{1,0:T(8,128)(2,1)S(1)} %get-tuple-element.82.rest_1_, bf16[48,1536]{1,0:T(8,128)(2,1)S(1)} %get-tuple-element.83.rest_2_, ...), custom_call_target="tpu_custom_call" | custom-call | flops 3019898880 | bytes 11796480 | tf_op jit(solution)/shard_map/down/pallas_call | solution.py:328
  59.7 2.0 %collective-permute-start.26 = (bf16[2,40,1280]{2,1,0:T(8,128)(2,1)S(1)}, bf16[2,40,1280]{2,1,0:T(8,128)(2,1)S(1)}, u32[]{:S(2)}, u32[]{:S(2)}) collective-permute-start(bf16[2,40,1280]{2,1,0:T(8,128)(2,1)S(1)} %get-tuple-element.86.rest_0_), channel_id=1, source_target_pairs={{0,4},{4,0},{8,12},{12,8},{1,5},{5,1},{9,13},{13,9},{2,6},{6,2},{1... | collective-permute-start | bytes 614408 | tf_op jit(solution)/shard_map/ppermute | solution.py:30
  61.7 2.4 %down.4 = (f32[2,40,768]{2,1,0:T(8,128)S(1)}, bf16[2,40,768]{2,1,0:T(8,128)(2,1)S(1)}) custom-call(s32[2]{0:T(128)S(1)} %pad_add_fusion.where, bf16[48,1536]{1,0:T(8,128)(2,1)S(1)} %get-tuple-element.81.rest_0_, bf16[48,1536]{1,0:T(8,128)(2,1)S(1)} %get-tuple-element.82.rest_1_, bf16[48,1536]{1,0:T(8,128)(2,1)S(1)} %get-tuple-element.83.rest_2_, ...), custom_call_target="tpu_custom_call" | custom-call | flops 1811939328 | bytes 7077888 | tf_op jit(solution)/shard_map/down/pallas_call | solution.py:328
  64.6 2.6 %collective-permute-done.26.got = bf16[2,40,1280]{2,1,0:T(8,128)(2,1)S(1)} collective-permute-done((bf16[2,40,1280]{2,1,0:T(8,128)(2,1)S(1)}, bf16[2,40,1280]{2,1,0:T(8,128)(2,1)S(1)}, u32[]{:S(2)}, u32[]{:S(2)}) %collective-permute-start.26) | collective-permute-done | bytes 204832 | tf_op jit(solution)/shard_map/ppermute | solution.py:30
  67.3 1.4 %collective-permute-start.27 = (bf16[2,20,1280]{2,1,0:T(8,128)(2,1)S(1)}, bf16[2,20,1280]{2,1,0:T(8,128)(2,1)S(1)}, u32[]{:S(2)}, u32[]{:S(2)}) collective-permute-start(bf16[2,20,1280]{2,1,0:T(8,128)(2,1)S(1)} %get-tuple-element.92), channel_id=1, source_target_pairs={{0,16},{16,0},{1,17},{17,1},{2,18},{18,2},{3,19},{19,3},{4,20},{20... | collective-permute-start | bytes 307208 | tf_op jit(solution)/shard_map/ppermute | solution.py:30
  69.8 2.5 %collective-permute-done.27.got = bf16[2,20,1280]{2,1,0:T(8,128)(2,1)S(1)} collective-permute-done((bf16[2,20,1280]{2,1,0:T(8,128)(2,1)S(1)}, bf16[2,20,1280]{2,1,0:T(8,128)(2,1)S(1)}, u32[]{:S(2)}, u32[]{:S(2)}) %collective-permute-start.27) | collective-permute-done | bytes 102432 | tf_op jit(solution)/shard_map/ppermute | solution.py:30
  72.3 1.6 %collective-permute-start.29 = (bf16[2,10,1280]{2,1,0:T(8,128)(2,1)S(1)}, bf16[2,10,1280]{2,1,0:T(8,128)(2,1)S(1)}, u32[]{:S(2)}, u32[]{:S(2)}) collective-permute-start(bf16[2,10,1280]{2,1,0:T(8,128)(2,1)S(1)} %get-tuple-element.95), channel_id=1, source_target_pairs={{0,8},{4,12},{8,0},{12,4},{1,9},{5,13},{9,1},{13,5},{2,10},{6,14},... | collective-permute-start | bytes 153608 | tf_op jit(solution)/shard_map/ppermute | solution.py:30
  73.9 1.4 %collective-permute-start.28 = (bf16[2,10,768]{2,1,0:T(8,128)(2,1)S(1)}, bf16[2,10,768]{2,1,0:T(8,128)(2,1)S(1)}, u32[]{:S(2)}, u32[]{:S(2)}) collective-permute-start(bf16[2,10,768]{2,1,0:T(8,128)(2,1)S(1)} %get-tuple-element.94), channel_id=1, source_target_pairs={{0,8},{4,12},{8,0},{12,4},{1,9},{5,13},{9,1},{13,5},{2,10},{6,14},... | collective-permute-start | bytes 92168 | tf_op jit(solution)/shard_map/ppermute | solution.py:30
  75.3 4.7 %collective-permute-done.28.refs_2_ = bf16[2,10,768]{2,1,0:T(8,128)(2,1)S(1)} collective-permute-done((bf16[2,10,768]{2,1,0:T(8,128)(2,1)S(1)}, bf16[2,10,768]{2,1,0:T(8,128)(2,1)S(1)}, u32[]{:S(2)}, u32[]{:S(2)}) %collective-permute-start.28) | collective-permute-done | bytes 30752 | tf_op jit(solution)/shard_map/ppermute | solution.py:30
  (61 shorter events, 12.9 us)
Async XLA Ops:
  0.6 9.3 %collective-permute-start = (bf16[10,2048]{1,0:T(8,128)(2,1)}, bf16[10,2048]{1,0:T(8,128)(2,1)S(1)}, u32[]{:S(2)}, u32[]{:S(2)}) collective-permute-start(bf16[10,2048]{1,0:T(8,128)(2,1)} %refs_0_.5), channel_id=1, source_target_pairs={{0,8},{4,12},{8,0},{12,4},{1,9},{5,13},{9,1},{13,5},{2,10},{6,14},... | collective-permute-start | bytes 122888 | tf_op jit(solution)/shard_map/ppermute | solution.py:30
  4.7 5.3 %collective-permute-start.1 = (bf16[10,2048]{1,0:T(8,128)(2,1)}, bf16[10,2048]{1,0:T(8,128)(2,1)S(1)}, u32[]{:S(2)}, u32[]{:S(2)}) collective-permute-start(bf16[10,2048]{1,0:T(8,128)(2,1)} %refs_1_.2), channel_id=1, source_target_pairs={{0,16},{16,0},{1,17},{17,1},{2,18},{18,2},{3,19},{19,3},{4,20},{20... | collective-permute-start | bytes 122888 | tf_op jit(solution)/shard_map/ppermute | solution.py:30
  10.1 8.1 %collective-permute-start.2 = (bf16[20,2048]{1,0:T(8,128)(2,1)S(1)}, bf16[20,2048]{1,0:T(8,128)(2,1)S(1)}, u32[]{:S(2)}, u32[]{:S(2)}) collective-permute-start(bf16[20,2048]{1,0:T(8,128)(2,1)S(1)} %get-tuple-element.49.refs_2_.refs_0_), channel_id=1, source_target_pairs={{0,4},{4,0},{8,12},{12,8},{1,5},{5,1},{9,13},{13,9},{2,6},{6,2},{1... | collective-permute-start | bytes 245768 | tf_op jit(solution)/shard_map/ppermute | solution.py:30
  11.7 6.6 %collective-permute-start.3 = (bf16[20,2048]{1,0:T(8,128)(2,1)S(1)}, bf16[20,2048]{1,0:T(8,128)(2,1)S(1)}, u32[]{:S(2)}, u32[]{:S(2)}) collective-permute-start(bf16[20,2048]{1,0:T(8,128)(2,1)S(1)} %get-tuple-element.50.refs_3_.refs_1_), channel_id=1, source_target_pairs={{0,8},{4,12},{8,0},{12,4},{1,9},{5,13},{9,1},{13,5},{2,10},{6,14},... | collective-permute-start | bytes 245768 | tf_op jit(solution)/shard_map/ppermute | solution.py:30
  18.4 5.4 %collective-permute-start.5 = (bf16[40,2048]{1,0:T(8,128)(2,1)S(1)}, bf16[40,2048]{1,0:T(8,128)(2,1)S(1)}, u32[]{:S(2)}, u32[]{:S(2)}) collective-permute-start(bf16[40,2048]{1,0:T(8,128)(2,1)S(1)} %get-tuple-element.54.refs_2_.refs_0_.refs_1_), channel_id=1, source_target_pairs={{0,4},{4,0},{8,12},{12,8},{1,5},{5,1},{9,13},{13,9},{2,6},{6,2},{1... | collective-permute-start | bytes 491528 | tf_op jit(solution)/shard_map/ppermute | solution.py:30
  18.5 8.7 %collective-permute-start.4 = (bf16[40,2048]{1,0:T(8,128)(2,1)S(1)}, bf16[40,2048]{1,0:T(8,128)(2,1)S(1)}, u32[]{:S(2)}, u32[]{:S(2)}) collective-permute-start(bf16[40,2048]{1,0:T(8,128)(2,1)S(1)} %get-tuple-element.53.refs_1_.refs_0_), channel_id=1, source_target_pairs={{0,16},{16,0},{1,17},{17,1},{2,18},{18,2},{3,19},{19,3},{4,20},{20... | collective-permute-start | bytes 491528 | tf_op jit(solution)/shard_map/ppermute | solution.py:30
  27.1 4.2 %collective-permute-start.8 = (f32[40,1792]{1,0:T(8,128)S(1)}, f32[40,1792]{1,0:T(8,128)S(1)}, u32[]{:S(2)}, u32[]{:S(2)}) collective-permute-start(f32[40,1792]{1,0:T(8,128)S(1)} %get-tuple-element.62), channel_id=1, source_target_pairs={{0,1},{1,0},{2,3},{3,2},{4,5},{5,4},{6,7},{7,6},{8,9},{9,8},{10,11... | collective-permute-start | bytes 860168 | tf_op jit(solution)/shard_map/ppermute | solution.py:30
  30.7 1.8 %collective-permute-start.6 = (f32[40,1792]{1,0:T(8,128)S(1)}, f32[40,1792]{1,0:T(8,128)S(1)}, u32[]{:S(2)}, u32[]{:S(2)}) collective-permute-start(f32[40,1792]{1,0:T(8,128)S(1)} %get-tuple-element.60), channel_id=1, source_target_pairs={{0,1},{1,0},{2,3},{3,2},{4,5},{5,4},{6,7},{7,6},{8,9},{9,8},{10,11... | collective-permute-start | bytes 860168 | tf_op jit(solution)/shard_map/ppermute | solution.py:30
  31.3 1.6 %collective-permute-start.7 = (f32[40,1792]{1,0:T(8,128)S(1)}, f32[40,1792]{1,0:T(8,128)S(1)}, u32[]{:S(2)}, u32[]{:S(2)}) collective-permute-start(f32[40,1792]{1,0:T(8,128)S(1)} %get-tuple-element.61), channel_id=1, source_target_pairs={{0,1},{1,0},{2,3},{3,2},{4,5},{5,4},{6,7},{7,6},{8,9},{9,8},{10,11... | collective-permute-start | bytes 860168 | tf_op jit(solution)/shard_map/ppermute | solution.py:30
  33.0 12.4 %collective-permute-start.17 = (bf16[3,40,1792]{2,1,0:T(8,128)(2,1)S(1)}, bf16[3,40,1792]{2,1,0:T(8,128)(2,1)S(1)}, u32[]{:S(2)}, u32[]{:S(2)}) collective-permute-start(bf16[3,40,1792]{2,1,0:T(8,128)(2,1)S(1)} %get-tuple-element.63.refs_7_), channel_id=1, source_target_pairs={{0,2},{1,3},{2,0},{3,1},{4,6},{5,7},{6,4},{7,5},{8,10},{9,11},{10,... | collective-permute-start | bytes 1290248 | tf_op jit(solution)/shard_map/ppermute | solution.py:30
  39.7 2.3 %collective-permute-start.9 = (f32[24,1536]{1,0:T(8,128)S(1)}, f32[24,1536]{1,0:T(8,128)S(1)}, u32[]{:S(2)}, u32[]{:S(2)}) collective-permute-start(f32[24,1536]{1,0:T(8,128)S(1)} %get-tuple-element.67), channel_id=1, source_target_pairs={{0,1},{1,0},{2,3},{3,2},{4,5},{5,4},{6,7},{7,6},{8,9},{9,8},{10,11... | collective-permute-start | bytes 442376 | tf_op jit(solution)/shard_map/ppermute | solution.py:30
  39.8 2.2 %collective-permute-start.11 = (f32[24,1536]{1,0:T(8,128)S(1)}, f32[24,1536]{1,0:T(8,128)S(1)}, u32[]{:S(2)}, u32[]{:S(2)}) collective-permute-start(f32[24,1536]{1,0:T(8,128)S(1)} %get-tuple-element.69), channel_id=1, source_target_pairs={{0,1},{1,0},{2,3},{3,2},{4,5},{5,4},{6,7},{7,6},{8,9},{9,8},{10,11... | collective-permute-start | bytes 442376 | tf_op jit(solution)/shard_map/ppermute | solution.py:30
  40.5 1.5 %collective-permute-start.13 = (f32[24,1536]{1,0:T(8,128)S(1)}, f32[24,1536]{1,0:T(8,128)S(1)}, u32[]{:S(2)}, u32[]{:S(2)}) collective-permute-start(f32[24,1536]{1,0:T(8,128)S(1)} %get-tuple-element.71), channel_id=1, source_target_pairs={{0,1},{1,0},{2,3},{3,2},{4,5},{5,4},{6,7},{7,6},{8,9},{9,8},{10,11... | collective-permute-start | bytes 442376 | tf_op jit(solution)/shard_map/ppermute | solution.py:30
  42.1 11.7 %collective-permute-start.15 = (bf16[3,40,768]{2,1,0:T(8,128)(2,1)S(1)}, bf16[3,40,768]{2,1,0:T(8,128)(2,1)S(1)}, u32[]{:S(2)}, u32[]{:S(2)}) collective-permute-start(bf16[3,40,768]{2,1,0:T(8,128)(2,1)S(1)} %get-tuple-element.75.refs_2_), channel_id=1, source_target_pairs={{0,2},{1,3},{2,0},{3,1},{4,6},{5,7},{6,4},{7,5},{8,10},{9,11},{10,... | collective-permute-start | bytes 552968 | tf_op jit(solution)/shard_map/ppermute | solution.py:30
  42.7 11.2 %collective-permute-start.16 = (bf16[3,40,768]{2,1,0:T(8,128)(2,1)S(1)}, bf16[3,40,768]{2,1,0:T(8,128)(2,1)S(1)}, u32[]{:S(2)}, u32[]{:S(2)}) collective-permute-start(bf16[3,40,768]{2,1,0:T(8,128)(2,1)S(1)} %get-tuple-element.76.refs_3_), channel_id=1, source_target_pairs={{0,2},{1,3},{2,0},{3,1},{4,6},{5,7},{6,4},{7,5},{8,10},{9,11},{10,... | collective-permute-start | bytes 552968 | tf_op jit(solution)/shard_map/ppermute | solution.py:30
  45.6 1.5 %collective-permute-start.18 = (bf16[48,1792]{1,0:T(8,128)(2,1)S(1)}, bf16[48,1792]{1,0:T(8,128)(2,1)S(1)}, u32[]{:S(2)}, u32[]{:S(2)}) collective-permute-start(bf16[48,1792]{1,0:T(8,128)(2,1)S(1)} %get-tuple-element.78.rest_0_), channel_id=1, source_target_pairs={{0,1},{1,0},{2,3},{3,2},{4,5},{5,4},{6,7},{7,6},{8,9},{9,8},{10,11... | collective-permute-start | bytes 516104 | tf_op jit(solution)/shard_map/ppermute | solution.py:30
  45.7 1.6 %collective-permute-start.19 = (bf16[48,1792]{1,0:T(8,128)(2,1)S(1)}, bf16[48,1792]{1,0:T(8,128)(2,1)S(1)}, u32[]{:S(2)}, u32[]{:S(2)}) collective-permute-start(bf16[48,1792]{1,0:T(8,128)(2,1)S(1)} %get-tuple-element.79.rest_1_), channel_id=1, source_target_pairs={{0,1},{1,0},{2,3},{3,2},{4,5},{5,4},{6,7},{7,6},{8,9},{9,8},{10,11... | collective-permute-start | bytes 516104 | tf_op jit(solution)/shard_map/ppermute | solution.py:30
  54.1 1.4 %collective-permute-start.21 = (bf16[48,1536]{1,0:T(8,128)(2,1)S(1)}, bf16[48,1536]{1,0:T(8,128)(2,1)S(1)}, u32[]{:S(2)}, u32[]{:S(2)}) collective-permute-start(bf16[48,1536]{1,0:T(8,128)(2,1)S(1)} %get-tuple-element.81.rest_0_), channel_id=1, source_target_pairs={{0,1},{1,0},{2,3},{3,2},{4,5},{5,4},{6,7},{7,6},{8,9},{9,8},{10,11... | collective-permute-start | bytes 442376 | tf_op jit(solution)/shard_map/ppermute | solution.py:30
  59.7 7.5 %collective-permute-start.26 = (bf16[2,40,1280]{2,1,0:T(8,128)(2,1)S(1)}, bf16[2,40,1280]{2,1,0:T(8,128)(2,1)S(1)}, u32[]{:S(2)}, u32[]{:S(2)}) collective-permute-start(bf16[2,40,1280]{2,1,0:T(8,128)(2,1)S(1)} %get-tuple-element.86.rest_0_), channel_id=1, source_target_pairs={{0,4},{4,0},{8,12},{12,8},{1,5},{5,1},{9,13},{13,9},{2,6},{6,2},{1... | collective-permute-start | bytes 614408 | tf_op jit(solution)/shard_map/ppermute | solution.py:30
  64.1 5.3 %collective-permute-start.24 = (bf16[2,40,768]{2,1,0:T(8,128)(2,1)S(1)}, bf16[2,40,768]{2,1,0:T(8,128)(2,1)S(1)}, u32[]{:S(2)}, u32[]{:S(2)}) collective-permute-start(bf16[2,40,768]{2,1,0:T(8,128)(2,1)S(1)} %get-tuple-element.85), channel_id=1, source_target_pairs={{0,16},{16,0},{1,17},{17,1},{2,18},{18,2},{3,19},{19,3},{4,20},{20... | collective-permute-start | bytes 368648 | tf_op jit(solution)/shard_map/ppermute | solution.py:30
  67.3 5.0 %collective-permute-start.27 = (bf16[2,20,1280]{2,1,0:T(8,128)(2,1)S(1)}, bf16[2,20,1280]{2,1,0:T(8,128)(2,1)S(1)}, u32[]{:S(2)}, u32[]{:S(2)}) collective-permute-start(bf16[2,20,1280]{2,1,0:T(8,128)(2,1)S(1)} %get-tuple-element.92), channel_id=1, source_target_pairs={{0,16},{16,0},{1,17},{17,1},{2,18},{18,2},{3,19},{19,3},{4,20},{20... | collective-permute-start | bytes 307208 | tf_op jit(solution)/shard_map/ppermute | solution.py:30
  69.4 4.5 %collective-permute-start.25 = (bf16[2,20,768]{2,1,0:T(8,128)(2,1)S(1)}, bf16[2,20,768]{2,1,0:T(8,128)(2,1)S(1)}, u32[]{:S(2)}, u32[]{:S(2)}) collective-permute-start(bf16[2,20,768]{2,1,0:T(8,128)(2,1)S(1)} %get-tuple-element.88), channel_id=1, source_target_pairs={{0,4},{4,0},{8,12},{12,8},{1,5},{5,1},{9,13},{13,9},{2,6},{6,2},{1... | collective-permute-start | bytes 184328 | tf_op jit(solution)/shard_map/ppermute | solution.py:30
  72.3 7.7 %collective-permute-start.29 = (bf16[2,10,1280]{2,1,0:T(8,128)(2,1)S(1)}, bf16[2,10,1280]{2,1,0:T(8,128)(2,1)S(1)}, u32[]{:S(2)}, u32[]{:S(2)}) collective-permute-start(bf16[2,10,1280]{2,1,0:T(8,128)(2,1)S(1)} %get-tuple-element.95), channel_id=1, source_target_pairs={{0,8},{4,12},{8,0},{12,4},{1,9},{5,13},{9,1},{13,5},{2,10},{6,14},... | collective-permute-start | bytes 153608 | tf_op jit(solution)/shard_map/ppermute | solution.py:30
  73.9 6.1 %collective-permute-start.28 = (bf16[2,10,768]{2,1,0:T(8,128)(2,1)S(1)}, bf16[2,10,768]{2,1,0:T(8,128)(2,1)S(1)}, u32[]{:S(2)}, u32[]{:S(2)}) collective-permute-start(bf16[2,10,768]{2,1,0:T(8,128)(2,1)S(1)} %get-tuple-element.94), channel_id=1, source_target_pairs={{0,8},{4,12},{8,0},{12,4},{1,9},{5,13},{9,1},{13,5},{2,10},{6,14},... | collective-permute-start | bytes 92168 | tf_op jit(solution)/shard_map/ppermute | solution.py:30
  (8 other events, 15.6 us)

commit v8 on v7

--- a/solution.py
+++ b/solution.py
@@ -11,7 +11,7 @@
 BF16 = jnp.bfloat16
 NT = (((1,), (1,)), ((), ()))
 MIB = 2**20
-WINDOWS = [["g0"], ["u0", "g1"], ["d0"]]
+WINDOWS = [["g1"], ["u0", "g0"], ["d0"]]
 BESIDE = [[["d", ["u1"]], ["gu", ["d1"]]], [["gud", []]]]
 UPLIM = 3
 INNER = True

time: 80.9 us -> 81.1 us (level)
  transfers between devices with their start and end apart: 30 -> 30, of which waited for: 16 -> 15; matrix products, arithmetic and copies ran while one was open for 0% -> 0% of each run, Pallas kernels for 41% -> 41%
where the time goes in v8:
time: 81.1 us; the launch traced here: 80.9 us
  Pallas kernels  38.1 us (47%)
  starting transfers between devices  25 us (31%)
  waiting for transfers between devices  16.9 us (21%)
  between operations  0.84 us (1%)
    ppermute x30, starting transfers between devices, swap(): return lax.ppermute(value, axis, [(i, i ^ bit) for i in range(size)])  25 us
    ppermute x30, waiting for transfers between devices, swap(): return lax.ppermute(value, axis, [(i, i ^ bit) for i in range(size)])  16.9 us
    pallas_call x3, Pallas kernels, fetch(): call(kernel, 'fetch', [SMEM] + [HBM] * n + [ANY] * len(after), outs, [plt...  12.8 us
    pallas_call x3, Pallas kernels, down(): call(kernel, 'down', [SMEM] + [VMEM] * (9 + len(prev)), shapes, [pltpu.VM...  12.3 us
    pallas_call x3, Pallas kernels, up(): call(kernel, 'up', [SMEM] + [VMEM] * (2 * n + k) + [HBM] * m + [ANY] * le...  11.4 us
  transfers between devices with their start and end apart: 30, of which 15 were waited for; matrix products, arithmetic and copies ran while one was open for 0% of the time, Pallas kernels for 41%

profile of v8, /device:TPU:0, one launch (start us, length us, event | category | flops | bytes accessed | tf_op | source)
XLA Modules:
  0.0 80.9 jit_solution(167832007516779722)
XLA Ops:
  0.6 4.1 %collective-permute-start = (bf16[10,2048]{1,0:T(8,128)(2,1)}, bf16[10,2048]{1,0:T(8,128)(2,1)S(1)}, u32[]{:S(2)}, u32[]{:S(2)}) collective-permute-start(bf16[10,2048]{1,0:T(8,128)(2,1)} %refs_0_.5), channel_id=1, source_target_pairs={{0,8},{4,12},{8,0},{12,4},{1,9},{5,13},{9,1},{13,5},{2,10},{6,14},... | collective-permute-start | bytes 122888 | tf_op jit(solution)/shard_map/ppermute | solution.py:30
  4.7 1.5 %collective-permute-start.1 = (bf16[10,2048]{1,0:T(8,128)(2,1)}, bf16[10,2048]{1,0:T(8,128)(2,1)S(1)}, u32[]{:S(2)}, u32[]{:S(2)}) collective-permute-start(bf16[10,2048]{1,0:T(8,128)(2,1)} %refs_1_.2), channel_id=1, source_target_pairs={{0,16},{16,0},{1,17},{17,1},{2,18},{18,2},{3,19},{19,3},{4,20},{20... | collective-permute-start | bytes 122888 | tf_op jit(solution)/shard_map/ppermute | solution.py:30
  6.3 3.3 %fetch.3.refs_4_.rest_6_ = bf16[2048,1536]{1,0:T(8,128)(2,1)S(1)} custom-call(s32[2]{0:T(128)S(1)} %pad_add_fusion.where, bf16[2048,6656]{1,0:T(8,128)(2,1)} %refs_1_.3), custom_call_target="tpu_custom_call" | custom-call | bytes 6291456 | tf_op jit(solution)/shard_map/fetch/pallas_call | solution.py:94
  9.8 1.6 %collective-permute-start.2 = (bf16[20,2048]{1,0:T(8,128)(2,1)S(1)}, bf16[20,2048]{1,0:T(8,128)(2,1)S(1)}, u32[]{:S(2)}, u32[]{:S(2)}) collective-permute-start(bf16[20,2048]{1,0:T(8,128)(2,1)S(1)} %get-tuple-element.49.refs_2_.refs_0_), channel_id=1, source_target_pairs={{0,4},{4,0},{8,12},{12,8},{1,5},{5,1},{9,13},{13,9},{2,6},{6,2},{1... | collective-permute-start | bytes 245768 | tf_op jit(solution)/shard_map/ppermute | solution.py:30
  11.4 1.3 %collective-permute-start.3 = (bf16[20,2048]{1,0:T(8,128)(2,1)S(1)}, bf16[20,2048]{1,0:T(8,128)(2,1)S(1)}, u32[]{:S(2)}, u32[]{:S(2)}) collective-permute-start(bf16[20,2048]{1,0:T(8,128)(2,1)S(1)} %get-tuple-element.50.refs_3_.refs_1_), channel_id=1, source_target_pairs={{0,8},{4,12},{8,0},{12,4},{1,9},{5,13},{9,1},{13,5},{2,10},{6,14},... | collective-permute-start | bytes 245768 | tf_op jit(solution)/shard_map/ppermute | solution.py:30
  12.7 5.8 %fetch.4 = (bf16[2048,1792]{1,0:T(8,128)(2,1)S(1)}, bf16[2048,1792]{1,0:T(8,128)(2,1)S(1)}) custom-call(s32[2]{0:T(128)S(1)} %pad_add_fusion.where, bf16[2048,6656]{1,0:T(8,128)(2,1)} %refs_3_.1, bf16[2048,6656]{1,0:T(8,128)(2,1)} %refs_1_.3, bf16[20,2048]{1,0:T(8,128)(2,1)S(1)} %get-tuple-element.49.refs_2_.refs_0_, ...), custom_call_target="tpu_custom_call" | custom-call | bytes 14680064 | tf_op jit(solution)/shard_map/fetch/pallas_call | solution.py:94
  18.7 1.6 %collective-permute-start.4 = (bf16[40,2048]{1,0:T(8,128)(2,1)S(1)}, bf16[40,2048]{1,0:T(8,128)(2,1)S(1)}, u32[]{:S(2)}, u32[]{:S(2)}) collective-permute-start(bf16[40,2048]{1,0:T(8,128)(2,1)S(1)} %get-tuple-element.53.refs_1_.refs_0_), channel_id=1, source_target_pairs={{0,16},{16,0},{1,17},{17,1},{2,18},{18,2},{3,19},{19,3},{4,20},{20... | collective-permute-start | bytes 491528 | tf_op jit(solution)/shard_map/ppermute | solution.py:30
  20.3 3.6 %fetch.5.refs_2_.rest_8_ = bf16[1792,2048]{1,0:T(8,128)(2,1)S(1)} custom-call(s32[2]{0:T(128)S(1)} %pad_add_fusion.where, bf16[6656,2048]{1,0:T(8,128)(2,1)} %refs_4_.1, bf16[40,2048]{1,0:T(8,128)(2,1)S(1)} %get-tuple-element.53.refs_1_.refs_0_, bf16[40,2048]{1,0:T(8,128)(2,1)S(1)} %get-tuple-element.54.refs_2_.refs_0_.refs_1_), custom_call_target="tpu_custom_call" | custom-call | bytes 7340032 | tf_op jit(solution)/shard_map/fetch/pallas_call | solution.py:94
  23.9 3.3 %up.3 = (f32[40,1792]{1,0:T(8,128)S(1)}, f32[40,1792]{1,0:T(8,128)S(1)}, bf16[2048,1536]{1,0:T(8,128)(2,1)S(1)}) custom-call(s32[2]{0:T(128)S(1)} %pad_add_fusion.where, bf16[40,2048]{1,0:T(8,128)(2,1)S(1)} %get-tuple-element.54.refs_2_.refs_0_.refs_1_, bf16[40,2048]{1,0:T(8,128)(2,1)S(1)} %collective-permute-done.5.refs_1_.refs_3_, ...), custom_call_target="tpu_custom_call" | custom-call | flops 1879048192 | bytes 7340032 | tf_op jit(solution)/shard_map/up/pallas_call | solution.py:192
  27.4 3.5 %up.4 = (f32[40,1792]{1,0:T(8,128)S(1)}, f32[40,1792]{1,0:T(8,128)S(1)}, f32[40,1792]{1,0:T(8,128)S(1)}, f32[40,1792]{1,0:T(8,128)S(1)}, bf16[1536,2048]{1,0:T(8,128)(2,1)S(1)}) custom-call(s32[2]{0:T(128)S(1)} %pad_add_fusion.where, bf16[40,2048]{1,0:T(8,128)(2,1)S(1)} %get-tuple-element.53.refs_1_.refs_0_, ...), custom_call_target="tpu_custom_call" | custom-call | flops 3758096384 | bytes 14680064 | tf_op jit(solution)/shard_map/up/pallas_call | solution.py:192
  33.2 1.6 %collective-permute-start.17 = (bf16[3,40,1792]{2,1,0:T(8,128)(2,1)S(1)}, bf16[3,40,1792]{2,1,0:T(8,128)(2,1)S(1)}, u32[]{:S(2)}, u32[]{:S(2)}) collective-permute-start(bf16[3,40,1792]{2,1,0:T(8,128)(2,1)S(1)} %get-tuple-element.63.refs_7_), channel_id=1, source_target_pairs={{0,2},{1,3},{2,0},{3,1},{4,6},{5,7},{6,4},{7,5},{8,10},{9,11},{10,... | collective-permute-start | bytes 1290248 | tf_op jit(solution)/shard_map/ppermute | solution.py:30
  34.7 4.5 %up.5 = (f32[40,1536]{1,0:T(8,128)S(1)}, f32[24,1536]{1,0:T(8,128)S(1)}, f32[16,1536]{1,0:T(8,128)S(1)}, f32[40,1536]{1,0:T(8,128)S(1)}, f32[24,1536]{1,0:T(8,12...) custom-call(s32[2]{0:T(128)S(1)} %pad_add_fusion.where, ...), custom_call_target="tpu_custom_call" | custom-call | flops 4831838208 | bytes 18874368 | tf_op jit(solution)/shard_map/up/pallas_call | solution.py:192
  42.9 1.5 %collective-permute-start.16 = (bf16[3,40,768]{2,1,0:T(8,128)(2,1)S(1)}, bf16[3,40,768]{2,1,0:T(8,128)(2,1)S(1)}, u32[]{:S(2)}, u32[]{:S(2)}) collective-permute-start(bf16[3,40,768]{2,1,0:T(8,128)(2,1)S(1)} %get-tuple-element.76.refs_3_), channel_id=1, source_target_pairs={{0,2},{1,3},{2,0},{3,1},{4,6},{5,7},{6,4},{7,5},{8,10},{9,11},{10,... | collective-permute-start | bytes 552968 | tf_op jit(solution)/shard_map/ppermute | solution.py:30
  44.4 1.2 %collective-permute-done.17.refs_1_ = bf16[3,40,1792]{2,1,0:T(8,128)(2,1)S(1)} collective-permute-done((bf16[3,40,1792]{2,1,0:T(8,128)(2,1)S(1)}, bf16[3,40,1792]{2,1,0:T(8,128)(2,1)S(1)}, u32[]{:S(2)}, u32[]{:S(2)}) %collective-permute-start.17) | collective-permute-done | bytes 430112 | tf_op jit(solution)/shard_map/ppermute | solution.py:30
  47.8 6.3 %down.3.refs_4_.rest_9_ = f32[2,96,2048]{2,1,0:T(8,128)S(1)} custom-call(s32[2]{0:T(128)S(1)} %pad_add_fusion.where, bf16[48,1792]{1,0:T(8,128)(2,1)S(1)} %get-tuple-element.78.rest_0_, bf16[48,1792]{1,0:T(8,128)(2,1)S(1)} %get-tuple-element.79.rest_1_, bf16[48,1792]{1,0:T(8,128)(2,1)S(1)} %get-tuple-element.80.rest_2_, ...), custom_call_target="tpu_custom_call" | custom-call | flops 1 | bytes 1 | tf_op jit(solution)/shard_map/down/pallas_call | solution.py:328
  56.2 3.6 %down.5 = (f32[2,40,1280]{2,1,0:T(8,128)S(1)}, bf16[2,40,1280]{2,1,0:T(8,128)(2,1)S(1)}) custom-call(s32[2]{0:T(128)S(1)} %pad_add_fusion.where, bf16[48,1536]{1,0:T(8,128)(2,1)S(1)} %get-tuple-element.81.rest_0_, bf16[48,1536]{1,0:T(8,128)(2,1)S(1)} %get-tuple-element.82.rest_1_, bf16[48,1536]{1,0:T(8,128)(2,1)S(1)} %get-tuple-element.83.rest_2_, ...), custom_call_target="tpu_custom_call" | custom-call | flops 3019898880 | bytes 11796480 | tf_op jit(solution)/shard_map/down/pallas_call | solution.py:328
  59.9 2.0 %collective-permute-start.26 = (bf16[2,40,1280]{2,1,0:T(8,128)(2,1)S(1)}, bf16[2,40,1280]{2,1,0:T(8,128)(2,1)S(1)}, u32[]{:S(2)}, u32[]{:S(2)}) collective-permute-start(bf16[2,40,1280]{2,1,0:T(8,128)(2,1)S(1)} %get-tuple-element.86.rest_0_), channel_id=1, source_target_pairs={{0,4},{4,0},{8,12},{12,8},{1,5},{5,1},{9,13},{13,9},{2,6},{6,2},{1... | collective-permute-start | bytes 614408 | tf_op jit(solution)/shard_map/ppermute | solution.py:30
  61.9 2.4 %down.4 = (f32[2,40,768]{2,1,0:T(8,128)S(1)}, bf16[2,40,768]{2,1,0:T(8,128)(2,1)S(1)}) custom-call(s32[2]{0:T(128)S(1)} %pad_add_fusion.where, bf16[48,1536]{1,0:T(8,128)(2,1)S(1)} %get-tuple-element.81.rest_0_, bf16[48,1536]{1,0:T(8,128)(2,1)S(1)} %get-tuple-element.82.rest_1_, bf16[48,1536]{1,0:T(8,128)(2,1)S(1)} %get-tuple-element.83.rest_2_, ...), custom_call_target="tpu_custom_call" | custom-call | flops 1811939328 | bytes 7077888 | tf_op jit(solution)/shard_map/down/pallas_call | solution.py:328
  64.8 2.6 %collective-permute-done.26.got = bf16[2,40,1280]{2,1,0:T(8,128)(2,1)S(1)} collective-permute-done((bf16[2,40,1280]{2,1,0:T(8,128)(2,1)S(1)}, bf16[2,40,1280]{2,1,0:T(8,128)(2,1)S(1)}, u32[]{:S(2)}, u32[]{:S(2)}) %collective-permute-start.26) | collective-permute-done | bytes 204832 | tf_op jit(solution)/shard_map/ppermute | solution.py:30
  67.4 1.4 %collective-permute-start.27 = (bf16[2,20,1280]{2,1,0:T(8,128)(2,1)S(1)}, bf16[2,20,1280]{2,1,0:T(8,128)(2,1)S(1)}, u32[]{:S(2)}, u32[]{:S(2)}) collective-permute-start(bf16[2,20,1280]{2,1,0:T(8,128)(2,1)S(1)} %get-tuple-element.92), channel_id=1, source_target_pairs={{0,16},{16,0},{1,17},{17,1},{2,18},{18,2},{3,19},{19,3},{4,20},{20... | collective-permute-start | bytes 307208 | tf_op jit(solution)/shard_map/ppermute | solution.py:30
  69.9 2.4 %collective-permute-done.27.got = bf16[2,20,1280]{2,1,0:T(8,128)(2,1)S(1)} collective-permute-done((bf16[2,20,1280]{2,1,0:T(8,128)(2,1)S(1)}, bf16[2,20,1280]{2,1,0:T(8,128)(2,1)S(1)}, u32[]{:S(2)}, u32[]{:S(2)}) %collective-permute-start.27) | collective-permute-done | bytes 102432 | tf_op jit(solution)/shard_map/ppermute | solution.py:30
  72.4 1.5 %collective-permute-start.29 = (bf16[2,10,1280]{2,1,0:T(8,128)(2,1)S(1)}, bf16[2,10,1280]{2,1,0:T(8,128)(2,1)S(1)}, u32[]{:S(2)}, u32[]{:S(2)}) collective-permute-start(bf16[2,10,1280]{2,1,0:T(8,128)(2,1)S(1)} %get-tuple-element.95), channel_id=1, source_target_pairs={{0,8},{4,12},{8,0},{12,4},{1,9},{5,13},{9,1},{13,5},{2,10},{6,14},... | collective-permute-start | bytes 153608 | tf_op jit(solution)/shard_map/ppermute | solution.py:30
  74.0 1.5 %collective-permute-start.28 = (bf16[2,10,768]{2,1,0:T(8,128)(2,1)S(1)}, bf16[2,10,768]{2,1,0:T(8,128)(2,1)S(1)}, u32[]{:S(2)}, u32[]{:S(2)}) collective-permute-start(bf16[2,10,768]{2,1,0:T(8,128)(2,1)S(1)} %get-tuple-element.94), channel_id=1, source_target_pairs={{0,8},{4,12},{8,0},{12,4},{1,9},{5,13},{9,1},{13,5},{2,10},{6,14},... | collective-permute-start | bytes 92168 | tf_op jit(solution)/shard_map/ppermute | solution.py:30
  75.5 4.7 %collective-permute-done.28.refs_2_ = bf16[2,10,768]{2,1,0:T(8,128)(2,1)S(1)} collective-permute-done((bf16[2,10,768]{2,1,0:T(8,128)(2,1)S(1)}, bf16[2,10,768]{2,1,0:T(8,128)(2,1)S(1)}, u32[]{:S(2)}, u32[]{:S(2)}) %collective-permute-start.28) | collective-permute-done | bytes 30752 | tf_op jit(solution)/shard_map/ppermute | solution.py:30
  (61 shorter events, 13.1 us)
Async XLA Ops:
  0.6 9.1 %collective-permute-start = (bf16[10,2048]{1,0:T(8,128)(2,1)}, bf16[10,2048]{1,0:T(8,128)(2,1)S(1)}, u32[]{:S(2)}, u32[]{:S(2)}) collective-permute-start(bf16[10,2048]{1,0:T(8,128)(2,1)} %refs_0_.5), channel_id=1, source_target_pairs={{0,8},{4,12},{8,0},{12,4},{1,9},{5,13},{9,1},{13,5},{2,10},{6,14},... | collective-permute-start | bytes 122888 | tf_op jit(solution)/shard_map/ppermute | solution.py:30
  4.7 5.0 %collective-permute-start.1 = (bf16[10,2048]{1,0:T(8,128)(2,1)}, bf16[10,2048]{1,0:T(8,128)(2,1)S(1)}, u32[]{:S(2)}, u32[]{:S(2)}) collective-permute-start(bf16[10,2048]{1,0:T(8,128)(2,1)} %refs_1_.2), channel_id=1, source_target_pairs={{0,16},{16,0},{1,17},{17,1},{2,18},{18,2},{3,19},{19,3},{4,20},{20... | collective-permute-start | bytes 122888 | tf_op jit(solution)/shard_map/ppermute | solution.py:30
  9.8 8.7 %collective-permute-start.2 = (bf16[20,2048]{1,0:T(8,128)(2,1)S(1)}, bf16[20,2048]{1,0:T(8,128)(2,1)S(1)}, u32[]{:S(2)}, u32[]{:S(2)}) collective-permute-start(bf16[20,2048]{1,0:T(8,128)(2,1)S(1)} %get-tuple-element.49.refs_2_.refs_0_), channel_id=1, source_target_pairs={{0,4},{4,0},{8,12},{12,8},{1,5},{5,1},{9,13},{13,9},{2,6},{6,2},{1... | collective-permute-start | bytes 245768 | tf_op jit(solution)/shard_map/ppermute | solution.py:30
  11.4 7.1 %collective-permute-start.3 = (bf16[20,2048]{1,0:T(8,128)(2,1)S(1)}, bf16[20,2048]{1,0:T(8,128)(2,1)S(1)}, u32[]{:S(2)}, u32[]{:S(2)}) collective-permute-start(bf16[20,2048]{1,0:T(8,128)(2,1)S(1)} %get-tuple-element.50.refs_3_.refs_1_), channel_id=1, source_target_pairs={{0,8},{4,12},{8,0},{12,4},{1,9},{5,13},{9,1},{13,5},{2,10},{6,14},... | collective-permute-start | bytes 245768 | tf_op jit(solution)/shard_map/ppermute | solution.py:30
  18.6 5.4 %collective-permute-start.5 = (bf16[40,2048]{1,0:T(8,128)(2,1)S(1)}, bf16[40,2048]{1,0:T(8,128)(2,1)S(1)}, u32[]{:S(2)}, u32[]{:S(2)}) collective-permute-start(bf16[40,2048]{1,0:T(8,128)(2,1)S(1)} %get-tuple-element.54.refs_2_.refs_0_.refs_1_), channel_id=1, source_target_pairs={{0,4},{4,0},{8,12},{12,8},{1,5},{5,1},{9,13},{13,9},{2,6},{6,2},{1... | collective-permute-start | bytes 491528 | tf_op jit(solution)/shard_map/ppermute | solution.py:30
  18.7 8.7 %collective-permute-start.4 = (bf16[40,2048]{1,0:T(8,128)(2,1)S(1)}, bf16[40,2048]{1,0:T(8,128)(2,1)S(1)}, u32[]{:S(2)}, u32[]{:S(2)}) collective-permute-start(bf16[40,2048]{1,0:T(8,128)(2,1)S(1)} %get-tuple-element.53.refs_1_.refs_0_), channel_id=1, source_target_pairs={{0,16},{16,0},{1,17},{17,1},{2,18},{18,2},{3,19},{19,3},{4,20},{20... | collective-permute-start | bytes 491528 | tf_op jit(solution)/shard_map/ppermute | solution.py:30
  27.3 4.2 %collective-permute-start.8 = (f32[40,1792]{1,0:T(8,128)S(1)}, f32[40,1792]{1,0:T(8,128)S(1)}, u32[]{:S(2)}, u32[]{:S(2)}) collective-permute-start(f32[40,1792]{1,0:T(8,128)S(1)} %get-tuple-element.62), channel_id=1, source_target_pairs={{0,1},{1,0},{2,3},{3,2},{4,5},{5,4},{6,7},{7,6},{8,9},{9,8},{10,11... | collective-permute-start | bytes 860168 | tf_op jit(solution)/shard_map/ppermute | solution.py:30
  30.9 1.8 %collective-permute-start.6 = (f32[40,1792]{1,0:T(8,128)S(1)}, f32[40,1792]{1,0:T(8,128)S(1)}, u32[]{:S(2)}, u32[]{:S(2)}) collective-permute-start(f32[40,1792]{1,0:T(8,128)S(1)} %get-tuple-element.60), channel_id=1, source_target_pairs={{0,1},{1,0},{2,3},{3,2},{4,5},{5,4},{6,7},{7,6},{8,9},{9,8},{10,11... | collective-permute-start | bytes 860168 | tf_op jit(solution)/shard_map/ppermute | solution.py:30
  31.5 1.6 %collective-permute-start.7 = (f32[40,1792]{1,0:T(8,128)S(1)}, f32[40,1792]{1,0:T(8,128)S(1)}, u32[]{:S(2)}, u32[]{:S(2)}) collective-permute-start(f32[40,1792]{1,0:T(8,128)S(1)} %get-tuple-element.61), channel_id=1, source_target_pairs={{0,1},{1,0},{2,3},{3,2},{4,5},{5,4},{6,7},{7,6},{8,9},{9,8},{10,11... | collective-permute-start | bytes 860168 | tf_op jit(solution)/shard_map/ppermute | solution.py:30
  33.2 12.4 %collective-permute-start.17 = (bf16[3,40,1792]{2,1,0:T(8,128)(2,1)S(1)}, bf16[3,40,1792]{2,1,0:T(8,128)(2,1)S(1)}, u32[]{:S(2)}, u32[]{:S(2)}) collective-permute-start(bf16[3,40,1792]{2,1,0:T(8,128)(2,1)S(1)} %get-tuple-element.63.refs_7_), channel_id=1, source_target_pairs={{0,2},{1,3},{2,0},{3,1},{4,6},{5,7},{6,4},{7,5},{8,10},{9,11},{10,... | collective-permute-start | bytes 1290248 | tf_op jit(solution)/shard_map/ppermute | solution.py:30
  39.9 2.3 %collective-permute-start.9 = (f32[24,1536]{1,0:T(8,128)S(1)}, f32[24,1536]{1,0:T(8,128)S(1)}, u32[]{:S(2)}, u32[]{:S(2)}) collective-permute-start(f32[24,1536]{1,0:T(8,128)S(1)} %get-tuple-element.67), channel_id=1, source_target_pairs={{0,1},{1,0},{2,3},{3,2},{4,5},{5,4},{6,7},{7,6},{8,9},{9,8},{10,11... | collective-permute-start | bytes 442376 | tf_op jit(solution)/shard_map/ppermute | solution.py:30
  39.9 2.2 %collective-permute-start.11 = (f32[24,1536]{1,0:T(8,128)S(1)}, f32[24,1536]{1,0:T(8,128)S(1)}, u32[]{:S(2)}, u32[]{:S(2)}) collective-permute-start(f32[24,1536]{1,0:T(8,128)S(1)} %get-tuple-element.69), channel_id=1, source_target_pairs={{0,1},{1,0},{2,3},{3,2},{4,5},{5,4},{6,7},{7,6},{8,9},{9,8},{10,11... | collective-permute-start | bytes 442376 | tf_op jit(solution)/shard_map/ppermute | solution.py:30
  40.7 1.5 %collective-permute-start.13 = (f32[24,1536]{1,0:T(8,128)S(1)}, f32[24,1536]{1,0:T(8,128)S(1)}, u32[]{:S(2)}, u32[]{:S(2)}) collective-permute-start(f32[24,1536]{1,0:T(8,128)S(1)} %get-tuple-element.71), channel_id=1, source_target_pairs={{0,1},{1,0},{2,3},{3,2},{4,5},{5,4},{6,7},{7,6},{8,9},{9,8},{10,11... | collective-permute-start | bytes 442376 | tf_op jit(solution)/shard_map/ppermute | solution.py:30
  42.3 11.8 %collective-permute-start.15 = (bf16[3,40,768]{2,1,0:T(8,128)(2,1)S(1)}, bf16[3,40,768]{2,1,0:T(8,128)(2,1)S(1)}, u32[]{:S(2)}, u32[]{:S(2)}) collective-permute-start(bf16[3,40,768]{2,1,0:T(8,128)(2,1)S(1)} %get-tuple-element.75.refs_2_), channel_id=1, source_target_pairs={{0,2},{1,3},{2,0},{3,1},{4,6},{5,7},{6,4},{7,5},{8,10},{9,11},{10,... | collective-permute-start | bytes 552968 | tf_op jit(solution)/shard_map/ppermute | solution.py:30
  42.9 11.2 %collective-permute-start.16 = (bf16[3,40,768]{2,1,0:T(8,128)(2,1)S(1)}, bf16[3,40,768]{2,1,0:T(8,128)(2,1)S(1)}, u32[]{:S(2)}, u32[]{:S(2)}) collective-permute-start(bf16[3,40,768]{2,1,0:T(8,128)(2,1)S(1)} %get-tuple-element.76.refs_3_), channel_id=1, source_target_pairs={{0,2},{1,3},{2,0},{3,1},{4,6},{5,7},{6,4},{7,5},{8,10},{9,11},{10,... | collective-permute-start | bytes 552968 | tf_op jit(solution)/shard_map/ppermute | solution.py:30
  45.8 1.5 %collective-permute-start.18 = (bf16[48,1792]{1,0:T(8,128)(2,1)S(1)}, bf16[48,1792]{1,0:T(8,128)(2,1)S(1)}, u32[]{:S(2)}, u32[]{:S(2)}) collective-permute-start(bf16[48,1792]{1,0:T(8,128)(2,1)S(1)} %get-tuple-element.78.rest_0_), channel_id=1, source_target_pairs={{0,1},{1,0},{2,3},{3,2},{4,5},{5,4},{6,7},{7,6},{8,9},{9,8},{10,11... | collective-permute-start | bytes 516104 | tf_op jit(solution)/shard_map/ppermute | solution.py:30
  45.9 1.6 %collective-permute-start.19 = (bf16[48,1792]{1,0:T(8,128)(2,1)S(1)}, bf16[48,1792]{1,0:T(8,128)(2,1)S(1)}, u32[]{:S(2)}, u32[]{:S(2)}) collective-permute-start(bf16[48,1792]{1,0:T(8,128)(2,1)S(1)} %get-tuple-element.79.rest_1_), channel_id=1, source_target_pairs={{0,1},{1,0},{2,3},{3,2},{4,5},{5,4},{6,7},{7,6},{8,9},{9,8},{10,11... | collective-permute-start | bytes 516104 | tf_op jit(solution)/shard_map/ppermute | solution.py:30
  54.3 1.4 %collective-permute-start.21 = (bf16[48,1536]{1,0:T(8,128)(2,1)S(1)}, bf16[48,1536]{1,0:T(8,128)(2,1)S(1)}, u32[]{:S(2)}, u32[]{:S(2)}) collective-permute-start(bf16[48,1536]{1,0:T(8,128)(2,1)S(1)} %get-tuple-element.81.rest_0_), channel_id=1, source_target_pairs={{0,1},{1,0},{2,3},{3,2},{4,5},{5,4},{6,7},{7,6},{8,9},{9,8},{10,11... | collective-permute-start | bytes 442376 | tf_op jit(solution)/shard_map/ppermute | solution.py:30
  59.9 7.5 %collective-permute-start.26 = (bf16[2,40,1280]{2,1,0:T(8,128)(2,1)S(1)}, bf16[2,40,1280]{2,1,0:T(8,128)(2,1)S(1)}, u32[]{:S(2)}, u32[]{:S(2)}) collective-permute-start(bf16[2,40,1280]{2,1,0:T(8,128)(2,1)S(1)} %get-tuple-element.86.rest_0_), channel_id=1, source_target_pairs={{0,4},{4,0},{8,12},{12,8},{1,5},{5,1},{9,13},{13,9},{2,6},{6,2},{1... | collective-permute-start | bytes 614408 | tf_op jit(solution)/shard_map/ppermute | solution.py:30
  64.3 5.2 %collective-permute-start.24 = (bf16[2,40,768]{2,1,0:T(8,128)(2,1)S(1)}, bf16[2,40,768]{2,1,0:T(8,128)(2,1)S(1)}, u32[]{:S(2)}, u32[]{:S(2)}) collective-permute-start(bf16[2,40,768]{2,1,0:T(8,128)(2,1)S(1)} %get-tuple-element.85), channel_id=1, source_target_pairs={{0,16},{16,0},{1,17},{17,1},{2,18},{18,2},{3,19},{19,3},{4,20},{20... | collective-permute-start | bytes 368648 | tf_op jit(solution)/shard_map/ppermute | solution.py:30
  67.4 5.0 %collective-permute-start.27 = (bf16[2,20,1280]{2,1,0:T(8,128)(2,1)S(1)}, bf16[2,20,1280]{2,1,0:T(8,128)(2,1)S(1)}, u32[]{:S(2)}, u32[]{:S(2)}) collective-permute-start(bf16[2,20,1280]{2,1,0:T(8,128)(2,1)S(1)} %get-tuple-element.92), channel_id=1, source_target_pairs={{0,16},{16,0},{1,17},{17,1},{2,18},{18,2},{3,19},{19,3},{4,20},{20... | collective-permute-start | bytes 307208 | tf_op jit(solution)/shard_map/ppermute | solution.py:30
  69.6 4.4 %collective-permute-start.25 = (bf16[2,20,768]{2,1,0:T(8,128)(2,1)S(1)}, bf16[2,20,768]{2,1,0:T(8,128)(2,1)S(1)}, u32[]{:S(2)}, u32[]{:S(2)}) collective-permute-start(bf16[2,20,768]{2,1,0:T(8,128)(2,1)S(1)} %get-tuple-element.88), channel_id=1, source_target_pairs={{0,4},{4,0},{8,12},{12,8},{1,5},{5,1},{9,13},{13,9},{2,6},{6,2},{1... | collective-permute-start | bytes 184328 | tf_op jit(solution)/shard_map/ppermute | solution.py:30
  72.4 7.7 %collective-permute-start.29 = (bf16[2,10,1280]{2,1,0:T(8,128)(2,1)S(1)}, bf16[2,10,1280]{2,1,0:T(8,128)(2,1)S(1)}, u32[]{:S(2)}, u32[]{:S(2)}) collective-permute-start(bf16[2,10,1280]{2,1,0:T(8,128)(2,1)S(1)} %get-tuple-element.95), channel_id=1, source_target_pairs={{0,8},{4,12},{8,0},{12,4},{1,9},{5,13},{9,1},{13,5},{2,10},{6,14},... | collective-permute-start | bytes 153608 | tf_op jit(solution)/shard_map/ppermute | solution.py:30
  74.0 6.2 %collective-permute-start.28 = (bf16[2,10,768]{2,1,0:T(8,128)(2,1)S(1)}, bf16[2,10,768]{2,1,0:T(8,128)(2,1)S(1)}, u32[]{:S(2)}, u32[]{:S(2)}) collective-permute-start(bf16[2,10,768]{2,1,0:T(8,128)(2,1)S(1)} %get-tuple-element.94), channel_id=1, source_target_pairs={{0,8},{4,12},{8,0},{12,4},{1,9},{5,13},{9,1},{13,5},{2,10},{6,14},... | collective-permute-start | bytes 92168 | tf_op jit(solution)/shard_map/ppermute | solution.py:30
  (8 other events, 15.0 us)
